TPU v7x, 128 devices: a whole 4x4x4 slice. The times are simulated.
128 devices in a mesh: rep: 2 (over x_hi), blk: 64 (over z, x_lo, y, core).
Axes of the slice: x: 4 (x_hi: 2, x_lo: 2; x = x_hi * 2 + x_lo), y: 4, z: 4, core: 2. Of those that a mesh axis runs over, the one named last changes fastest.
Arguments:
- features: bfloat16 [16384, 512], P(('rep', 'blk')), may hold values from -6 to 6
- weight: bfloat16 [512, 512], replicated, may hold values from -0.25 to 0.25
- tile_values: bfloat16 [2, 64, 64, 2, 128, 128], P('rep', 'blk'), as said below
- tile_list: int32 [2, 64, 64, 2], P('rep', 'blk'), may hold values from -1 to 1, as said below
- train_mask: int32 [16384], P(('rep', 'blk')), may hold values 0 or 1
- cotangent: bfloat16 [16384, 512], P(('rep', 'blk')), may hold values from -6 to 6
Outputs:
- activated: bfloat16 [16384, 512], P(('rep', 'blk'))
- weight_grad: float32 [512, 512], replicated
- feature_grad: bfloat16 [16384, 512], P(('rep', 'blk'))
Inputs may be any that keep to these rules, and one draw needn't show every extreme that they name: `tile_list`: -1 marks an empty slot; 0 or 1 names the half h whose tile [r, b, j, h] is nonempty; the two slots of a pair never name the same half. The graph is undirected: block (u, v) of A is nonempty exactly when block (v, u) is, and every block (u, u) is nonempty. How many nonempty tiles a device holds differs from device to device. `tile_values`: the tile of block (u, v) is the transpose of the tile of block (v, u), so A is symmetric.
All inputs are finite; a program needn't handle non-finite values. No bound on the sum of `train_mask` on one device may be relied on, other than what follows from the above.
Results may differ from a plain program's by a relative error of at most 0.014.
Values may be sent and summed in bfloat16 or wider, within the bound.
No kernel may reach another device: no remote copies, remote signals or barrier semaphores. Data moves between devices by JAX's collectives and lax.ppermute only.
A program may use at most 128 MiB of HBM per device.

v0:
```python
import math

import jax
import jax.numpy as jnp
from jax import lax
from jax.sharding import PartitionSpec as P

GELU_SCALE = math.sqrt(2.0 / math.pi)


def activation(pre_act):
    inner = GELU_SCALE * (pre_act + 0.044715 * pre_act * pre_act * pre_act)
    tanh_part = jnp.tanh(inner)
    act_value = 0.5 * pre_act * (1.0 + tanh_part)
    act_slope = 0.5 * (1.0 + tanh_part) + 0.5 * pre_act * (
        1.0 - tanh_part * tanh_part
    ) * GELU_SCALE * (1.0 + 3.0 * 0.044715 * pre_act * pre_act)
    return (act_value, act_slope)


def on_device(features, weight, tile_values, tile_list, train_mask, cotangent):
    tile_rows = features.shape[0]
    feat_width = features.shape[1]
    pair_list = tile_list[0, 0]
    presence = jnp.stack(
        [jnp.any(pair_list == 0, axis=1), jnp.any(pair_list == 1, axis=1)], axis=1
    ).astype(jnp.bfloat16)
    masked = tile_values[0, 0] * presence[:, :, None, None]
    projected = jnp.dot(features, weight, preferred_element_type=jnp.float32).astype(jnp.bfloat16)
    incoming = lax.all_gather(projected, "blk", axis=0, tiled=True)
    shard_count = incoming.shape[0] // tile_rows
    tile_block = masked
    partial_value = jnp.einsum(
        "jhst,jtf->hsf",
        tile_block,
        incoming.reshape(shard_count, tile_rows, feat_width),
        preferred_element_type=jnp.float32,
    )
    summed = lax.psum_scatter(
        partial_value.reshape(2 * tile_rows, feat_width).astype(jnp.bfloat16),
        "rep",
        scatter_dimension=0,
        tiled=True,
    ).astype(jnp.float32)
    act_value, act_slope = activation(summed)
    activated = act_value.astype(jnp.bfloat16)
    grad_z = (
        cotangent.astype(jnp.float32) * train_mask.astype(jnp.float32)[:, None] * act_slope
    ).astype(jnp.bfloat16)
    panel_rows = lax.all_gather(grad_z, "rep", axis=0, tiled=True).reshape(2, tile_rows, feat_width)
    tile_block = masked
    prop_sums = lax.psum_scatter(
        jnp.einsum(
            "jhst,hsf->jtf", tile_block, panel_rows, preferred_element_type=jnp.float32
        ).reshape(lax.axis_size("blk") * tile_rows, feat_width),
        "blk",
        scatter_dimension=0,
        tiled=True,
    )
    prop_grad = prop_sums.astype(jnp.bfloat16)
    local_term = lax.dot_general(
        features, prop_grad, (((0,), (0,)), ((), ())), preferred_element_type=jnp.float32
    )
    weight_grad = lax.psum(local_term, ("rep", "blk"))
    feature_grad = lax.dot_general(
        prop_grad, weight, (((1,), (1,)), ((), ())), preferred_element_type=jnp.float32
    ).astype(jnp.bfloat16)
    return (activated, weight_grad, feature_grad)


def solution(mesh):
    in_specs = (
        P(("rep", "blk"), None),
        P(),
        P("rep", "blk", None, None, None, None),
        P("rep", "blk", None, None),
        P(("rep", "blk")),
        P(("rep", "blk"), None),
    )
    out_specs = (P(("rep", "blk"), None), P(), P(("rep", "blk"), None))
    return jax.shard_map(
        on_device, mesh=mesh, in_specs=in_specs, out_specs=out_specs, check_vma=False
    )
```

profile of v0, /device:TPU:1, one launch (start us, length us, event | category | flops | bytes accessed | tf_op | source)
XLA Modules:
  0.0 637.2 jit_solution(3244289704318403908)
XLA Ops:
  7.2 0.0 all-gather.2.cloned.1.call-start
  7.2 1.0 copy-done
  8.2 1.8 convolution_convert_fusion.1
  10.0 0.0 all-gather.2.cloned.1.call-update
  10.0 0.0 reduce-scatter.3.cloned.1.call-start
  10.1 0.7 compare_reduce_fusion.1
  10.8 6.8 %bitcast_multiply_fusion = bf16[64,2,128,128]{3,0,2,1:T(8,128)(2,1)} fusion(bf16[1,1,64,2,128,128]{5,4,3,2,1,0:T(8,128)(2,1)} %param.8, bf16[64,2]{0,1:T(2,128)(2,1)S(1)} %add_convert_fusion), kind=kLoop, calls=%fused_computation.1 | loop fusion | flops 2097152 | bytes 8388864 | tf_op jit(solution)/shard_map/mul | solution.py:28
  17.6 107.9 %all-gather.2.cloned.1.call-done = bf16[8192,512]{1,0:T(8,128)(2,1)} async-done(((bf16[128,512]{1,0:T(8,128)(2,1)}), bf16[8192,512]{1,0:T(8,128)(2,1)}) %all-gather.2.cloned.1.call-update) | async-done | bytes 8388624 | tf_op jit(solution)/shard_map/all_gather | solution.py:30
  125.5 9.8 %fusion.5 = bf16[256,512]{1,0:T(8,128)(2,1)} fusion(bf16[64,128,512]{2,1,0:T(8,128)(2,1)} %bitcast.34, bf16[256,64,128]{2,1,0:T(8,128)(2,1)} %bitcast.30), kind=kOutput, calls=%fused_computation.6 | convolution fusion | flops 2147614720 | bytes 12845056 | tf_op jit(solution)/shard_map/jhst,jtf->hsf/dot_general | solution.py:33
  135.3 0.0 reduce-scatter.5.cloned.1.call-start
  135.3 6.8 %fusion.28 = bf16[64,128,2,128]{1,0,3,2:T(8,128)(2,1)} fusion(bf16[64,2]{0,1:T(2,128)(2,1)S(1)} %add_convert_fusion, bf16[1,1,64,2,128,128]{5,4,3,2,1,0:T(8,128)(2,1)} %param.8), kind=kLoop, calls=%fused_computation.32 | loop fusion | flops 2097152 | bytes 8388864 | tf_op jit(solution)/shard_map/jhst,hsf->jtf/dot_general | solution.py:53
  142.2 6.7 %copy.15 = bf16[64,128,2,128]{3,1,0,2:T(8,128)(2,1)} copy(bf16[64,128,2,128]{1,0,3,2:T(8,128)(2,1)} %fusion.28) | data formatting | bytes 8388608 | tf_op jit(solution)/shard_map/jhst,hsf->jtf/dot_general | solution.py:53
  148.8 0.5 reduce-scatter.3.cloned.1.call-done
  149.3 1.8 fusion.15
  151.1 6.5 %all_gather.7 = bf16[256,512]{1,0:T(8,128)(2,1)S(1)} all-gather(bf16[128,512]{1,0:T(8,128)(2,1)S(1)} %get-tuple-element.14), channel_id=1, replica_groups=mesh['rep'=2,'blk'=64] {'rep'}, dimensions={0}, use_global_device_ids=true | all-gather | bytes 393216 | tf_op jit(solution)/shard_map/all_gather | solution.py:50
  157.6 9.3 %convolution_bitcast_fusion = f32[8192,512]{1,0:T(8,128)} fusion(bf16[8192,2,128]{2,0,1:T(8,128)(2,1)} %bitcast.29, bf16[2,128,512]{2,1,0:T(8,128)(2,1)S(1)} %bitcast.31), kind=kOutput, calls=%fused_computation | convolution fusion | flops 2147483648 | bytes 21233664 | tf_op jit(solution)/shard_map/jhst,hsf->jtf/dot_general | solution.py:53
  167.0 0.0 reduce-scatter.5.cloned.1.call-update
  167.0 0.0 all-reduce.2.cloned.1.call-start
  167.1 306.4 %reduce-scatter.5.cloned.1.call-done = f32[128,512]{1,0:T(8,128)} async-done(((f32[8192,512]{1,0:T(8,128)}), f32[128,512]{1,0:T(8,128)}) %reduce-scatter.5.cloned.1.call-update) | async-done | bytes 262160 | tf_op jit(solution)/shard_map/reduce_scatter | solution.py:52
  473.5 2.2 convolution_bitcast_fusion.1
  475.7 0.0 all-reduce.2.cloned.1.call-update
  475.7 1.9 convolution_convert_fusion
  477.7 150.4 %all-reduce.2.cloned.1.call-done = f32[512,512]{0,1:T(8,128)} async-done(((f32[512,512]{0,1:T(8,128)}), f32[512,512]{0,1:T(8,128)}) %all-reduce.2.cloned.1.call-update) | async-done | bytes 1048592 | tf_op jit(solution)/shard_map/psum | solution.py:64
  628.1 2.5 copy.16
  (10 shorter events, 0.1 us)
Async XLA Ops:
  7.2 1.0 copy-start
  7.2 118.3 %all-gather.2.cloned.1.call-start = ((), (), s32[]{:S(2)}) async-start(), calls=%async_computation.2 | async-start | bytes 8519680 | tf_op jit(solution)/shard_map/all_gather | solution.py:30
  10.0 139.3 %reduce-scatter.3.cloned.1.call-start = ((), (), s32[]{:S(2)}) async-start(), calls=%async_computation.3 | async-start | bytes 393216 | tf_op jit(solution)/shard_map/reduce_scatter | solution.py:39
  125.5 9.8 %copy-start.3 = (s32[128]{0:T(128)S(1)}, s32[128]{0:T(128)}, u32[]{:S(2)}) copy-start(s32[128]{0:T(128)} %param.10) | copy-start | bytes 1540
  135.3 338.2 %reduce-scatter.5.cloned.1.call-start = ((), (), s32[]{:S(2)}) async-start(), calls=%async_computation.4 | async-start | bytes 17039360 | tf_op jit(solution)/shard_map/reduce_scatter | solution.py:52
  142.2 7.2 %copy-start.2 = (bf16[128,512]{1,0:T(8,128)(2,1)S(1)}, bf16[128,512]{1,0:T(8,128)(2,1)}, u32[]{:S(2)}) copy-start(bf16[128,512]{1,0:T(8,128)(2,1)} %param.11) | copy-start | bytes 393220
  167.0 306.5 %copy-start.1 = (bf16[128,512]{1,0:T(8,128)(2,1)S(1)}, bf16[128,512]{1,0:T(8,128)(2,1)}, u32[]{:S(2)}) copy-start(bf16[128,512]{1,0:T(8,128)(2,1)} %param.6) | copy-start | bytes 393220
  167.0 461.1 %all-reduce.2.cloned.1.call-start = ((), (), s32[]{:S(2)}) async-start(), calls=%async_computation.5 | async-start | bytes 2097152 | tf_op jit(solution)/shard_map/psum | solution.py:64
Sparse Core Ops, SparseCore 0:
  10.3 115.1 all-gather.1
  135.4 13.8 reduce-scatter.2
  167.1 306.3 reduce-scatter.4
  479.4 148.6 all-reduce.1
where the time goes:
time: 638 us; the launch traced here: 637 us
  waiting for transfers between devices  565 us (89%)
  matrix products  25 us (4%)
  other arithmetic  16.1 us (3%)
  between operations  13.8 us (2%)
  local copies, waits for them, and re-layouts  10.2 us (2%)
  blocking collectives  6.54 us (1%)
    reduce_scatter x1, waiting for transfers between devices, on_device(): lax.psum_scatter(jnp.einsum('jhst,hsf->jtf', tile_block, panel_rows, pref...  306 us
    psum x1, waiting for transfers between devices, on_device(): weight_grad = lax.psum(local_term, ('rep', 'blk'))  150 us
    all_gather x1, waiting for transfers between devices, on_device(): incoming = lax.all_gather(projected, 'blk', axis=0, tiled=True)  108 us
  transfers between devices with their start and end apart: 4, of which 4 were waited for; matrix products, arithmetic and copies ran while one was open for 4% of the time, Pallas kernels for 0%

commit v1 on v0

v1 whole, which is shorter than its diff:
```python
import functools
import math

import jax
import jax.numpy as jnp
from jax import lax
from jax.experimental import pallas as pl
from jax.experimental.pallas import tpu as pltpu
from jax.sharding import PartitionSpec as P

GELU_SCALE = math.sqrt(2.0 / math.pi)
AXES = ("rep", "blk")
T = 128
H = 256
VMEM_LIMIT = 24 * 1024 * 1024


def activation(pre_act):
    inner = GELU_SCALE * (pre_act + 0.044715 * pre_act * pre_act * pre_act)
    tanh_part = jnp.tanh(inner)
    act_value = 0.5 * pre_act * (1.0 + tanh_part)
    act_slope = 0.5 * (1.0 + tanh_part) + 0.5 * pre_act * (
        1.0 - tanh_part * tanh_part
    ) * GELU_SCALE * (1.0 + 3.0 * 0.044715 * pre_act * pre_act)
    return (act_value, act_slope)


def flat(r, z, x, y, c):
    return (((r * 4 + z) * 2 + x) * 4 + y) * 2 + c


def pairs(move):
    return [
        (flat(r, z, x, y, c), flat(*move(r, z, x, y, c)))
        for r in range(2)
        for z in range(4)
        for x in range(2)
        for y in range(4)
        for c in range(2)
    ]


def along_y(d):
    return lambda r, z, x, y, c: (r, z, x, (y + d) % 4, c)


def along_z(d):
    return lambda r, z, x, y, c: (r, (z + d) % 4, x, y, c)


def first_ring(d):
    return pairs(lambda r, z, x, y, c: (along_z(d) if c else along_y(d))(r, z, x, y, c))


def second_ring(d):
    return pairs(lambda r, z, x, y, c: (along_y(d) if c else along_z(d))(r, z, x, y, c))


TO_PLANE = pairs(lambda r, z, x, y, c: (r, z, 1 - x, y, c))
TO_CORE = pairs(lambda r, z, x, y, c: (r, z, x, y, 1 - c))
TO_REP = pairs(lambda r, z, x, y, c: (1 - r, z, x, y, c))
NEAR = {
    "y": pairs(lambda r, z, x, y, c: (r, z, x, y ^ 1, c)),
    "z": pairs(lambda r, z, x, y, c: (r, z ^ 1, x, y, c)),
}
FAR = {
    "y": pairs(lambda r, z, x, y, c: (r, z, x, 3 - y, c)),
    "z": pairs(lambda r, z, x, y, c: (r, 3 - z, x, y, c)),
}


def move(value, wiring):
    return lax.ppermute(value, AXES, wiring)


FIRST = (0, -1, 1, 2)
GROUPS = (
    ((0, 0, FIRST), (0, -1, FIRST), (0, 1, FIRST)),
    ((1, 0, FIRST), (0, 2, FIRST[:2]), (0, 2, FIRST[2:])),
    ((1, -1, FIRST), (1, 1, FIRST)),
    ((1, 2, FIRST[:2]), (1, 2, FIRST[2:])),
)


def chip_orders(z, x, y, c):
    orders = []
    for group in GROUPS:
        chips = []
        for plane, second, firsts in group:
            for first in firsts:
                zz = jnp.where(c == 0, z + second, z + first) % 4
                yy = jnp.where(c == 0, y + first, y + second) % 4
                xx = x if plane == 0 else 1 - x
                chips.append((zz * 2 + xx) * 4 + yy)
        orders.append(jnp.stack(chips).astype(jnp.int32))
    return orders


def gather(block):
    from_left = move(block, first_ring(1))
    from_right = move(block, first_ring(-1))
    from_far = move(block, first_ring(2))
    rest = jnp.concatenate([from_left, from_right, from_far], axis=0)
    other = move(block, TO_PLANE)
    other_rest = move(rest, TO_PLANE)

    def spread(row):
        left = move(row, second_ring(1))
        right = move(row, second_ring(-1))
        far_a = move(left[: 4 * T], second_ring(1))
        far_b = move(right[4 * T :], second_ring(-1))
        return left, right, far_a, far_b

    mine = jnp.concatenate([block, rest], axis=0)
    theirs = jnp.concatenate([other, other_rest], axis=0)
    left, right, far_a, far_b = spread(mine)
    left_x, right_x, far_ax, far_bx = spread(theirs)
    return (
        (mine, left, right),
        (theirs, far_a, far_b),
        (left_x, right_x),
        (far_ax, far_bx),
    )


def product_kernel(counts, has_total, last, place, order, lists, own, sibling, *refs):
    blocks = refs[: len(counts)]
    refs = refs[len(counts) :]
    if has_total:
        total_in, refs = refs[0], refs[1:]
    outs, (tiles, left, sems) = refs[:-3], refs[-3:]
    chips = sum(counts)

    def fetch(k, s):
        source = (own, sibling)[s]
        return pltpu.make_async_copy(
            source.at[pl.ds(2 * order[k], 2)], tiles.at[k, s], sems.at[k, s]
        )

    for k in range(chips):
        for s in range(2):
            fetch(k, s).start()
    c = place[1]
    for k in range(chips):
        for s in range(2):
            fetch(k, s).wait()
        for q in range(2):
            side = c if q == 0 else 1 - c
            slot = 2 * (2 * order[k] + side)
            for s in range(2):
                for h in range(2):
                    present = jnp.logical_or(
                        lists[s * T + slot] == h, lists[s * T + slot + 1] == h
                    )
                    tile = tiles[k, s, side, h]
                    left[(2 * s + h) * T : (2 * s + h + 1) * T, (2 * k + q) * T : (2 * k + q + 1) * T] = (
                        jnp.where(present, tile, jnp.zeros_like(tile))
                    )
    total = None
    at = 0
    for block, count in zip(blocks, counts):
        width = count * 2 * T
        part = jnp.dot(left[:, at : at + width], block[...], preferred_element_type=jnp.float32)
        total = part if total is None else total + part
        at += width
    if has_total:
        total = total + total_in[...]
    if not last:
        outs[0][...] = total
        return
    r = place[0]
    keep, send = outs
    for s in range(2):
        zero, one = total[2 * s * T : (2 * s + 1) * T], total[(2 * s + 1) * T : (2 * s + 2) * T]
        keep[s * T : (s + 1) * T] = jnp.where(r == 0, zero, one)
        send[s * T : (s + 1) * T] = jnp.where(r == 0, one, zero).astype(send.dtype)


def product(place, order, lists, own, sibling, blocks, total, last):
    counts = tuple(block.shape[0] // (2 * T) for block in blocks)
    chips = sum(counts)
    vmem = pl.BlockSpec(memory_space=pltpu.VMEM)
    smem = pl.BlockSpec(memory_space=pltpu.SMEM)
    hbm = pl.BlockSpec(memory_space=pl.ANY)
    args = [place, order, lists, own, sibling, *blocks] + ([] if total is None else [total])
    specs = [smem, smem, smem, hbm, hbm] + [vmem] * (len(args) - 5)
    if last:
        out_shape = (
            jax.ShapeDtypeStruct((2 * T, H), jnp.float32),
            jax.ShapeDtypeStruct((2 * T, H), jnp.bfloat16),
        )
        out_specs = (vmem, vmem)
    else:
        out_shape = jax.ShapeDtypeStruct((4 * T, H), jnp.float32)
        out_specs = vmem
    return pl.pallas_call(
        functools.partial(product_kernel, counts, total is not None, last),
        out_shape=out_shape,
        in_specs=specs,
        out_specs=out_specs,
        scratch_shapes=[
            pltpu.VMEM((chips, 2, 2, 2, T, T), jnp.bfloat16),
            pltpu.VMEM((4 * T, chips * 2 * T), jnp.bfloat16),
            pltpu.SemaphoreType.DMA((chips, 2)),
        ],
        compiler_params=pltpu.CompilerParams(vmem_limit_bytes=VMEM_LIMIT),
        cost_estimate=pl.CostEstimate(
            flops=2 * 4 * T * chips * 2 * T * H,
            bytes_accessed=chips * (2 * 4 * T * T * 2 + 2 * T * H * 2) + 4 * T * H * 4,
            transcendentals=0,
        ),
    )(*args)


def propagate(place, orders, lists, own, sibling, block):
    groups = gather(block)
    total = None
    for at, (order, blocks) in enumerate(zip(orders, groups)):
        total = product(place, order, lists, own, sibling, blocks, total, at == len(groups) - 1)
    keep, send = total
    return keep + move(send, TO_REP).astype(jnp.float32)


def middle_kernel(place, half, other, weight, factor_own, factor_sibling, act, grad_half, grad):
    c = place[1]
    mine = half[...]
    swapped = jnp.concatenate([other[T:], other[:T]], axis=0)
    summed = None
    for at in range(2):
        value = jnp.where(c == at, mine, swapped)
        head = value.astype(jnp.bfloat16)
        tail = (value - head.astype(jnp.float32)).astype(jnp.bfloat16)
        rows = weight[at * H : (at + 1) * H, :]
        part = jnp.dot(head, rows, preferred_element_type=jnp.float32) + jnp.dot(
            tail, rows, preferred_element_type=jnp.float32
        )
        summed = part if summed is None else summed + part
    act_value, act_slope = activation(summed)
    act[...] = act_value[:T].astype(act.dtype)
    factor = jnp.concatenate([factor_own[...], factor_sibling[...]], axis=0)
    grad_value = (factor.astype(jnp.float32) * act_slope).astype(grad.dtype)
    grad[...] = grad_value
    grad_half[...] = jnp.where(c == 0, grad_value[:, :H], grad_value[:, H:])


def term_kernel(half, grad, out):
    out[...] = lax.dot_general(
        half[...].astype(jnp.bfloat16),
        grad[...],
        (((0,), (0,)), ((), ())),
        preferred_element_type=jnp.float32,
    )


def final_kernel(place, mine, other, weight, out):
    c = place[1]
    low = jnp.where(c == 0, mine[...], other[...])
    high = jnp.where(c == 0, other[...], mine[...])
    contract = (((1,), (1,)), ((), ()))
    out[...] = (
        lax.dot_general(low, weight[:, :H], contract, preferred_element_type=jnp.float32)
        + lax.dot_general(high, weight[:, H:], contract, preferred_element_type=jnp.float32)
    ).astype(out.dtype)


def local_call(kernel, out_shape, *args):
    vmem = pl.BlockSpec(memory_space=pltpu.VMEM)
    smem = pl.BlockSpec(memory_space=pltpu.SMEM)
    many = isinstance(out_shape, tuple)
    return pl.pallas_call(
        kernel,
        out_shape=out_shape,
        in_specs=[smem if a.dtype == jnp.int32 else vmem for a in args],
        out_specs=tuple(vmem for _ in out_shape) if many else vmem,
        compiler_params=pltpu.CompilerParams(vmem_limit_bytes=VMEM_LIMIT),
    )(*args)


def split_sum(value, bit, wiring):
    rows = value.shape[0] // 2
    keep = lax.dynamic_slice_in_dim(value, bit * rows, rows, 0)
    send = lax.dynamic_slice_in_dim(value, (1 - bit) * rows, rows, 0)
    return keep + move(send.astype(jnp.bfloat16), wiring).astype(jnp.float32)


def join(value, bit, wiring):
    got = move(value, wiring)
    return jnp.where(
        bit == 0,
        jnp.concatenate([value, got], axis=0),
        jnp.concatenate([got, value], axis=0),
    )


def sum_terms(term, z, y, c):
    bits = {"y": ((y ^ (y >> 1)) & 1, y >> 1), "z": ((z ^ (z >> 1)) & 1, z >> 1)}
    for axis in ("y", "z"):
        term = split_sum(term, bits[axis][0], NEAR[axis])
        term = split_sum(term, bits[axis][1], FAR[axis])
    for wiring in (TO_PLANE, TO_REP):
        rounded = term.astype(jnp.bfloat16)
        term = rounded.astype(jnp.float32) + move(rounded, wiring).astype(jnp.float32)
    term = term.astype(jnp.bfloat16)
    for axis in ("z", "y"):
        term = join(term, bits[axis][1], FAR[axis])
        term = join(term, bits[axis][0], NEAR[axis])
    return join(term, c, TO_CORE).astype(jnp.float32)


def on_device(features, weight, tile_values, tile_list, train_mask, cotangent):
    r = lax.axis_index("rep")
    b = lax.axis_index("blk")
    c, y, x, z = b % 2, (b // 2) % 4, (b // 8) % 2, b // 16
    place = jnp.stack([r, c]).astype(jnp.int32)
    orders = chip_orders(z, x, y, c)

    low, high = features[:, :H], features[:, H:]
    first = c == 0
    block = jnp.concatenate(
        [jnp.where(first, low, high), move(jnp.where(first, high, low), TO_CORE)], axis=0
    )

    own = tile_values[0, 0]
    sibling = move(own, TO_CORE)
    own_list = tile_list.reshape(T)
    lists = jnp.concatenate([own_list, move(own_list, TO_CORE)])
    factor = cotangent * train_mask.astype(jnp.bfloat16)[:, None]
    factor_sibling = move(factor, TO_CORE)

    half = propagate(place, orders, lists, own, sibling, block)
    act, grad_half, grad = local_call(
        middle_kernel,
        (
            jax.ShapeDtypeStruct((T, 2 * H), jnp.bfloat16),
            jax.ShapeDtypeStruct((2 * T, H), jnp.bfloat16),
            jax.ShapeDtypeStruct((2 * T, 2 * H), jnp.bfloat16),
        ),
        place,
        half,
        move(half, TO_CORE),
        weight,
        factor,
        factor_sibling,
    )
    term = local_call(term_kernel, jax.ShapeDtypeStruct((H, 2 * H), jnp.float32), half, grad)
    weight_grad = sum_terms(term, z, y, c)

    prop = propagate(place, orders, lists, own, sibling, grad_half).astype(jnp.bfloat16)
    feature_grad = local_call(
        final_kernel,
        jax.ShapeDtypeStruct((T, 2 * H), jnp.bfloat16),
        place,
        prop[:T],
        move(prop[T:], TO_CORE),
        weight,
    )
    return (act, weight_grad, feature_grad)


def solution(mesh):
    in_specs = (
        P(("rep", "blk"), None),
        P(),
        P("rep", "blk", None, None, None, None),
        P("rep", "blk", None, None),
        P(("rep", "blk")),
        P(("rep", "blk"), None),
    )
    out_specs = (P(("rep", "blk"), None), P(), P(("rep", "blk"), None))
    return jax.shard_map(
        on_device, mesh=mesh, in_specs=in_specs, out_specs=out_specs, check_vma=False
    )
```

time: 638 us -> 158 us (0.25)
  waiting for transfers between devices: 565 us -> 33.9 us
  starting transfers between devices: 0.16 us -> 71.8 us
  Pallas kernels: 0 us -> 34.6 us
  matrix products: 25 us -> 0 us
  between operations: 13.8 us -> 1.42 us
  other arithmetic: 16.1 us -> 6.12 us
  blocking collectives: 6.54 us -> 0 us
    reduce_scatter x2 -> x0, waiting for transfers between devices: 307 us -> none  [the longest x1 306 us: on_device(): lax.psum_scatter(jnp.einsum('jhst,hsf->jtf', tile_block, panel_rows, pref...]
    psum x1 -> x0, waiting for transfers between devices: 150 us -> none  [on_device(): weight_grad = lax.psum(local_term, ('rep', 'blk'))]
    all_gather x1 -> x0, waiting for transfers between devices: 108 us -> none  [on_device(): incoming = lax.all_gather(projected, 'blk', axis=0, tiled=True)]
    ppermute x0 -> x45, starting transfers between devices: none -> 71.8 us  [move(): return lax.ppermute(value, AXES, wiring)]
    pallas_call x0 -> x11, Pallas kernels: none -> 34.6 us  [the longest x8 31.1 us: product(): pl.pallas_call(functools.partial(product_kernel, counts, total is not Non...]
    ppermute x0 -> x45, waiting for transfers between devices: none -> 33.9 us  [move(): return lax.ppermute(value, AXES, wiring)]
    dot_general x5 -> x0, matrix products: 25 us -> none  [the longest x1 9.77 us: on_device(): jnp.einsum('jhst,jtf->hsf', tile_block, incoming.reshape(shard_count, til...]
    dot_general x1 -> x0, other arithmetic: 6.81 us -> none  [on_device(): jnp.einsum('jhst,hsf->jtf', tile_block, panel_rows, preferred_element_typ...]
  transfers between devices with their start and end apart: 4 -> 45, of which waited for: 4 -> 13; matrix products, arithmetic and copies ran while one was open for 4% -> 7% of each run, Pallas kernels for 0% -> 18%
where the time goes in v1:
time: 158 us; the launch traced here: 157 us
  starting transfers between devices  71.8 us (45%)
  Pallas kernels  34.6 us (22%)
  waiting for transfers between devices  33.9 us (21%)
  local copies, waits for them, and re-layouts  9.52 us (6%)
  other arithmetic  6.12 us (4%)
    ppermute x45, starting transfers between devices, move(): return lax.ppermute(value, AXES, wiring)  71.8 us
    ppermute x45, waiting for transfers between devices, move(): return lax.ppermute(value, AXES, wiring)  33.9 us
    pallas_call x8, Pallas kernels, product(): pl.pallas_call(functools.partial(product_kernel, counts, total is not Non...  31.1 us
    unnamed x26, local copies, waits for them, and re-layouts  5.24 us
    select_n x4, other arithmetic, join(): jnp.where(bit == 0, jnp.concatenate([value, got], axis=0), jnp.concatenat...  3.62 us
    pallas_call x3, Pallas kernels, local_call(): pl.pallas_call(kernel, out_shape=out_shape, in_specs=[smem if a.dtype ==...  3.52 us
  transfers between devices with their start and end apart: 45, of which 13 were waited for; matrix products, arithmetic and copies ran while one was open for 7% of the time, Pallas kernels for 18%

profile of v1, /device:TPU:1, one launch (start us, length us, event | category | flops | bytes accessed | tf_op | source)
XLA Modules:
  0.0 157.3 jit_solution(2753442313987010550)
XLA Ops:
  3.2 5.9 %collective-permute-done.2 = bf16[128,256]{1,0:T(8,128)(2,1)S(1)} collective-permute-done((bf16[128,256]{1,0:T(8,128)(2,1)S(1)}, bf16[128,256]{1,0:T(8,128)(2,1)S(1)}, u32[]{:S(2)}, u32[]{:S(2)}) %collective-permute-start.2) | collective-permute-done | bytes 65568 | tf_op jit(solution)/shard_map/ppermute | solution.py:73
  15.5 3.2 %collective-permute-done.6 = bf16[256,256]{1,0:T(8,128)(2,1)S(1)} collective-permute-done((bf16[256,256]{1,0:T(8,128)(2,1)S(1)}, bf16[256,256]{1,0:T(8,128)(2,1)S(1)}, u32[]{:S(2)}, u32[]{:S(2)}) %collective-permute-start.6) | collective-permute-done | bytes 131104 | tf_op jit(solution)/shard_map/ppermute | solution.py:73
  22.8 6.1 %collective-permute-done.7 = bf16[768,256]{1,0:T(8,128)(2,1)S(1)} collective-permute-done((bf16[768,256]{1,0:T(8,128)(2,1)S(1)}, bf16[768,256]{1,0:T(8,128)(2,1)S(1)}, u32[]{:S(2)}, u32[]{:S(2)}) %collective-permute-start.7) | collective-permute-done | bytes 393248 | tf_op jit(solution)/shard_map/ppermute | solution.py:73
  28.9 3.3 %collective-permute-start.10 = (bf16[1024,256]{1,0:T(8,128)(2,1)S(1)}, bf16[1024,256]{1,0:T(8,128)(2,1)S(1)}, u32[]{:S(2)}, u32[]{:S(2)}) collective-permute-start(bf16[1024,256]{1,0:T(8,128)(2,1)S(1)} %constant_dynamic-update-slice_fusion.1.refs_0_), channel_id=1, source_target_pairs={{0,48},{1,7},{2,50},{3,1},{4,52},{5,3},{6,54},{7,5},{8,56},{9,15},... | collective-permute-start | bytes 1572872 | tf_op jit(solution)/shard_map/ppermute | solution.py:73
  34.5 2.7 %collective-permute-start.15 = (bf16[512,256]{1,0:T(8,128)(2,1)}, bf16[512,256]{1,0:T(8,128)(2,1)}, u32[]{:S(2)}, u32[]{:S(2)}) collective-permute-start(bf16[512,256]{1,0:T(8,128)(2,1)} %slice.51), channel_id=1, source_target_pairs={{0,48},{1,7},{2,50},{3,1},{4,52},{5,3},{6,54},{7,5},{8,56},{9,15},... | collective-permute-start | bytes 786440 | tf_op jit(solution)/shard_map/ppermute | solution.py:73
  45.6 4.8 %shard_map.85.refs_3_ = f32[512,256]{1,0:T(8,128)S(1)} custom-call(s32[2]{0:T(128)S(1)} %pad_add_fusion.place, s32[12]{0:T(128)S(1)} %stack.155.order, s32[256]{0:T(256)S(1)} %constant_dynamic-update-slice_fusion.14.lists, bf16[64,2,128,128]{3,2,1,0:T(8,128)(2,1)S(1)} %bitcast.38, bf16[64,2,128,128]{3,2,1,0:T(8,128)(2,1)} %collective-permute-done.1.sibling, ...), custom_call_target="tpu_custom_call" | custom-call | flops 805306368 | bytes 5242880 | tf_op jit(solution)/shard_map/pallas_call | solution.py:196
  50.4 4.2 %shard_map.86.refs_2_ = f32[512,256]{1,0:T(8,128)S(1)} custom-call(s32[2]{0:T(128)S(1)} %pad_add_fusion.place, s32[8]{0:T(128)S(1)} %stack.142.order, s32[256]{0:T(256)S(1)} %constant_dynamic-update-slice_fusion.14.lists, bf16[64,2,128,128]{3,2,1,0:T(8,128)(2,1)S(1)} %bitcast.39, bf16[64,2,128,128]{3,2,1,0:T(8,128)(2,1)} %collective-permute-done.1.sibling, ...), custom_call_target="tpu_custom_call" | custom-call | flops 536870912 | bytes 3670016 | tf_op jit(solution)/shard_map/pallas_call | solution.py:196
  54.6 3.8 %shard_map.87.refs_2_ = f32[512,256]{1,0:T(8,128)S(1)} custom-call(s32[2]{0:T(128)S(1)} %pad_add_fusion.place, s32[8]{0:T(128)S(1)} %stack.133.order, s32[256]{0:T(256)S(1)} %constant_dynamic-update-slice_fusion.14.lists, bf16[64,2,128,128]{3,2,1,0:T(8,128)(2,1)S(1)} %bitcast.40, bf16[64,2,128,128]{3,2,1,0:T(8,128)(2,1)} %collective-permute-done.1.sibling, ...), custom_call_target="tpu_custom_call" | custom-call | flops 536870912 | bytes 3670016 | tf_op jit(solution)/shard_map/pallas_call | solution.py:196
  58.4 2.7 %shard_map.88 = (f32[256,256]{1,0:T(8,128)S(1)}, bf16[256,256]{1,0:T(8,128)(2,1)S(1)}) custom-call(s32[2]{0:T(128)S(1)} %pad_add_fusion.place, s32[4]{0:T(128)S(1)} %pad_add_fusion.1.order, s32[256]{0:T(256)S(1)} %constant_dynamic-update-slice_fusion.14.lists, bf16[64,2,128,128]{3,2,1,0:T(8,128)(2,1)S(1)} %bitcast.41, ...), custom_call_target="tpu_custom_call" | custom-call | flops 268435456 | bytes 2097152 | tf_op jit(solution)/shard_map/pallas_call | solution.py:196
  61.1 2.8 %collective-permute-start.16 = (bf16[256,256]{1,0:T(8,128)(2,1)S(1)}, bf16[256,256]{1,0:T(8,128)(2,1)S(1)}, u32[]{:S(2)}, u32[]{:S(2)}) collective-permute-start(bf16[256,256]{1,0:T(8,128)(2,1)S(1)} %get-tuple-element.11), channel_id=1, source_target_pairs={{0,64},{1,65},{2,66},{3,67},{4,68},{5,69},{6,70},{7,71},{8,72},{9,... | collective-permute-start | bytes 393224 | tf_op jit(solution)/shard_map/ppermute | solution.py:73
  64.0 2.6 %collective-permute-done.16 = bf16[256,256]{1,0:T(8,128)(2,1)S(1)} collective-permute-done((bf16[256,256]{1,0:T(8,128)(2,1)S(1)}, bf16[256,256]{1,0:T(8,128)(2,1)S(1)}, u32[]{:S(2)}, u32[]{:S(2)}) %collective-permute-start.16) | collective-permute-done | bytes 131104 | tf_op jit(solution)/shard_map/ppermute | solution.py:73
  66.6 2.9 %collective-permute-start.17 = (f32[256,256]{1,0:T(8,128)S(1)}, f32[256,256]{1,0:T(8,128)S(1)}, u32[]{:S(2)}, u32[]{:S(2)}) collective-permute-start(f32[256,256]{1,0:T(8,128)S(1)} %convert_add_fusion.1.half), channel_id=1, source_target_pairs={{0,1},{1,0},{2,3},{3,2},{4,5},{5,4},{6,7},{7,6},{8,9},{9,8},{10,11... | collective-permute-start | bytes 786440 | tf_op jit(solution)/shard_map/ppermute | solution.py:73
  73.9 2.7 %collective-permute-start.32 = (bf16[256,256]{1,0:T(8,128)(2,1)S(1)}, bf16[256,256]{1,0:T(8,128)(2,1)S(1)}, u32[]{:S(2)}, u32[]{:S(2)}) collective-permute-start(bf16[256,256]{1,0:T(8,128)(2,1)S(1)} %get-tuple-element.14), channel_id=1, source_target_pairs={{0,6},{1,49},{2,0},{3,51},{4,2},{5,53},{6,4},{7,55},{8,14},{9,57},... | collective-permute-start | bytes 393224 | tf_op jit(solution)/shard_map/ppermute | solution.py:73
  80.7 3.2 %collective-permute-done.20 = bf16[64,512]{1,0:T(8,128)(2,1)S(1)} collective-permute-done((bf16[64,512]{1,0:T(8,128)(2,1)S(1)}, bf16[64,512]{1,0:T(8,128)(2,1)S(1)}, u32[]{:S(2)}, u32[]{:S(2)}) %collective-permute-start.20) | collective-permute-done | bytes 65568 | tf_op jit(solution)/shard_map/ppermute | solution.py:73
  84.1 2.7 %collective-permute-start.41 = (bf16[1024,256]{1,0:T(8,128)(2,1)S(1)}, bf16[1024,256]{1,0:T(8,128)(2,1)S(1)}, u32[]{:S(2)}, u32[]{:S(2)}) collective-permute-start(bf16[1024,256]{1,0:T(8,128)(2,1)S(1)} %constant_dynamic-update-slice_fusion.10.refs_0_), channel_id=1, source_target_pairs={{0,48},{1,7},{2,50},{3,1},{4,52},{5,3},{6,54},{7,5},{8,56},{9,15},... | collective-permute-start | bytes 1572872 | tf_op jit(solution)/shard_map/ppermute | solution.py:73
  93.1 2.6 %collective-permute-done.23 = bf16[16,512]{1,0:T(8,128)(2,1)S(1)} collective-permute-done((bf16[16,512]{1,0:T(8,128)(2,1)S(1)}, bf16[16,512]{1,0:T(8,128)(2,1)S(1)}, u32[]{:S(2)}, u32[]{:S(2)}) %collective-permute-start.23) | collective-permute-done | bytes 16416 | tf_op jit(solution)/shard_map/ppermute | solution.py:73
  103.2 2.7 %collective-permute-done.25 = bf16[16,512]{1,0:T(8,128)(2,1)S(1)} collective-permute-done((bf16[16,512]{1,0:T(8,128)(2,1)S(1)}, bf16[16,512]{1,0:T(8,128)(2,1)S(1)}, u32[]{:S(2)}, u32[]{:S(2)}) %collective-permute-start.25) | collective-permute-done | bytes 16416 | tf_op jit(solution)/shard_map/ppermute | solution.py:73
  111.9 2.7 %collective-permute-start.38 = (bf16[512,256]{1,0:T(8,128)(2,1)S(1)}, bf16[512,256]{1,0:T(8,128)(2,1)S(1)}, u32[]{:S(2)}, u32[]{:S(2)}) collective-permute-start(bf16[512,256]{1,0:T(8,128)(2,1)S(1)} %slice.53), channel_id=1, source_target_pairs={{0,48},{1,7},{2,50},{3,1},{4,52},{5,3},{6,54},{7,5},{8,56},{9,15},... | collective-permute-start | bytes 786440 | tf_op jit(solution)/shard_map/ppermute | solution.py:73
  119.9 4.8 %shard_map.91.refs_3_ = f32[512,256]{1,0:T(8,128)S(1)} custom-call(s32[2]{0:T(128)S(1)} %pad_add_fusion.place, s32[12]{0:T(128)S(1)} %stack.155.order, s32[256]{0:T(256)S(1)} %constant_dynamic-update-slice_fusion.14.lists, bf16[64,2,128,128]{3,2,1,0:T(8,128)(2,1)S(1)} %bitcast.42, bf16[64,2,128,128]{3,2,1,0:T(8,128)(2,1)} %collective-permute-done.1.sibling, ...), custom_call_target="tpu_custom_call" | custom-call | flops 805306368 | bytes 5242880 | tf_op jit(solution)/shard_map/pallas_call | solution.py:196
  124.8 4.3 %shard_map.92.refs_2_ = f32[512,256]{1,0:T(8,128)S(1)} custom-call(s32[2]{0:T(128)S(1)} %pad_add_fusion.place, s32[8]{0:T(128)S(1)} %stack.142.order, s32[256]{0:T(256)S(1)} %constant_dynamic-update-slice_fusion.14.lists, bf16[64,2,128,128]{3,2,1,0:T(8,128)(2,1)S(1)} %bitcast.43, bf16[64,2,128,128]{3,2,1,0:T(8,128)(2,1)} %collective-permute-done.1.sibling, ...), custom_call_target="tpu_custom_call" | custom-call | flops 536870912 | bytes 3670016 | tf_op jit(solution)/shard_map/pallas_call | solution.py:196
  129.1 3.8 %shard_map.93.refs_2_ = f32[512,256]{1,0:T(8,128)S(1)} custom-call(s32[2]{0:T(128)S(1)} %pad_add_fusion.place, s32[8]{0:T(128)S(1)} %stack.133.order, s32[256]{0:T(256)S(1)} %constant_dynamic-update-slice_fusion.14.lists, bf16[64,2,128,128]{3,2,1,0:T(8,128)(2,1)S(1)} %bitcast.44, bf16[64,2,128,128]{3,2,1,0:T(8,128)(2,1)} %collective-permute-done.1.sibling, ...), custom_call_target="tpu_custom_call" | custom-call | flops 536870912 | bytes 3670016 | tf_op jit(solution)/shard_map/pallas_call | solution.py:196
  132.9 2.7 %shard_map.94 = (f32[256,256]{1,0:T(8,128)S(1)}, bf16[256,256]{1,0:T(8,128)(2,1)S(1)}) custom-call(s32[2]{0:T(128)S(1)} %pad_add_fusion.place, s32[4]{0:T(128)S(1)} %pad_add_fusion.1.order, s32[256]{0:T(256)S(1)} %constant_dynamic-update-slice_fusion.14.lists, bf16[64,2,128,128]{3,2,1,0:T(8,128)(2,1)S(1)} %bitcast.45, ...), custom_call_target="tpu_custom_call" | custom-call | flops 268435456 | bytes 2097152 | tf_op jit(solution)/shard_map/pallas_call | solution.py:196
  137.5 12.6 %collective-permute-start.29 = (bf16[256,512]{1,0:T(8,128)(2,1)S(1)}, bf16[256,512]{1,0:T(8,128)(2,1)S(1)}, u32[]{:S(2)}, u32[]{:S(2)}) collective-permute-start(bf16[256,512]{1,0:T(8,128)(2,1)S(1)} %maximum_select_fusion.1), channel_id=1, source_target_pairs={{0,1},{1,0},{2,3},{3,2},{4,5},{5,4},{6,7},{7,6},{8,9},{9,8},{10,11... | collective-permute-start | bytes 786440 | tf_op jit(solution)/shard_map/ppermute | solution.py:73
  150.1 4.5 %collective-permute-start.44 = (bf16[128,256]{1,0:T(8,128)(2,1)S(1)}, bf16[128,256]{1,0:T(8,128)(2,1)S(1)}, u32[]{:S(2)}, u32[]{:S(2)}) collective-permute-start(bf16[128,256]{1,0:T(8,128)(2,1)S(1)} %get-tuple-element.19), channel_id=1, source_target_pairs={{0,1},{1,0},{2,3},{3,2},{4,5},{5,4},{6,7},{7,6},{8,9},{9,8},{10,11... | collective-permute-start | bytes 196616 | tf_op jit(solution)/shard_map/ppermute | solution.py:73
  (147 shorter events, 61.7 us)
Async XLA Ops:
  0.6 42.7 %collective-permute-start.1 = (bf16[64,2,128,128]{3,2,1,0:T(8,128)(2,1)}, bf16[64,2,128,128]{3,2,1,0:T(8,128)(2,1)}, u32[]{:S(2)}, u32[]{:S(2)}) collective-permute-start(bf16[64,2,128,128]{3,2,1,0:T(8,128)(2,1)} %bitcast.37), channel_id=1, source_target_pairs={{0,1},{1,0},{2,3},{3,2},{4,5},{5,4},{6,7},{7,6},{8,9},{9,8},{10,11... | collective-permute-start | bytes 12582920 | tf_op jit(solution)/shard_map/ppermute | solution.py:73
  14.3 8.5 %collective-permute-start.3 = (bf16[256,256]{1,0:T(8,128)(2,1)S(1)}, bf16[256,256]{1,0:T(8,128)(2,1)S(1)}, u32[]{:S(2)}, u32[]{:S(2)}) collective-permute-start(bf16[256,256]{1,0:T(8,128)(2,1)S(1)} %pad_maximum_fusion.2), channel_id=1, source_target_pairs={{0,8},{1,9},{2,10},{3,11},{4,12},{5,13},{6,14},{7,15},{8,0},{9,1},... | collective-permute-start | bytes 393224 | tf_op jit(solution)/shard_map/ppermute | solution.py:73
  18.7 10.2 %collective-permute-start.7 = (bf16[768,256]{1,0:T(8,128)(2,1)S(1)}, bf16[768,256]{1,0:T(8,128)(2,1)S(1)}, u32[]{:S(2)}, u32[]{:S(2)}) collective-permute-start(bf16[768,256]{1,0:T(8,128)(2,1)S(1)} %pad_maximum_fusion), channel_id=1, source_target_pairs={{0,8},{1,9},{2,10},{3,11},{4,12},{5,13},{6,14},{7,15},{8,0},{9,1},... | collective-permute-start | bytes 1179656 | tf_op jit(solution)/shard_map/ppermute | solution.py:73
  20.0 13.0 %collective-permute-start.12 = (bf16[1024,256]{1,0:T(8,128)(2,1)S(1)}, bf16[1024,256]{1,0:T(8,128)(2,1)S(1)}, u32[]{:S(2)}, u32[]{:S(2)}) collective-permute-start(bf16[1024,256]{1,0:T(8,128)(2,1)S(1)} %constant_dynamic-update-slice_fusion.3.refs_0_), channel_id=1, source_target_pairs={{0,16},{1,3},{2,18},{3,5},{4,20},{5,7},{6,22},{7,1},{8,24},{9,11},... | collective-permute-start | bytes 1572872 | tf_op jit(solution)/shard_map/ppermute | solution.py:73
  21.1 12.7 %collective-permute-start.14 = (bf16[1024,256]{1,0:T(8,128)(2,1)S(1)}, bf16[1024,256]{1,0:T(8,128)(2,1)S(1)}, u32[]{:S(2)}, u32[]{:S(2)}) collective-permute-start(bf16[1024,256]{1,0:T(8,128)(2,1)S(1)} %constant_dynamic-update-slice_fusion.3.refs_0_), channel_id=1, source_target_pairs={{0,48},{1,7},{2,50},{3,1},{4,52},{5,3},{6,54},{7,5},{8,56},{9,15},... | collective-permute-start | bytes 1572872 | tf_op jit(solution)/shard_map/ppermute | solution.py:73
  28.9 9.5 %collective-permute-start.10 = (bf16[1024,256]{1,0:T(8,128)(2,1)S(1)}, bf16[1024,256]{1,0:T(8,128)(2,1)S(1)}, u32[]{:S(2)}, u32[]{:S(2)}) collective-permute-start(bf16[1024,256]{1,0:T(8,128)(2,1)S(1)} %constant_dynamic-update-slice_fusion.1.refs_0_), channel_id=1, source_target_pairs={{0,48},{1,7},{2,50},{3,1},{4,52},{5,3},{6,54},{7,5},{8,56},{9,15},... | collective-permute-start | bytes 1572872 | tf_op jit(solution)/shard_map/ppermute | solution.py:73
  32.3 9.5 %collective-permute-start.8 = (bf16[1024,256]{1,0:T(8,128)(2,1)S(1)}, bf16[1024,256]{1,0:T(8,128)(2,1)S(1)}, u32[]{:S(2)}, u32[]{:S(2)}) collective-permute-start(bf16[1024,256]{1,0:T(8,128)(2,1)S(1)} %constant_dynamic-update-slice_fusion.1.refs_0_), channel_id=1, source_target_pairs={{0,16},{1,3},{2,18},{3,5},{4,20},{5,7},{6,22},{7,1},{8,24},{9,11},... | collective-permute-start | bytes 1572872 | tf_op jit(solution)/shard_map/ppermute | solution.py:73
  33.8 16.6 %collective-permute-start.13 = (bf16[512,256]{1,0:T(8,128)(2,1)}, bf16[512,256]{1,0:T(8,128)(2,1)S(1)}, u32[]{:S(2)}, u32[]{:S(2)}) collective-permute-start(bf16[512,256]{1,0:T(8,128)(2,1)} %slice.50), channel_id=1, source_target_pairs={{0,16},{1,3},{2,18},{3,5},{4,20},{5,7},{6,22},{7,1},{8,24},{9,11},... | collective-permute-start | bytes 786440 | tf_op jit(solution)/shard_map/ppermute | solution.py:73
  34.5 15.9 %collective-permute-start.15 = (bf16[512,256]{1,0:T(8,128)(2,1)}, bf16[512,256]{1,0:T(8,128)(2,1)}, u32[]{:S(2)}, u32[]{:S(2)}) collective-permute-start(bf16[512,256]{1,0:T(8,128)(2,1)} %slice.51), channel_id=1, source_target_pairs={{0,48},{1,7},{2,50},{3,1},{4,52},{5,3},{6,54},{7,5},{8,56},{9,15},... | collective-permute-start | bytes 786440 | tf_op jit(solution)/shard_map/ppermute | solution.py:73
  41.8 16.6 %collective-permute-start.11 = (bf16[512,256]{1,0:T(8,128)(2,1)S(1)}, bf16[512,256]{1,0:T(8,128)(2,1)S(1)}, u32[]{:S(2)}, u32[]{:S(2)}) collective-permute-start(bf16[512,256]{1,0:T(8,128)(2,1)S(1)} %slice.49), channel_id=1, source_target_pairs={{0,48},{1,7},{2,50},{3,1},{4,52},{5,3},{6,54},{7,5},{8,56},{9,15},... | collective-permute-start | bytes 786440 | tf_op jit(solution)/shard_map/ppermute | solution.py:73
  42.2 16.2 %collective-permute-start.9 = (bf16[512,256]{1,0:T(8,128)(2,1)S(1)}, bf16[512,256]{1,0:T(8,128)(2,1)S(1)}, u32[]{:S(2)}, u32[]{:S(2)}) collective-permute-start(bf16[512,256]{1,0:T(8,128)(2,1)S(1)} %slice.48), channel_id=1, source_target_pairs={{0,16},{1,3},{2,18},{3,5},{4,20},{5,7},{6,22},{7,1},{8,24},{9,11},... | collective-permute-start | bytes 786440 | tf_op jit(solution)/shard_map/ppermute | solution.py:73
  76.5 15.9 %collective-permute-start.30 = (bf16[256,256]{1,0:T(8,128)(2,1)S(1)}, bf16[256,256]{1,0:T(8,128)(2,1)S(1)}, u32[]{:S(2)}, u32[]{:S(2)}) collective-permute-start(bf16[256,256]{1,0:T(8,128)(2,1)S(1)} %get-tuple-element.14), channel_id=1, source_target_pairs={{0,8},{1,9},{2,10},{3,11},{4,12},{5,13},{6,14},{7,15},{8,0},{9,1},... | collective-permute-start | bytes 393224 | tf_op jit(solution)/shard_map/ppermute | solution.py:73
  84.1 22.5 %collective-permute-start.39 = (bf16[1024,256]{1,0:T(8,128)(2,1)S(1)}, bf16[1024,256]{1,0:T(8,128)(2,1)S(1)}, u32[]{:S(2)}, u32[]{:S(2)}) collective-permute-start(bf16[1024,256]{1,0:T(8,128)(2,1)S(1)} %constant_dynamic-update-slice_fusion.10.refs_0_), channel_id=1, source_target_pairs={{0,16},{1,3},{2,18},{3,5},{4,20},{5,7},{6,22},{7,1},{8,24},{9,11},... | collective-permute-start | bytes 1572872 | tf_op jit(solution)/shard_map/ppermute | solution.py:73
  84.1 23.5 %collective-permute-start.41 = (bf16[1024,256]{1,0:T(8,128)(2,1)S(1)}, bf16[1024,256]{1,0:T(8,128)(2,1)S(1)}, u32[]{:S(2)}, u32[]{:S(2)}) collective-permute-start(bf16[1024,256]{1,0:T(8,128)(2,1)S(1)} %constant_dynamic-update-slice_fusion.10.refs_0_), channel_id=1, source_target_pairs={{0,48},{1,7},{2,50},{3,1},{4,52},{5,3},{6,54},{7,5},{8,56},{9,15},... | collective-permute-start | bytes 1572872 | tf_op jit(solution)/shard_map/ppermute | solution.py:73
  88.5 9.8 %collective-permute-start.34 = (bf16[768,256]{1,0:T(8,128)(2,1)S(1)}, bf16[768,256]{1,0:T(8,128)(2,1)S(1)}, u32[]{:S(2)}, u32[]{:S(2)}) collective-permute-start(bf16[768,256]{1,0:T(8,128)(2,1)S(1)} %pad_maximum_fusion.1), channel_id=1, source_target_pairs={{0,8},{1,9},{2,10},{3,11},{4,12},{5,13},{6,14},{7,15},{8,0},{9,1},... | collective-permute-start | bytes 1179656 | tf_op jit(solution)/shard_map/ppermute | solution.py:73
  99.1 12.6 %collective-permute-start.35 = (bf16[1024,256]{1,0:T(8,128)(2,1)}, bf16[1024,256]{1,0:T(8,128)(2,1)S(1)}, u32[]{:S(2)}, u32[]{:S(2)}) collective-permute-start(bf16[1024,256]{1,0:T(8,128)(2,1)} %constant_dynamic-update-slice_fusion.8.refs_0_), channel_id=1, source_target_pairs={{0,16},{1,3},{2,18},{3,5},{4,20},{5,7},{6,22},{7,1},{8,24},{9,11},... | collective-permute-start | bytes 1572872 | tf_op jit(solution)/shard_map/ppermute | solution.py:73
  101.5 10.3 %collective-permute-start.37 = (bf16[1024,256]{1,0:T(8,128)(2,1)}, bf16[1024,256]{1,0:T(8,128)(2,1)S(1)}, u32[]{:S(2)}, u32[]{:S(2)}) collective-permute-start(bf16[1024,256]{1,0:T(8,128)(2,1)} %constant_dynamic-update-slice_fusion.8.refs_0_), channel_id=1, source_target_pairs={{0,48},{1,7},{2,50},{3,1},{4,52},{5,3},{6,54},{7,5},{8,56},{9,15},... | collective-permute-start | bytes 1572872 | tf_op jit(solution)/shard_map/ppermute | solution.py:73
  107.3 17.4 %collective-permute-start.40 = (bf16[512,256]{1,0:T(8,128)(2,1)}, bf16[512,256]{1,0:T(8,128)(2,1)S(1)}, u32[]{:S(2)}, u32[]{:S(2)}) collective-permute-start(bf16[512,256]{1,0:T(8,128)(2,1)} %slice.54), channel_id=1, source_target_pairs={{0,16},{1,3},{2,18},{3,5},{4,20},{5,7},{6,22},{7,1},{8,24},{9,11},... | collective-permute-start | bytes 786440 | tf_op jit(solution)/shard_map/ppermute | solution.py:73
  108.4 16.3 %collective-permute-start.42 = (bf16[512,256]{1,0:T(8,128)(2,1)}, bf16[512,256]{1,0:T(8,128)(2,1)}, u32[]{:S(2)}, u32[]{:S(2)}) collective-permute-start(bf16[512,256]{1,0:T(8,128)(2,1)} %slice.55), channel_id=1, source_target_pairs={{0,48},{1,7},{2,50},{3,1},{4,52},{5,3},{6,54},{7,5},{8,56},{9,15},... | collective-permute-start | bytes 786440 | tf_op jit(solution)/shard_map/ppermute | solution.py:73
  111.7 21.1 %collective-permute-start.36 = (bf16[512,256]{1,0:T(8,128)(2,1)S(1)}, bf16[512,256]{1,0:T(8,128)(2,1)S(1)}, u32[]{:S(2)}, u32[]{:S(2)}) collective-permute-start(bf16[512,256]{1,0:T(8,128)(2,1)S(1)} %slice.52), channel_id=1, source_target_pairs={{0,16},{1,3},{2,18},{3,5},{4,20},{5,7},{6,22},{7,1},{8,24},{9,11},... | collective-permute-start | bytes 786440 | tf_op jit(solution)/shard_map/ppermute | solution.py:73
  111.9 21.0 %collective-permute-start.38 = (bf16[512,256]{1,0:T(8,128)(2,1)S(1)}, bf16[512,256]{1,0:T(8,128)(2,1)S(1)}, u32[]{:S(2)}, u32[]{:S(2)}) collective-permute-start(bf16[512,256]{1,0:T(8,128)(2,1)S(1)} %slice.53), channel_id=1, source_target_pairs={{0,48},{1,7},{2,50},{3,1},{4,52},{5,3},{6,54},{7,5},{8,56},{9,15},... | collective-permute-start | bytes 786440 | tf_op jit(solution)/shard_map/ppermute | solution.py:73
  117.7 18.6 %collective-permute-start.28 = (bf16[128,512]{1,0:T(8,128)(2,1)}, bf16[128,512]{1,0:T(8,128)(2,1)}, u32[]{:S(2)}, u32[]{:S(2)}) collective-permute-start(bf16[128,512]{1,0:T(8,128)(2,1)} %maximum_select_fusion.2), channel_id=1, source_target_pairs={{0,2},{1,3},{2,0},{3,1},{4,6},{5,7},{6,4},{7,5},{8,10},{9,11},{10,... | collective-permute-start | bytes 393224 | tf_op jit(solution)/shard_map/ppermute | solution.py:73
  135.6 14.5 %collective-permute-start.43 = (bf16[256,256]{1,0:T(8,128)(2,1)S(1)}, bf16[256,256]{1,0:T(8,128)(2,1)S(1)}, u32[]{:S(2)}, u32[]{:S(2)}) collective-permute-start(bf16[256,256]{1,0:T(8,128)(2,1)S(1)} %get-tuple-element.16), channel_id=1, source_target_pairs={{0,64},{1,65},{2,66},{3,67},{4,68},{5,69},{6,70},{7,71},{8,72},{9,... | collective-permute-start | bytes 393224 | tf_op jit(solution)/shard_map/ppermute | solution.py:73
  137.5 17.2 %collective-permute-start.29 = (bf16[256,512]{1,0:T(8,128)(2,1)S(1)}, bf16[256,512]{1,0:T(8,128)(2,1)S(1)}, u32[]{:S(2)}, u32[]{:S(2)}) collective-permute-start(bf16[256,512]{1,0:T(8,128)(2,1)S(1)} %maximum_select_fusion.1), channel_id=1, source_target_pairs={{0,1},{1,0},{2,3},{3,2},{4,5},{5,4},{6,7},{7,6},{8,9},{9,8},{10,11... | collective-permute-start | bytes 786440 | tf_op jit(solution)/shard_map/ppermute | solution.py:73
  (29 other events, 181.5 us)

commit v2 on v0

v2 whole, which is shorter than its diff:
```python
import functools
import math

import jax
import jax.numpy as jnp
from jax import lax
from jax.experimental import pallas as pl
from jax.experimental.pallas import tpu as pltpu
from jax.sharding import PartitionSpec as P

GELU_SCALE = math.sqrt(2.0 / math.pi)
AXES = ("rep", "blk")
T = 128
H = 256
PRODUCT_LIMIT = 14 * 1024 * 1024
VMEM = pl.BlockSpec(memory_space=pltpu.VMEM)
SMEM = pl.BlockSpec(memory_space=pltpu.SMEM)


def bf16(*shape):
    return jax.ShapeDtypeStruct(shape, jnp.bfloat16)


def f32(*shape):
    return jax.ShapeDtypeStruct(shape, jnp.float32)


def activation(pre_act):
    inner = GELU_SCALE * (pre_act + 0.044715 * pre_act * pre_act * pre_act)
    tanh_part = jnp.tanh(inner)
    act_value = 0.5 * pre_act * (1.0 + tanh_part)
    act_slope = 0.5 * (1.0 + tanh_part) + 0.5 * pre_act * (
        1.0 - tanh_part * tanh_part
    ) * GELU_SCALE * (1.0 + 3.0 * 0.044715 * pre_act * pre_act)
    return (act_value, act_slope)


def flat(r, z, x, y, c):
    return (((r * 4 + z) * 2 + x) * 4 + y) * 2 + c


def pairs(move):
    return [
        (flat(r, z, x, y, c), flat(*move(r, z, x, y, c)))
        for r in range(2)
        for z in range(4)
        for x in range(2)
        for y in range(4)
        for c in range(2)
    ]


def along_y(d):
    return lambda r, z, x, y, c: (r, z, x, (y + d) % 4, c)


def along_z(d):
    return lambda r, z, x, y, c: (r, (z + d) % 4, x, y, c)


def first_ring(d):
    return pairs(lambda r, z, x, y, c: (along_z(d) if c else along_y(d))(r, z, x, y, c))


def second_ring(d):
    return pairs(lambda r, z, x, y, c: (along_y(d) if c else along_z(d))(r, z, x, y, c))


TO_PLANE = pairs(lambda r, z, x, y, c: (r, z, 1 - x, y, c))
TO_CORE = pairs(lambda r, z, x, y, c: (r, z, x, y, 1 - c))
TO_REP = pairs(lambda r, z, x, y, c: (1 - r, z, x, y, c))
ACROSS = pairs(lambda r, z, x, y, c: (1 - r, z, x, y, 1 - c))
TO_PLANE_REP = pairs(lambda r, z, x, y, c: (1 - r, z, 1 - x, y, c))
NEAR = pairs(lambda r, z, x, y, c: (r, z ^ 1, x, y, c) if c else (r, z, x, y ^ 1, c))


def move(value, wiring):
    return lax.ppermute(value, AXES, wiring)


FIRST = (0, -1, 1, 2)
GROUPS = (
    ((0, 0, FIRST), (0, -1, FIRST), (0, 1, FIRST)),
    (
        (1, 0, FIRST),
        (0, 2, FIRST[:2]),
        (0, 2, FIRST[2:]),
        (1, -1, FIRST),
        (1, 1, FIRST),
    ),
    ((1, 2, FIRST[:2]), (1, 2, FIRST[2:])),
)
SIZES = tuple(sum(len(firsts) for _, _, firsts in group) for group in GROUPS)
CHIPS = sum(SIZES)


def chip_order(z, x, y, c):
    chips = []
    for group in GROUPS:
        for plane, second, firsts in group:
            for first in firsts:
                zz = jnp.where(c == 0, z + second, z + first) & 3
                yy = jnp.where(c == 0, y + first, y + second) & 3
                xx = x if plane == 0 else 1 - x
                chips.append((zz * 2 + xx) * 4 + yy)
    return jnp.stack(chips).astype(jnp.int32)


def tiles_kernel(place, order, present, source, *outs):
    c = place[1]
    at = 0
    for out, size in zip(outs, SIZES):
        for i in range(size):
            for q in range(2):
                tile_at = 2 * order[at + i] + (c if q == 0 else 1 - c)
                for h in range(2):
                    keep = jnp.full((16, T), present[2 * tile_at + h], jnp.float32)
                    tile = source[tile_at, h].reshape(T // 16, 16, T)
                    tile = tile * keep.astype(tile.dtype)[None]
                    out[h * T : (h + 1) * T, (2 * i + q) * T : (2 * i + q + 1) * T] = (
                        tile.reshape(T, T)
                    )
        at += size


def lay_out_tiles(place, order, present, source):
    return pl.pallas_call(
        tiles_kernel,
        out_shape=tuple(bf16(2 * T, n * 2 * T) for n in SIZES),
        in_specs=[SMEM, SMEM, SMEM, VMEM],
        out_specs=tuple(VMEM for _ in SIZES),
        compiler_params=pltpu.CompilerParams(vmem_limit_bytes=PRODUCT_LIMIT),
        cost_estimate=pl.CostEstimate(
            flops=0, bytes_accessed=2 * CHIPS * 2 * T * 2 * T * 2, transcendentals=0
        ),
    )(place, order, present, source)


def product_kernel(counts, has_total, last, *refs):
    if last:
        place, refs = refs[0], refs[1:]
    lefts, refs = refs[:2], refs[2:]
    blocks, outs = refs[: len(counts)], refs[len(counts) :]
    if has_total:
        total_in, outs = outs[0], outs[1:]
    totals = []
    for s, left in enumerate(lefts):
        rows = total_in[2 * s * T : 2 * (s + 1) * T] if has_total else None
        at = 0
        for block, count in zip(blocks, counts):
            width = count * 2 * T
            part = jnp.dot(
                left[:, at : at + width], block[:width], preferred_element_type=jnp.float32
            )
            rows = part if rows is None else rows + part
            at += width
        totals.append(rows)
    total = jnp.concatenate(totals, axis=0)
    if not last:
        outs[0][...] = total
        return
    r = place[0]
    for s in range(2):
        zero, one = total[2 * s * T : (2 * s + 1) * T], total[(2 * s + 1) * T : (2 * s + 2) * T]
        keep, send = jnp.where(r == 0, zero, one), jnp.where(r == 0, one, zero)
        if len(outs) == 2:
            outs[0][s * T : (s + 1) * T] = keep
            outs[1][s * T : (s + 1) * T] = send.astype(outs[1].dtype)
        else:
            outs[s][...] = keep.astype(outs[s].dtype)
            outs[2 + s][...] = send.astype(outs[2 + s].dtype)


def product(place, lefts, counts, blocks, total, out_shape):
    chips = sum(counts)
    args = [*lefts, *blocks] + ([] if total is None else [total])
    specs = [VMEM] * len(args)
    last = isinstance(out_shape, tuple)
    if last:
        args, specs = [place] + args, [SMEM] + specs
    return pl.pallas_call(
        functools.partial(product_kernel, counts, total is not None, last),
        out_shape=out_shape,
        in_specs=specs,
        out_specs=tuple(VMEM for _ in out_shape) if last else VMEM,
        compiler_params=pltpu.CompilerParams(vmem_limit_bytes=PRODUCT_LIMIT),
        cost_estimate=pl.CostEstimate(
            flops=2 * 4 * T * chips * 2 * T * H,
            bytes_accessed=chips * (2 * 4 * T * T * 2 + 2 * T * H * 2) + 4 * T * H * 4,
            transcendentals=0,
        ),
    )(*args)


def row_kernel(extra, *refs):
    block, left, right, far, _ = refs[:5]
    refs = refs[5:]
    if extra:
        piece, refs = refs[0], refs[1:]
    row, rest = refs[:2]
    rows = 2 * T
    row[:rows] = block[:rows]
    for i, got in enumerate((left, right, far)):
        row[(i + 1) * rows : (i + 2) * rows] = got[:rows]
        rest[i * rows : (i + 1) * rows] = got[:rows]
    if extra:
        pair = piece[...].astype(jnp.float32) + far[rows:].astype(jnp.float32)
        others = left[rows:].astype(jnp.float32) + right[rows:].astype(jnp.float32)
        row[4 * rows :] = (pair + others).astype(row.dtype)


def join_rows_kernel(first, rest, out):
    rows = first.shape[0]
    out[:rows] = first[...]
    out[rows:] = rest[...]


def far_kernel(left, right, out_a, out_b):
    half = 4 * T
    out_a[:half] = left[:half]
    if out_a.shape[0] > half:
        out_a[half:] = left[2 * half :]
    out_b[...] = right[half : 2 * half]


def after(value, *others):
    return lax.optimization_barrier((value, *others))[0]


def local_call(kernel, out_shape, *args):
    many = isinstance(out_shape, tuple)
    return pl.pallas_call(
        kernel,
        out_shape=out_shape,
        in_specs=[SMEM if a.dtype == jnp.int32 else VMEM for a in args],
        out_specs=tuple(VMEM for _ in out_shape) if many else VMEM,
        compiler_params=pltpu.CompilerParams(vmem_limit_bytes=PRODUCT_LIMIT),
    )(*args)


def propagate(place, blocks, piece, get_own, get_sib, out_shape):
    extra = piece is not None
    to_side, to_far, block = blocks
    other = move(block, TO_PLANE)
    from_far = move(to_far, first_ring(2))
    from_left = move(to_side, first_ring(1))
    from_right = move(to_side, first_ring(-1))
    panels_own = get_own(block)
    more = 2 * T if extra else 0
    mine, rest = local_call(
        functools.partial(row_kernel, extra),
        (bf16(8 * T + more, H), bf16(6 * T, H)),
        block,
        after(from_left, panels_own[0]),
        from_right,
        from_far,
        other,
        *([piece] if extra else []),
    )
    other_rest = move(rest, TO_PLANE)
    left = move(mine, second_ring(1))
    right = move(mine, second_ring(-1))
    panels_sib = get_sib(mine)
    panels = tuple(zip(panels_own, panels_sib))
    other_rest = after(other_rest, panels_sib[0])
    theirs = local_call(join_rows_kernel, bf16(8 * T, H), other, other_rest)
    left_x = move(theirs, second_ring(1))
    right_x = move(theirs, second_ring(-1))
    left, right, theirs_here = lax.optimization_barrier((left, right, theirs))
    to_a, to_b = local_call(far_kernel, (bf16(4 * T + more, H), bf16(4 * T, H)), left, right)
    far_a = move(to_a, second_ring(1))
    far_b = move(to_b, second_ring(-1))
    part = f32(4 * T, H)
    total = product(place, panels[0], (4, 4, 4), (mine, left, right), None, part)
    left_x, right_x, total = lax.optimization_barrier((left_x, right_x, total))
    to_a, to_b = local_call(far_kernel, (bf16(4 * T, H), bf16(4 * T, H)), left_x, right_x)
    far_ax = move(to_a, second_ring(1))
    far_bx = move(to_b, second_ring(-1))
    total = product(
        place, panels[1], (4, 2, 2, 4, 4), (theirs_here, far_a, far_b, left_x, right_x), total, part
    )
    outs = product(place, panels[2], (2, 2), (far_ax, far_bx), total, out_shape)
    if not extra:
        return outs, None
    summed = (mine[8 * T :].astype(jnp.float32) + far_a[4 * T :].astype(jnp.float32)) + (
        left[8 * T :].astype(jnp.float32) + right[8 * T :].astype(jnp.float32)
    )
    part = after(summed.astype(jnp.bfloat16), to_a)
    sent = [move(part, wiring) for wiring in (TO_PLANE, TO_REP, TO_PLANE_REP)]
    plane, rep, both, _ = lax.optimization_barrier((*sent, outs[0]))
    whole = (part.astype(jnp.float32) + both.astype(jnp.float32)) + (
        plane.astype(jnp.float32) + rep.astype(jnp.float32)
    )
    return outs, whole.astype(jnp.bfloat16)


def middle_kernel(
    place, ring, keep, got, keep_other, got_other, weight, factor_own, factor_sibling,
    act, to_side, to_far, block, piece, term,
):
    c = place[1]
    mine = keep[...] + got[...].astype(jnp.float32)
    other = keep_other[...] + got_other[...].astype(jnp.float32)
    swapped = jnp.concatenate([other[T:], other[:T]], axis=0)
    summed = None
    for at in range(2):
        value = jnp.where(c == at, mine, swapped)
        head = value.astype(jnp.bfloat16)
        tail = (value - head.astype(jnp.float32)).astype(jnp.bfloat16)
        rows = weight[at * H : (at + 1) * H, :]
        part = jnp.dot(head, rows, preferred_element_type=jnp.float32) + jnp.dot(
            tail, rows, preferred_element_type=jnp.float32
        )
        summed = part if summed is None else summed + part
    act_value, act_slope = activation(summed)
    act[...] = act_value[:T].astype(act.dtype)
    factor = jnp.concatenate([factor_own[...], factor_sibling[...]], axis=0)
    grad_value = (factor.astype(jnp.float32) * act_slope).astype(block.dtype)
    half = jnp.where(c == 0, grad_value[:, :H], grad_value[:, H:])
    block[...] = half
    term[...] = lax.dot_general(
        mine.astype(jnp.bfloat16),
        grad_value,
        (((0,), (0,)), ((), ())),
        preferred_element_type=jnp.float32,
    )
    own_half = ring[0] & 1
    for out, half_at in ((to_side, 1 - own_half), (to_far, own_half), (piece, own_half)):
        rows = pl.ds(pl.multiple_of(half_at * T, T), T)
        at = 0
        if out is not piece:
            out[: 2 * T] = half
            at = 2 * T
        out[at : at + T] = term[rows, :H].astype(out.dtype)
        out[at + T : at + 2 * T] = term[rows, H:].astype(out.dtype)


def final_kernel(place, keep, got_rep, got_core, got_across, weight, out):
    c = place[1]
    mine = (keep[...] + got_rep[...].astype(jnp.float32)).astype(jnp.bfloat16)
    other = (got_core[...].astype(jnp.float32) + got_across[...].astype(jnp.float32)).astype(
        jnp.bfloat16
    )
    low = jnp.where(c == 0, mine, other)
    high = jnp.where(c == 0, other, mine)
    contract = (((1,), (1,)), ((), ()))
    out[...] = (
        lax.dot_general(low, weight[:, :H], contract, preferred_element_type=jnp.float32)
        + lax.dot_general(high, weight[:, H:], contract, preferred_element_type=jnp.float32)
    ).astype(out.dtype)


def join_kernel(place, ring, mine, near, sibling, out):
    c = place[1]
    for at, (side, half) in enumerate(
        ((c, ring[0] & 1), (c, 1 - (ring[0] & 1)), (1 - c, ring[1] & 1), (1 - c, 1 - (ring[1] & 1)))
    ):
        rows = pl.ds(pl.multiple_of(side * H + half * T, T), T)
        part = (mine[...], near[...], sibling[: 2 * T], sibling[2 * T :])[at].astype(jnp.float32)
        out[rows, :H] = part[:T]
        out[rows, H:] = part[T:]


def join_terms(place, ring, part):
    near = move(part, NEAR)
    both = local_call(join_rows_kernel, bf16(4 * T, H), part, near)
    sibling = move(both, TO_CORE)
    return local_call(join_kernel, f32(2 * H, 2 * H), place, ring, part, near, sibling)


def on_device(features, weight, tile_values, tile_list, train_mask, cotangent):
    r = lax.axis_index("rep")
    b = lax.axis_index("blk")
    c, y, x, z = b & 1, (b >> 1) & 3, (b >> 3) & 1, b >> 4
    place = jnp.stack([r, c]).astype(jnp.int32)
    ring = jnp.where(c == 0, jnp.stack([y, z]), jnp.stack([z, y])).astype(jnp.int32)
    order = chip_order(z, x, y, c)

    low, high = features[:, :H], features[:, H:]
    first = c == 0
    block = jnp.concatenate(
        [jnp.where(first, low, high), move(jnp.where(first, high, low), TO_CORE)], axis=0
    )

    own = tile_values[0, 0]
    pair_list = tile_list[0, 0]
    present = jnp.stack(
        [jnp.any(pair_list == 0, axis=1), jnp.any(pair_list == 1, axis=1)], axis=1
    ).astype(jnp.float32).reshape(T)
    factor = cotangent * train_mask.astype(jnp.bfloat16)[:, None]
    sibling = move(after(own, block), TO_CORE)
    present_sibling = move(after(present, block), TO_CORE)
    factor_sibling = move(after(factor, block), TO_CORE)

    panels = []

    def lay_out(present, source):
        def now(started):
            panels.append(lay_out_tiles(place, order, present, source))
            return panels[-1]

        return now

    (keep, send), _ = propagate(
        place,
        (block,) * 3,
        None,
        lay_out(present, own),
        lay_out(present_sibling, sibling),
        (f32(2 * T, H), bf16(2 * T, H)),
    )
    with_term = bf16(4 * T, H)
    act, to_side, to_far, block, piece = pl.pallas_call(
        middle_kernel,
        out_shape=(bf16(T, 2 * H), with_term, with_term, bf16(2 * T, H), bf16(2 * T, H)),
        in_specs=[SMEM] * 2 + [VMEM] * 7,
        out_specs=(VMEM,) * 5,
        scratch_shapes=[pltpu.VMEM((H, 2 * H), jnp.float32)],
        compiler_params=pltpu.CompilerParams(vmem_limit_bytes=PRODUCT_LIMIT),
    )(
        place,
        ring,
        keep,
        move(send, TO_REP),
        move(keep, TO_CORE),
        move(send, ACROSS),
        weight,
        factor,
        factor_sibling,
    )
    (keep, keep_other, send, send_other), part = propagate(
        place,
        (to_side, to_far, block),
        piece,
        lambda started: panels[0],
        lambda started: panels[1],
        (f32(T, H), bf16(T, H), bf16(T, H), bf16(T, H)),
    )
    weight_grad = join_terms(place, ring, part)
    feature_grad = local_call(
        final_kernel,
        bf16(T, 2 * H),
        place,
        keep,
        move(send, TO_REP),
        move(keep_other, TO_CORE),
        move(send_other, ACROSS),
        weight,
    )
    return (act, weight_grad, feature_grad)


def solution(mesh):
    in_specs = (
        P(("rep", "blk"), None),
        P(),
        P("rep", "blk", None, None, None, None),
        P("rep", "blk", None, None),
        P(("rep", "blk")),
        P(("rep", "blk"), None),
    )
    out_specs = (P(("rep", "blk"), None), P(), P(("rep", "blk"), None))
    return jax.shard_map(
        on_device, mesh=mesh, in_specs=in_specs, out_specs=out_specs, check_vma=False
    )
```

time: 638 us -> 124 us (0.19)
  waiting for transfers between devices: 565 us -> 42.9 us
  starting transfers between devices: 0.16 us -> 58.3 us
  matrix products: 25 us -> 0 us
  Pallas kernels: 0 us -> 16.9 us
  other arithmetic: 16.1 us -> 1.98 us
  between operations: 13.8 us -> 1.18 us
  local copies, waits for them, and re-layouts: 10.2 us -> 2.55 us
  blocking collectives: 6.54 us -> 0 us
    reduce_scatter x2 -> x0, waiting for transfers between devices: 307 us -> none  [the longest x1 306 us: on_device(): lax.psum_scatter(jnp.einsum('jhst,hsf->jtf', tile_block, panel_rows, pref...]
    psum x1 -> x0, waiting for transfers between devices: 150 us -> none  [on_device(): weight_grad = lax.psum(local_term, ('rep', 'blk'))]
    all_gather x1 -> x0, waiting for transfers between devices: 108 us -> none  [on_device(): incoming = lax.all_gather(projected, 'blk', axis=0, tiled=True)]
    ppermute x0 -> x41, starting transfers between devices: none -> 58.3 us  [move(): return lax.ppermute(value, AXES, wiring)]
    ppermute x0 -> x41, waiting for transfers between devices: none -> 42.9 us  [move(): return lax.ppermute(value, AXES, wiring)]
    dot_general x5 -> x0, matrix products: 25 us -> none  [the longest x1 9.77 us: on_device(): jnp.einsum('jhst,jtf->hsf', tile_block, incoming.reshape(shard_count, til...]
    pallas_call x0 -> x20, Pallas kernels: none -> 16.9 us  [the longest x6 6.38 us: product(): pl.pallas_call(functools.partial(product_kernel, counts, total is not Non...]
    dot_general x1 -> x0, other arithmetic: 6.81 us -> none  [on_device(): jnp.einsum('jhst,hsf->jtf', tile_block, panel_rows, preferred_element_typ...]
  transfers between devices with their start and end apart: 4 -> 41, of which waited for: 4 -> 20; matrix products, arithmetic and copies ran while one was open for 4% -> 1% of each run, Pallas kernels for 0% -> 10%
where the time goes in v2:
time: 124 us
  starting transfers between devices  58.3 us (47%)
  waiting for transfers between devices  42.9 us (35%)
  Pallas kernels  16.9 us (14%)
  local copies, waits for them, and re-layouts  2.55 us (2%)
  other arithmetic  1.98 us (2%)
    ppermute x41, starting transfers between devices, move(): return lax.ppermute(value, AXES, wiring)  58.3 us
    ppermute x41, waiting for transfers between devices, move(): return lax.ppermute(value, AXES, wiring)  42.9 us
    pallas_call x6, Pallas kernels, product(): pl.pallas_call(functools.partial(product_kernel, counts, total is not Non...  6.38 us
    pallas_call x2, Pallas kernels, lay_out_tiles(): pl.pallas_call(tiles_kernel, out_shape=tuple((bf16(2 * T, n * 2 * T) for...  5.06 us
    pallas_call x11, Pallas kernels, local_call(): pl.pallas_call(kernel, out_shape=out_shape, in_specs=[SMEM if a.dtype ==...  3.5 us
  transfers between devices with their start and end apart: 41, of which 20 were waited for; matrix products, arithmetic and copies ran while one was open for 1% of the time, Pallas kernels for 10%

profile of v2, /device:TPU:1, one launch (start us, length us, event | category | flops | bytes accessed | tf_op | source)
XLA Modules:
  0.0 123.8 jit_solution(11468385968611541878)
XLA Ops:
  8.1 2.2 %collective-permute-start.5 = (bf16[256,256]{1,0:T(8,128)(2,1)S(1)}, bf16[256,256]{1,0:T(8,128)(2,1)S(1)}, u32[]{:S(2)}, u32[]{:S(2)}) collective-permute-start(bf16[256,256]{1,0:T(8,128)(2,1)S(1)} %pad_maximum_fusion.refs_0_), channel_id=1, source_target_pairs={{0,6},{1,49},{2,0},{3,51},{4,2},{5,53},{6,4},{7,55},{8,14},{9,57},... | collective-permute-start | bytes 393224 | tf_op jit(solution)/shard_map/ppermute | solution.py:78
  12.2 2.2 %copy-done = bf16[1,1,64,2,128,128]{5,4,3,2,1,0:T(8,128)(2,1)S(1)} copy-done((bf16[1,1,64,2,128,128]{5,4,3,2,1,0:T(8,128)(2,1)S(1)}, bf16[1,1,64,2,128,128]{5,4,3,2,1,0:T(8,128)(2,1)}, u32[]{:S(2)}) %copy-start) | copy-done | bytes 4194328
  19.3 2.2 %collective-permute-start.1 = (f32[128]{0:T(128)S(1)}, f32[128]{0:T(128)S(1)}, u32[]{:S(2)}, u32[]{:S(2)}) collective-permute-start(f32[128]{0:T(128)S(1)} %reshape.15.present), channel_id=1, source_target_pairs={{0,1},{1,0},{2,3},{3,2},{4,5},{5,4},{6,7},{7,6},{8,9},{9,8},{10,11... | collective-permute-start | bytes 1544 | tf_op jit(solution)/shard_map/ppermute | solution.py:78
  22.3 3.4 %shard_map.86 = (bf16[256,3072]{1,0:T(8,128)(2,1)S(1)}, bf16[256,4096]{1,0:T(8,128)(2,1)S(1)}, bf16[256,1024]{1,0:T(8,128)(2,1)S(1)}) custom-call(s32[2]{0:T(128)S(1)} %pad_add_fusion.place.refs_0_, s32[32]{0:T(128)S(1)} %stack.170.order, f32[128]{0:T(128)S(1)} %collective-permute-done.1.present, bf16[64,2,128,128]{3,2,1,0:T(8,128)(2,1)} %collective-permute-done.2.source), custom_call_target="tpu_custom_call" | custom-call | bytes 8388608 | tf_op jit(solution)/shard_map/pallas_call | solution.py:127
  26.5 2.3 %collective-permute-start.8 = (bf16[1024,256]{1,0:T(8,128)(2,1)S(1)}, bf16[1024,256]{1,0:T(8,128)(2,1)S(1)}, u32[]{:S(2)}, u32[]{:S(2)}) collective-permute-start(bf16[1024,256]{1,0:T(8,128)(2,1)S(1)} %shard_map.88.refs_2_), channel_id=1, source_target_pairs={{0,16},{1,3},{2,18},{3,5},{4,20},{5,7},{6,22},{7,1},{8,24},{9,11},... | collective-permute-start | bytes 1572872 | tf_op jit(solution)/shard_map/ppermute | solution.py:78
  30.3 2.3 %collective-permute-start.15 = (bf16[512,256]{1,0:T(8,128)(2,1)S(1)}, bf16[512,256]{1,0:T(8,128)(2,1)S(1)}, u32[]{:S(2)}, u32[]{:S(2)}) collective-permute-start(bf16[512,256]{1,0:T(8,128)(2,1)S(1)} %get-tuple-element.75), channel_id=1, source_target_pairs={{0,48},{1,7},{2,50},{3,1},{4,52},{5,3},{6,54},{7,5},{8,56},{9,15},... | collective-permute-start | bytes 786440 | tf_op jit(solution)/shard_map/ppermute | solution.py:78
  33.5 3.0 %collective-permute-done.8.left.refs_5_ = bf16[1024,256]{1,0:T(8,128)(2,1)S(1)} collective-permute-done((bf16[1024,256]{1,0:T(8,128)(2,1)S(1)}, bf16[1024,256]{1,0:T(8,128)(2,1)S(1)}, u32[]{:S(2)}, u32[]{:S(2)}) %collective-permute-start.8) | collective-permute-done | bytes 524320 | tf_op jit(solution)/shard_map/ppermute | solution.py:78
  41.1 2.8 %collective-permute-done.12.refs_3_ = bf16[512,256]{1,0:T(8,128)(2,1)S(1)} collective-permute-done((bf16[512,256]{1,0:T(8,128)(2,1)S(1)}, bf16[512,256]{1,0:T(8,128)(2,1)S(1)}, u32[]{:S(2)}, u32[]{:S(2)}) %collective-permute-start.12) | collective-permute-done | bytes 262176 | tf_op jit(solution)/shard_map/ppermute | solution.py:78
  44.9 2.2 %collective-permute-start.17 = (f32[256,256]{1,0:T(8,128)S(1)}, f32[256,256]{1,0:T(8,128)S(1)}, u32[]{:S(2)}, u32[]{:S(2)}) collective-permute-start(f32[256,256]{1,0:T(8,128)S(1)} %get-tuple-element.77.keep), channel_id=1, source_target_pairs={{0,1},{1,0},{2,3},{3,2},{4,5},{5,4},{6,7},{7,6},{8,9},{9,8},{10,11... | collective-permute-start | bytes 786440 | tf_op jit(solution)/shard_map/ppermute | solution.py:78
  47.3 2.5 %collective-permute-start.16 = (bf16[256,256]{1,0:T(8,128)(2,1)S(1)}, bf16[256,256]{1,0:T(8,128)(2,1)S(1)}, u32[]{:S(2)}, u32[]{:S(2)}) collective-permute-start(bf16[256,256]{1,0:T(8,128)(2,1)S(1)} %get-tuple-element.78), channel_id=1, source_target_pairs={{0,64},{1,65},{2,66},{3,67},{4,68},{5,69},{6,70},{7,71},{8,72},{9,... | collective-permute-start | bytes 393224 | tf_op jit(solution)/shard_map/ppermute | solution.py:78
  51.0 2.5 %collective-permute-done.16.got = bf16[256,256]{1,0:T(8,128)(2,1)S(1)} collective-permute-done((bf16[256,256]{1,0:T(8,128)(2,1)S(1)}, bf16[256,256]{1,0:T(8,128)(2,1)S(1)}, u32[]{:S(2)}, u32[]{:S(2)}) %collective-permute-start.16) | collective-permute-done | bytes 131104 | tf_op jit(solution)/shard_map/ppermute | solution.py:78
  53.6 3.9 %collective-permute-done.18.got_other = bf16[256,256]{1,0:T(8,128)(2,1)S(1)} collective-permute-done((bf16[256,256]{1,0:T(8,128)(2,1)S(1)}, bf16[256,256]{1,0:T(8,128)(2,1)S(1)}, u32[]{:S(2)}, u32[]{:S(2)}) %collective-permute-start.18) | collective-permute-done | bytes 131104 | tf_op jit(solution)/shard_map/ppermute | solution.py:78
  57.4 2.0 %shard_map.94 = (bf16[128,512]{1,0:T(8,128)(2,1)}, bf16[512,256]{1,0:T(8,128)(2,1)S(1)}, bf16[512,256]{1,0:T(8,128)(2,1)S(1)}, bf16[256,256]{1,0:T(8,128)(2,1)S(1)}, bf16[256,256]{1,0:T(8,128)(2,1)S(1)}) custom-call(s32[2]{0:T(128)S(1)} %pad_add_fusion.place.refs_0_, s32[2]{0:T(128)S(1)} %broadcast_select_fusion.2.ring, ...), custom_call_target="tpu_custom_call" | custom-call | tf_op jit(solution)/shard_map/pallas_call | solution.py:413
  64.1 2.4 %collective-permute-done.20.refs_1_ = bf16[512,256]{1,0:T(8,128)(2,1)S(1)} collective-permute-done((bf16[512,256]{1,0:T(8,128)(2,1)S(1)}, bf16[512,256]{1,0:T(8,128)(2,1)S(1)}, u32[]{:S(2)}, u32[]{:S(2)}) %collective-permute-start.20) | collective-permute-done | bytes 262176 | tf_op jit(solution)/shard_map/ppermute | solution.py:78
  68.6 1.9 %collective-permute-done.22.refs_3_ = bf16[512,256]{1,0:T(8,128)(2,1)S(1)} collective-permute-done((bf16[512,256]{1,0:T(8,128)(2,1)S(1)}, bf16[512,256]{1,0:T(8,128)(2,1)S(1)}, u32[]{:S(2)}, u32[]{:S(2)}) %collective-permute-start.22) | collective-permute-done | bytes 262176 | tf_op jit(solution)/shard_map/ppermute | solution.py:78
  73.4 9.2 %collective-permute-done.26.rest = bf16[768,256]{1,0:T(8,128)(2,1)S(1)} collective-permute-done((bf16[768,256]{1,0:T(8,128)(2,1)S(1)}, bf16[768,256]{1,0:T(8,128)(2,1)S(1)}, u32[]{:S(2)}, u32[]{:S(2)}) %collective-permute-start.26) | collective-permute-done | bytes 393248 | tf_op jit(solution)/shard_map/ppermute | solution.py:78
  82.7 2.7 %collective-permute-start.29 = (bf16[1024,256]{1,0:T(8,128)(2,1)S(1)}, bf16[1024,256]{1,0:T(8,128)(2,1)S(1)}, u32[]{:S(2)}, u32[]{:S(2)}) collective-permute-start(bf16[1024,256]{1,0:T(8,128)(2,1)S(1)} %shard_map.96.refs_2_), channel_id=1, source_target_pairs={{0,48},{1,7},{2,50},{3,1},{4,52},{5,3},{6,54},{7,5},{8,56},{9,15},... | collective-permute-start | bytes 1572872 | tf_op jit(solution)/shard_map/ppermute | solution.py:78
  85.5 2.7 %collective-permute-start.35 = (bf16[512,256]{1,0:T(8,128)(2,1)S(1)}, bf16[512,256]{1,0:T(8,128)(2,1)S(1)}, u32[]{:S(2)}, u32[]{:S(2)}) collective-permute-start(bf16[512,256]{1,0:T(8,128)(2,1)S(1)} %get-tuple-element.98), channel_id=1, source_target_pairs={{0,48},{1,7},{2,50},{3,1},{4,52},{5,3},{6,54},{7,5},{8,56},{9,15},... | collective-permute-start | bytes 786440 | tf_op jit(solution)/shard_map/ppermute | solution.py:78
  89.1 3.1 %collective-permute-done.28.left.refs_5_ = bf16[1024,256]{1,0:T(8,128)(2,1)S(1)} collective-permute-done((bf16[1024,256]{1,0:T(8,128)(2,1)S(1)}, bf16[1024,256]{1,0:T(8,128)(2,1)S(1)}, u32[]{:S(2)}, u32[]{:S(2)}) %collective-permute-start.28) | collective-permute-done | bytes 524320 | tf_op jit(solution)/shard_map/ppermute | solution.py:78
  92.3 2.7 %collective-permute-start.34 = (bf16[512,256]{1,0:T(8,128)(2,1)S(1)}, bf16[512,256]{1,0:T(8,128)(2,1)S(1)}, u32[]{:S(2)}, u32[]{:S(2)}) collective-permute-start(bf16[512,256]{1,0:T(8,128)(2,1)S(1)} %get-tuple-element.96), channel_id=1, source_target_pairs={{0,48},{1,7},{2,50},{3,1},{4,52},{5,3},{6,54},{7,5},{8,56},{9,15},... | collective-permute-start | bytes 786440 | tf_op jit(solution)/shard_map/ppermute | solution.py:78
  96.6 2.7 %collective-permute-start.31 = (bf16[256,256]{1,0:T(8,128)(2,1)S(1)}, bf16[256,256]{1,0:T(8,128)(2,1)S(1)}, u32[]{:S(2)}, u32[]{:S(2)}) collective-permute-start(bf16[256,256]{1,0:T(8,128)(2,1)S(1)} %add_convert_fusion.1), channel_id=1, source_target_pairs={{0,64},{1,65},{2,66},{3,67},{4,68},{5,69},{6,70},{7,71},{8,72},{9,... | collective-permute-start | bytes 393224 | tf_op jit(solution)/shard_map/ppermute | solution.py:78
  104.5 5.2 %collective-permute-start.36 = (bf16[256,256]{1,0:T(8,128)(2,1)S(1)}, bf16[256,256]{1,0:T(8,128)(2,1)S(1)}, u32[]{:S(2)}, u32[]{:S(2)}) collective-permute-start(bf16[256,256]{1,0:T(8,128)(2,1)S(1)} %add_convert_fusion.first.mine), channel_id=1, source_target_pairs={{0,2},{1,17},{2,0},{3,19},{4,6},{5,21},{6,4},{7,23},{8,10},{9,25},... | collective-permute-start | bytes 393224 | tf_op jit(solution)/shard_map/ppermute | solution.py:78
  109.6 2.7 %collective-permute-done.36.rest.near = bf16[256,256]{1,0:T(8,128)(2,1)S(1)} collective-permute-done((bf16[256,256]{1,0:T(8,128)(2,1)S(1)}, bf16[256,256]{1,0:T(8,128)(2,1)S(1)}, u32[]{:S(2)}, u32[]{:S(2)}) %collective-permute-start.36) | collective-permute-done | bytes 131104 | tf_op jit(solution)/shard_map/ppermute | solution.py:78
  115.3 2.1 %collective-permute-start.40 = (bf16[128,256]{1,0:T(8,128)(2,1)S(1)}, bf16[128,256]{1,0:T(8,128)(2,1)S(1)}, u32[]{:S(2)}, u32[]{:S(2)}) collective-permute-start(bf16[128,256]{1,0:T(8,128)(2,1)S(1)} %get-tuple-element.106), channel_id=1, source_target_pairs={{0,65},{1,64},{2,67},{3,66},{4,69},{5,68},{6,71},{7,70},{8,73},{9,... | collective-permute-start | bytes 196616 | tf_op jit(solution)/shard_map/ppermute | solution.py:78
  (99 shorter events, 52.1 us)
Async XLA Ops:
  3.9 18.4 %collective-permute-start.2 = (bf16[64,2,128,128]{3,2,1,0:T(8,128)(2,1)}, bf16[64,2,128,128]{3,2,1,0:T(8,128)(2,1)}, u32[]{:S(2)}, u32[]{:S(2)}) collective-permute-start(bf16[64,2,128,128]{3,2,1,0:T(8,128)(2,1)} %bitcast.39), channel_id=1, source_target_pairs={{0,1},{1,0},{2,3},{3,2},{4,5},{5,4},{6,7},{7,6},{8,9},{9,8},{10,11... | collective-permute-start | bytes 12582920 | tf_op jit(solution)/shard_map/ppermute | solution.py:78
  5.1 11.1 %collective-permute-start.4 = (bf16[256,256]{1,0:T(8,128)(2,1)S(1)}, bf16[256,256]{1,0:T(8,128)(2,1)S(1)}, u32[]{:S(2)}, u32[]{:S(2)}) collective-permute-start(bf16[256,256]{1,0:T(8,128)(2,1)S(1)} %pad_maximum_fusion.refs_0_), channel_id=1, source_target_pairs={{0,2},{1,17},{2,4},{3,19},{4,6},{5,21},{6,0},{7,23},{8,10},{9,25},... | collective-permute-start | bytes 393224 | tf_op jit(solution)/shard_map/ppermute | solution.py:78
  6.9 9.3 %collective-permute-start.3 = (bf16[256,256]{1,0:T(8,128)(2,1)S(1)}, bf16[256,256]{1,0:T(8,128)(2,1)S(1)}, u32[]{:S(2)}, u32[]{:S(2)}) collective-permute-start(bf16[256,256]{1,0:T(8,128)(2,1)S(1)} %pad_maximum_fusion.refs_0_), channel_id=1, source_target_pairs={{0,8},{1,9},{2,10},{3,11},{4,12},{5,13},{6,14},{7,15},{8,0},{9,1},... | collective-permute-start | bytes 393224 | tf_op jit(solution)/shard_map/ppermute | solution.py:78
  8.1 8.1 %collective-permute-start.5 = (bf16[256,256]{1,0:T(8,128)(2,1)S(1)}, bf16[256,256]{1,0:T(8,128)(2,1)S(1)}, u32[]{:S(2)}, u32[]{:S(2)}) collective-permute-start(bf16[256,256]{1,0:T(8,128)(2,1)S(1)} %pad_maximum_fusion.refs_0_), channel_id=1, source_target_pairs={{0,6},{1,49},{2,0},{3,51},{4,2},{5,53},{6,4},{7,55},{8,14},{9,57},... | collective-permute-start | bytes 393224 | tf_op jit(solution)/shard_map/ppermute | solution.py:78
  16.2 10.2 %collective-permute-start.7 = (bf16[768,256]{1,0:T(8,128)(2,1)S(1)}, bf16[768,256]{1,0:T(8,128)(2,1)S(1)}, u32[]{:S(2)}, u32[]{:S(2)}) collective-permute-start(bf16[768,256]{1,0:T(8,128)(2,1)S(1)} %get-tuple-element.61), channel_id=1, source_target_pairs={{0,8},{1,9},{2,10},{3,11},{4,12},{5,13},{6,14},{7,15},{8,0},{9,1},... | collective-permute-start | bytes 1179656 | tf_op jit(solution)/shard_map/ppermute | solution.py:78
  16.6 13.2 %collective-permute-start.10 = (bf16[1024,256]{1,0:T(8,128)(2,1)S(1)}, bf16[1024,256]{1,0:T(8,128)(2,1)S(1)}, u32[]{:S(2)}, u32[]{:S(2)}) collective-permute-start(bf16[1024,256]{1,0:T(8,128)(2,1)S(1)} %get-tuple-element.64.refs_2_), channel_id=1, source_target_pairs={{0,16},{1,3},{2,18},{3,5},{4,20},{5,7},{6,22},{7,1},{8,24},{9,11},... | collective-permute-start | bytes 1572872 | tf_op jit(solution)/shard_map/ppermute | solution.py:78
  17.9 11.9 %collective-permute-start.11 = (bf16[1024,256]{1,0:T(8,128)(2,1)S(1)}, bf16[1024,256]{1,0:T(8,128)(2,1)S(1)}, u32[]{:S(2)}, u32[]{:S(2)}) collective-permute-start(bf16[1024,256]{1,0:T(8,128)(2,1)S(1)} %get-tuple-element.64.refs_2_), channel_id=1, source_target_pairs={{0,48},{1,7},{2,50},{3,1},{4,52},{5,3},{6,54},{7,5},{8,56},{9,15},... | collective-permute-start | bytes 1572872 | tf_op jit(solution)/shard_map/ppermute | solution.py:78
  26.5 10.1 %collective-permute-start.8 = (bf16[1024,256]{1,0:T(8,128)(2,1)S(1)}, bf16[1024,256]{1,0:T(8,128)(2,1)S(1)}, u32[]{:S(2)}, u32[]{:S(2)}) collective-permute-start(bf16[1024,256]{1,0:T(8,128)(2,1)S(1)} %shard_map.88.refs_2_), channel_id=1, source_target_pairs={{0,16},{1,3},{2,18},{3,5},{4,20},{5,7},{6,22},{7,1},{8,24},{9,11},... | collective-permute-start | bytes 1572872 | tf_op jit(solution)/shard_map/ppermute | solution.py:78
  28.7 8.3 %collective-permute-start.9 = (bf16[1024,256]{1,0:T(8,128)(2,1)S(1)}, bf16[1024,256]{1,0:T(8,128)(2,1)S(1)}, u32[]{:S(2)}, u32[]{:S(2)}) collective-permute-start(bf16[1024,256]{1,0:T(8,128)(2,1)S(1)} %shard_map.88.refs_2_), channel_id=1, source_target_pairs={{0,48},{1,7},{2,50},{3,1},{4,52},{5,3},{6,54},{7,5},{8,56},{9,15},... | collective-permute-start | bytes 1572872 | tf_op jit(solution)/shard_map/ppermute | solution.py:78
  29.8 10.0 %collective-permute-start.14 = (bf16[512,256]{1,0:T(8,128)(2,1)S(1)}, bf16[512,256]{1,0:T(8,128)(2,1)S(1)}, u32[]{:S(2)}, u32[]{:S(2)}) collective-permute-start(bf16[512,256]{1,0:T(8,128)(2,1)S(1)} %get-tuple-element.74), channel_id=1, source_target_pairs={{0,16},{1,3},{2,18},{3,5},{4,20},{5,7},{6,22},{7,1},{8,24},{9,11},... | collective-permute-start | bytes 786440 | tf_op jit(solution)/shard_map/ppermute | solution.py:78
  30.3 9.6 %collective-permute-start.15 = (bf16[512,256]{1,0:T(8,128)(2,1)S(1)}, bf16[512,256]{1,0:T(8,128)(2,1)S(1)}, u32[]{:S(2)}, u32[]{:S(2)}) collective-permute-start(bf16[512,256]{1,0:T(8,128)(2,1)S(1)} %get-tuple-element.75), channel_id=1, source_target_pairs={{0,48},{1,7},{2,50},{3,1},{4,52},{5,3},{6,54},{7,5},{8,56},{9,15},... | collective-permute-start | bytes 786440 | tf_op jit(solution)/shard_map/ppermute | solution.py:78
  44.9 12.6 %collective-permute-start.17 = (f32[256,256]{1,0:T(8,128)S(1)}, f32[256,256]{1,0:T(8,128)S(1)}, u32[]{:S(2)}, u32[]{:S(2)}) collective-permute-start(f32[256,256]{1,0:T(8,128)S(1)} %get-tuple-element.77.keep), channel_id=1, source_target_pairs={{0,1},{1,0},{2,3},{3,2},{4,5},{5,4},{6,7},{7,6},{8,9},{9,8},{10,11... | collective-permute-start | bytes 786440 | tf_op jit(solution)/shard_map/ppermute | solution.py:78
  60.5 8.0 %collective-permute-start.21 = (bf16[512,256]{1,0:T(8,128)(2,1)S(1)}, bf16[512,256]{1,0:T(8,128)(2,1)S(1)}, u32[]{:S(2)}, u32[]{:S(2)}) collective-permute-start(bf16[512,256]{1,0:T(8,128)(2,1)S(1)} %get-tuple-element.82), channel_id=1, source_target_pairs={{0,6},{1,49},{2,0},{3,51},{4,2},{5,53},{6,4},{7,55},{8,14},{9,57},... | collective-permute-start | bytes 786440 | tf_op jit(solution)/shard_map/ppermute | solution.py:78
  62.4 8.0 %collective-permute-start.22 = (bf16[512,256]{1,0:T(8,128)(2,1)S(1)}, bf16[512,256]{1,0:T(8,128)(2,1)S(1)}, u32[]{:S(2)}, u32[]{:S(2)}) collective-permute-start(bf16[512,256]{1,0:T(8,128)(2,1)S(1)} %get-tuple-element.84), channel_id=1, source_target_pairs={{0,4},{1,33},{2,6},{3,35},{4,0},{5,37},{6,2},{7,39},{8,12},{9,41},... | collective-permute-start | bytes 786440 | tf_op jit(solution)/shard_map/ppermute | solution.py:78
  70.6 14.7 %collective-permute-start.24 = (bf16[1280,256]{1,0:T(8,128)(2,1)S(1)}, bf16[1280,256]{1,0:T(8,128)(2,1)S(1)}, u32[]{:S(2)}, u32[]{:S(2)}) collective-permute-start(bf16[1280,256]{1,0:T(8,128)(2,1)S(1)} %get-tuple-element.86.refs_2_), channel_id=1, source_target_pairs={{0,16},{1,3},{2,18},{3,5},{4,20},{5,7},{6,22},{7,1},{8,24},{9,11},... | collective-permute-start | bytes 1966088 | tf_op jit(solution)/shard_map/ppermute | solution.py:78
  71.7 13.7 %collective-permute-start.25 = (bf16[1280,256]{1,0:T(8,128)(2,1)S(1)}, bf16[1280,256]{1,0:T(8,128)(2,1)S(1)}, u32[]{:S(2)}, u32[]{:S(2)}) collective-permute-start(bf16[1280,256]{1,0:T(8,128)(2,1)S(1)} %get-tuple-element.86.refs_2_), channel_id=1, source_target_pairs={{0,48},{1,7},{2,50},{3,1},{4,52},{5,3},{6,54},{7,5},{8,56},{9,15},... | collective-permute-start | bytes 1966088 | tf_op jit(solution)/shard_map/ppermute | solution.py:78
  73.3 9.2 %collective-permute-start.26 = (bf16[768,256]{1,0:T(8,128)(2,1)S(1)}, bf16[768,256]{1,0:T(8,128)(2,1)S(1)}, u32[]{:S(2)}, u32[]{:S(2)}) collective-permute-start(bf16[768,256]{1,0:T(8,128)(2,1)S(1)} %get-tuple-element.87), channel_id=1, source_target_pairs={{0,8},{1,9},{2,10},{3,11},{4,12},{5,13},{6,14},{7,15},{8,0},{9,1},... | collective-permute-start | bytes 1179656 | tf_op jit(solution)/shard_map/ppermute | solution.py:78
  82.6 9.6 %collective-permute-start.28 = (bf16[1024,256]{1,0:T(8,128)(2,1)S(1)}, bf16[1024,256]{1,0:T(8,128)(2,1)S(1)}, u32[]{:S(2)}, u32[]{:S(2)}) collective-permute-start(bf16[1024,256]{1,0:T(8,128)(2,1)S(1)} %shard_map.96.refs_2_), channel_id=1, source_target_pairs={{0,16},{1,3},{2,18},{3,5},{4,20},{5,7},{6,22},{7,1},{8,24},{9,11},... | collective-permute-start | bytes 1572872 | tf_op jit(solution)/shard_map/ppermute | solution.py:78
  82.7 9.5 %collective-permute-start.29 = (bf16[1024,256]{1,0:T(8,128)(2,1)S(1)}, bf16[1024,256]{1,0:T(8,128)(2,1)S(1)}, u32[]{:S(2)}, u32[]{:S(2)}) collective-permute-start(bf16[1024,256]{1,0:T(8,128)(2,1)S(1)} %shard_map.96.refs_2_), channel_id=1, source_target_pairs={{0,48},{1,7},{2,50},{3,1},{4,52},{5,3},{6,54},{7,5},{8,56},{9,15},... | collective-permute-start | bytes 1572872 | tf_op jit(solution)/shard_map/ppermute | solution.py:78
  85.4 11.0 %collective-permute-start.27 = (bf16[768,256]{1,0:T(8,128)(2,1)S(1)}, bf16[768,256]{1,0:T(8,128)(2,1)S(1)}, u32[]{:S(2)}, u32[]{:S(2)}) collective-permute-start(bf16[768,256]{1,0:T(8,128)(2,1)S(1)} %get-tuple-element.91), channel_id=1, source_target_pairs={{0,16},{1,3},{2,18},{3,5},{4,20},{5,7},{6,22},{7,1},{8,24},{9,11},... | collective-permute-start | bytes 1179656 | tf_op jit(solution)/shard_map/ppermute | solution.py:78
  85.5 13.8 %collective-permute-start.35 = (bf16[512,256]{1,0:T(8,128)(2,1)S(1)}, bf16[512,256]{1,0:T(8,128)(2,1)S(1)}, u32[]{:S(2)}, u32[]{:S(2)}) collective-permute-start(bf16[512,256]{1,0:T(8,128)(2,1)S(1)} %get-tuple-element.98), channel_id=1, source_target_pairs={{0,48},{1,7},{2,50},{3,1},{4,52},{5,3},{6,54},{7,5},{8,56},{9,15},... | collective-permute-start | bytes 786440 | tf_op jit(solution)/shard_map/ppermute | solution.py:78
  92.2 9.4 %collective-permute-start.33 = (bf16[512,256]{1,0:T(8,128)(2,1)S(1)}, bf16[512,256]{1,0:T(8,128)(2,1)S(1)}, u32[]{:S(2)}, u32[]{:S(2)}) collective-permute-start(bf16[512,256]{1,0:T(8,128)(2,1)S(1)} %get-tuple-element.94), channel_id=1, source_target_pairs={{0,16},{1,3},{2,18},{3,5},{4,20},{5,7},{6,22},{7,1},{8,24},{9,11},... | collective-permute-start | bytes 786440 | tf_op jit(solution)/shard_map/ppermute | solution.py:78
  92.3 9.4 %collective-permute-start.34 = (bf16[512,256]{1,0:T(8,128)(2,1)S(1)}, bf16[512,256]{1,0:T(8,128)(2,1)S(1)}, u32[]{:S(2)}, u32[]{:S(2)}) collective-permute-start(bf16[512,256]{1,0:T(8,128)(2,1)S(1)} %get-tuple-element.96), channel_id=1, source_target_pairs={{0,48},{1,7},{2,50},{3,1},{4,52},{5,3},{6,54},{7,5},{8,56},{9,15},... | collective-permute-start | bytes 786440 | tf_op jit(solution)/shard_map/ppermute | solution.py:78
  112.3 10.0 %collective-permute-start.37 = (bf16[512,256]{1,0:T(8,128)(2,1)S(1)}, bf16[512,256]{1,0:T(8,128)(2,1)S(1)}, u32[]{:S(2)}, u32[]{:S(2)}) collective-permute-start(bf16[512,256]{1,0:T(8,128)(2,1)S(1)} %shard_map.102), channel_id=1, source_target_pairs={{0,1},{1,0},{2,3},{3,2},{4,5},{5,4},{6,7},{7,6},{8,9},{9,8},{10,11... | collective-permute-start | bytes 786440 | tf_op jit(solution)/shard_map/ppermute | solution.py:78
  (21 other events, 127.5 us)

commit v3 on v2

--- a/solution.py
+++ b/solution.py
@@ -69,7 +69,6 @@
 TO_PLANE = pairs(lambda r, z, x, y, c: (r, z, 1 - x, y, c))
 TO_CORE = pairs(lambda r, z, x, y, c: (r, z, x, y, 1 - c))
 TO_REP = pairs(lambda r, z, x, y, c: (1 - r, z, x, y, c))
-ACROSS = pairs(lambda r, z, x, y, c: (1 - r, z, x, y, 1 - c))
 TO_PLANE_REP = pairs(lambda r, z, x, y, c: (1 - r, z, 1 - x, y, c))
 NEAR = pairs(lambda r, z, x, y, c: (r, z ^ 1, x, y, c) if c else (r, z, x, y ^ 1, c))
 
@@ -106,15 +105,17 @@
     return jnp.stack(chips).astype(jnp.int32)
 
 
-def tiles_kernel(place, order, present, source, *outs):
+def tiles_kernel(place, order, lists, source, *outs):
     c = place[1]
     at = 0
     for out, size in zip(outs, SIZES):
         for i in range(size):
             for q in range(2):
                 tile_at = 2 * order[at + i] + (c if q == 0 else 1 - c)
+                one, two = lists[2 * tile_at], lists[2 * tile_at + 1]
                 for h in range(2):
-                    keep = jnp.full((16, T), present[2 * tile_at + h], jnp.float32)
+                    present = jnp.where(jnp.logical_or(one == h, two == h), 1.0, 0.0)
+                    keep = jnp.full((16, T), present, jnp.float32)
                     tile = source[tile_at, h].reshape(T // 16, 16, T)
                     tile = tile * keep.astype(tile.dtype)[None]
                     out[h * T : (h + 1) * T, (2 * i + q) * T : (2 * i + q + 1) * T] = (
@@ -123,7 +124,7 @@
         at += size
 
 
-def lay_out_tiles(place, order, present, source):
+def lay_out_tiles(place, order, lists, source):
     return pl.pallas_call(
         tiles_kernel,
         out_shape=tuple(bf16(2 * T, n * 2 * T) for n in SIZES),
@@ -133,7 +134,7 @@
         cost_estimate=pl.CostEstimate(
             flops=0, bytes_accessed=2 * CHIPS * 2 * T * 2 * T * 2, transcendentals=0
         ),
-    )(place, order, present, source)
+    )(place, order, lists, source)
 
 
 def product_kernel(counts, has_total, last, *refs):
@@ -163,12 +164,8 @@
     for s in range(2):
         zero, one = total[2 * s * T : (2 * s + 1) * T], total[(2 * s + 1) * T : (2 * s + 2) * T]
         keep, send = jnp.where(r == 0, zero, one), jnp.where(r == 0, one, zero)
-        if len(outs) == 2:
-            outs[0][s * T : (s + 1) * T] = keep
-            outs[1][s * T : (s + 1) * T] = send.astype(outs[1].dtype)
-        else:
-            outs[s][...] = keep.astype(outs[s].dtype)
-            outs[2 + s][...] = send.astype(outs[2 + s].dtype)
+        outs[0][s * T : (s + 1) * T] = keep
+        outs[1][s * T : (s + 1) * T] = send.astype(outs[1].dtype)
 
 
 def product(place, lefts, counts, blocks, total, out_shape):
@@ -193,7 +190,7 @@
 
 
 def row_kernel(extra, *refs):
-    block, left, right, far, _ = refs[:5]
+    _, left, right, far, block = refs[:5]
     refs = refs[5:]
     if extra:
         piece, refs = refs[0], refs[1:]
@@ -202,17 +199,19 @@
     row[:rows] = block[:rows]
     for i, got in enumerate((left, right, far)):
         row[(i + 1) * rows : (i + 2) * rows] = got[:rows]
-        rest[i * rows : (i + 1) * rows] = got[:rows]
+        if got is not far:
+            rest[i * rows : (i + 1) * rows] = got[:rows]
     if extra:
         pair = piece[...].astype(jnp.float32) + far[rows:].astype(jnp.float32)
         others = left[rows:].astype(jnp.float32) + right[rows:].astype(jnp.float32)
         row[4 * rows :] = (pair + others).astype(row.dtype)
 
 
-def join_rows_kernel(first, rest, out):
-    rows = first.shape[0]
-    out[:rows] = first[...]
-    out[rows:] = rest[...]
+def join_rows_kernel(*refs):
+    at, out = 0, refs[-1]
+    for part in refs[:-1]:
+        out[at : at + part.shape[0]] = part[...]
+        at += part.shape[0]
 
 
 def far_kernel(left, right, out_a, out_b):
@@ -245,25 +244,24 @@
     from_far = move(to_far, first_ring(2))
     from_left = move(to_side, first_ring(1))
     from_right = move(to_side, first_ring(-1))
-    panels_own = get_own(block)
     more = 2 * T if extra else 0
     mine, rest = local_call(
         functools.partial(row_kernel, extra),
-        (bf16(8 * T + more, H), bf16(6 * T, H)),
-        block,
-        after(from_left, panels_own[0]),
+        (bf16(8 * T + more, H), bf16(4 * T, H)),
+        other,
+        from_left,
         from_right,
         from_far,
-        other,
+        block,
         *([piece] if extra else []),
     )
     other_rest = move(rest, TO_PLANE)
+    other_far = move(other, first_ring(2))
     left = move(mine, second_ring(1))
     right = move(mine, second_ring(-1))
     panels_sib = get_sib(mine)
-    panels = tuple(zip(panels_own, panels_sib))
     other_rest = after(other_rest, panels_sib[0])
-    theirs = local_call(join_rows_kernel, bf16(8 * T, H), other, other_rest)
+    theirs = local_call(join_rows_kernel, bf16(8 * T, H), other, other_rest, other_far)
     left_x = move(theirs, second_ring(1))
     right_x = move(theirs, second_ring(-1))
     left, right, theirs_here = lax.optimization_barrier((left, right, theirs))
@@ -271,11 +269,14 @@
     far_a = move(to_a, second_ring(1))
     far_b = move(to_b, second_ring(-1))
     part = f32(4 * T, H)
-    total = product(place, panels[0], (4, 4, 4), (mine, left, right), None, part)
-    left_x, right_x, total = lax.optimization_barrier((left_x, right_x, total))
+    panels_own = get_own(block)
+    panels = tuple(zip(panels_own, panels_sib))
+    left_x, right_x, _ = lax.optimization_barrier((left_x, right_x, panels_own[0]))
     to_a, to_b = local_call(far_kernel, (bf16(4 * T, H), bf16(4 * T, H)), left_x, right_x)
     far_ax = move(to_a, second_ring(1))
     far_bx = move(to_b, second_ring(-1))
+    mine = after(mine, to_a)
+    total = product(place, panels[0], (4, 4, 4), (mine, left, right), None, part)
     total = product(
         place, panels[1], (4, 2, 2, 4, 4), (theirs_here, far_a, far_b, left_x, right_x), total, part
     )
@@ -294,13 +295,23 @@
     return outs, whole.astype(jnp.bfloat16)
 
 
+def split_kernel(place, rows, here, there):
+    low, high = rows[:, :H], rows[:, H:]
+    first = place[1] == 0
+    here[...] = jnp.where(first, low, high)
+    there[...] = jnp.where(first, high, low)
+
+
+def add_kernel(keep, got, out):
+    out[...] = keep[...] + got[...].astype(jnp.float32)
+
+
 def middle_kernel(
-    place, ring, keep, got, keep_other, got_other, weight, factor_own, factor_sibling,
+    place, ring, half_sum, half_other, weight, factor_own, factor_sibling,
     act, to_side, to_far, block, piece, term,
 ):
     c = place[1]
-    mine = keep[...] + got[...].astype(jnp.float32)
-    other = keep_other[...] + got_other[...].astype(jnp.float32)
+    mine, other = half_sum[...], half_other[...]
     swapped = jnp.concatenate([other[T:], other[:T]], axis=0)
     summed = None
     for at in range(2):
@@ -335,14 +346,18 @@
         out[at + T : at + 2 * T] = term[rows, H:].astype(out.dtype)
 
 
-def final_kernel(place, keep, got_rep, got_core, got_across, weight, out):
+def settle_kernel(keep, got, part, near, mine, to_core):
+    total = (keep[...] + got[...].astype(jnp.float32)).astype(mine.dtype)
+    mine[...] = total[:T]
+    to_core[:T] = total[T:]
+    to_core[T : 3 * T] = part[...]
+    to_core[3 * T :] = near[...]
+
+
+def final_kernel(place, mine, core, weight, out):
     c = place[1]
-    mine = (keep[...] + got_rep[...].astype(jnp.float32)).astype(jnp.bfloat16)
-    other = (got_core[...].astype(jnp.float32) + got_across[...].astype(jnp.float32)).astype(
-        jnp.bfloat16
-    )
-    low = jnp.where(c == 0, mine, other)
-    high = jnp.where(c == 0, other, mine)
+    low = jnp.where(c == 0, mine[...], core[:T])
+    high = jnp.where(c == 0, core[:T], mine[...])
     contract = (((1,), (1,)), ((), ()))
     out[...] = (
         lax.dot_general(low, weight[:, :H], contract, preferred_element_type=jnp.float32)
@@ -350,22 +365,20 @@
     ).astype(out.dtype)
 
 
-def join_kernel(place, ring, mine, near, sibling, out):
+def join_kernel(place, ring, mine, near, core, out):
     c = place[1]
-    for at, (side, half) in enumerate(
-        ((c, ring[0] & 1), (c, 1 - (ring[0] & 1)), (1 - c, ring[1] & 1), (1 - c, 1 - (ring[1] & 1)))
-    ):
+    p, q = ring[0] & 1, ring[1] & 1
+    parts = (
+        (mine[...], c, p),
+        (near[...], c, 1 - p),
+        (core[T : 3 * T], 1 - c, q),
+        (core[3 * T :], 1 - c, 1 - q),
+    )
+    for part, side, half in parts:
         rows = pl.ds(pl.multiple_of(side * H + half * T, T), T)
-        part = (mine[...], near[...], sibling[: 2 * T], sibling[2 * T :])[at].astype(jnp.float32)
-        out[rows, :H] = part[:T]
-        out[rows, H:] = part[T:]
-
-
-def join_terms(place, ring, part):
-    near = move(part, NEAR)
-    both = local_call(join_rows_kernel, bf16(4 * T, H), part, near)
-    sibling = move(both, TO_CORE)
-    return local_call(join_kernel, f32(2 * H, 2 * H), place, ring, part, near, sibling)
+        value = part.astype(jnp.float32)
+        out[rows, :H] = value[:T]
+        out[rows, H:] = value[T:]
 
 
 def on_device(features, weight, tile_values, tile_list, train_mask, cotangent):
@@ -376,28 +389,22 @@
     ring = jnp.where(c == 0, jnp.stack([y, z]), jnp.stack([z, y])).astype(jnp.int32)
     order = chip_order(z, x, y, c)
 
-    low, high = features[:, :H], features[:, H:]
-    first = c == 0
-    block = jnp.concatenate(
-        [jnp.where(first, low, high), move(jnp.where(first, high, low), TO_CORE)], axis=0
-    )
+    here, there = local_call(split_kernel, (bf16(T, H), bf16(T, H)), place, features)
+    block = local_call(join_rows_kernel, bf16(2 * T, H), here, move(there, TO_CORE))
 
     own = tile_values[0, 0]
-    pair_list = tile_list[0, 0]
-    present = jnp.stack(
-        [jnp.any(pair_list == 0, axis=1), jnp.any(pair_list == 1, axis=1)], axis=1
-    ).astype(jnp.float32).reshape(T)
+    lists = tile_list.reshape(T)
     factor = cotangent * train_mask.astype(jnp.bfloat16)[:, None]
     sibling = move(after(own, block), TO_CORE)
-    present_sibling = move(after(present, block), TO_CORE)
+    lists_sibling = move(after(lists, block), TO_CORE)
     factor_sibling = move(after(factor, block), TO_CORE)
 
-    panels = []
-
-    def lay_out(present, source):
+    panels = {}
+
+    def lay_out(name, lists, source):
         def now(started):
-            panels.append(lay_out_tiles(place, order, present, source))
-            return panels[-1]
+            panels[name] = lay_out_tiles(place, order, lists, source)
+            return panels[name]
 
         return now
 
@@ -405,47 +412,46 @@
         place,
         (block,) * 3,
         None,
-        lay_out(present, own),
-        lay_out(present_sibling, sibling),
+        lay_out("own", lists, own),
+        lay_out("sibling", lists_sibling, sibling),
         (f32(2 * T, H), bf16(2 * T, H)),
     )
+    half_sum = local_call(add_kernel, f32(2 * T, H), keep, move(send, TO_REP))
     with_term = bf16(4 * T, H)
     act, to_side, to_far, block, piece = pl.pallas_call(
         middle_kernel,
         out_shape=(bf16(T, 2 * H), with_term, with_term, bf16(2 * T, H), bf16(2 * T, H)),
-        in_specs=[SMEM] * 2 + [VMEM] * 7,
+        in_specs=[SMEM] * 2 + [VMEM] * 5,
         out_specs=(VMEM,) * 5,
         scratch_shapes=[pltpu.VMEM((H, 2 * H), jnp.float32)],
         compiler_params=pltpu.CompilerParams(vmem_limit_bytes=PRODUCT_LIMIT),
     )(
         place,
         ring,
-        keep,
-        move(send, TO_REP),
-        move(keep, TO_CORE),
-        move(send, ACROSS),
+        half_sum,
+        move(half_sum, TO_CORE),
         weight,
         factor,
         factor_sibling,
     )
-    (keep, keep_other, send, send_other), part = propagate(
+    (keep, send), part = propagate(
         place,
         (to_side, to_far, block),
         piece,
-        lambda started: panels[0],
-        lambda started: panels[1],
-        (f32(T, H), bf16(T, H), bf16(T, H), bf16(T, H)),
-    )
-    weight_grad = join_terms(place, ring, part)
+        lambda started: panels["own"],
+        lambda started: panels["sibling"],
+        (f32(2 * T, H), bf16(2 * T, H)),
+    )
+    near = move(part, NEAR)
+    mine, to_core = local_call(
+        settle_kernel, (bf16(T, H), bf16(5 * T, H)), keep, move(send, TO_REP), part, near
+    )
+    got_core = move(to_core, TO_CORE)
     feature_grad = local_call(
-        final_kernel,
-        bf16(T, 2 * H),
-        place,
-        keep,
-        move(send, TO_REP),
-        move(keep_other, TO_CORE),
-        move(send_other, ACROSS),
-        weight,
+        final_kernel, bf16(T, 2 * H), place, mine, got_core, weight
+    )
+    weight_grad = local_call(
+        join_kernel, f32(2 * H, 2 * H), place, ring, part, near, got_core
     )
     return (act, weight_grad, feature_grad)
 

time: 124 us -> 119 us (0.960)
  waiting for transfers between devices: 42.9 us -> 36.2 us
  starting transfers between devices: 58.3 us -> 61.9 us
  other arithmetic: 1.98 us -> 0.38 us
    ppermute x41 -> x40, waiting for transfers between devices: 42.9 us -> 36.2 us  [move(): return lax.ppermute(value, AXES, wiring)]
    ppermute x41 -> x40, starting transfers between devices: 58.3 us -> 61.9 us  [move(): return lax.ppermute(value, AXES, wiring)]
    pallas_call x11 -> x14, Pallas kernels: 3.5 us -> 4.1 us  [local_call(): pl.pallas_call(kernel, out_shape=out_shape, in_specs=[SMEM if a.dtype ==...]
  transfers between devices with their start and end apart: 41 -> 40, of which waited for: 20 -> 19; matrix products, arithmetic and copies ran while one was open for 1% -> 1% of each run, Pallas kernels for 10% -> 9%
where the time goes in v3:
time: 119 us
  starting transfers between devices  61.9 us (52%)
  waiting for transfers between devices  36.2 us (30%)
  Pallas kernels  17.8 us (15%)
  local copies, waits for them, and re-layouts  1.94 us (2%)
    ppermute x40, starting transfers between devices, move(): return lax.ppermute(value, AXES, wiring)  61.9 us
    ppermute x40, waiting for transfers between devices, move(): return lax.ppermute(value, AXES, wiring)  36.2 us
    pallas_call x6, Pallas kernels, product(): pl.pallas_call(functools.partial(product_kernel, counts, total is not Non...  6.4 us
    pallas_call x2, Pallas kernels, lay_out_tiles(): pl.pallas_call(tiles_kernel, out_shape=tuple((bf16(2 * T, n * 2 * T) for...  5.36 us
    pallas_call x14, Pallas kernels, local_call(): pl.pallas_call(kernel, out_shape=out_shape, in_specs=[SMEM if a.dtype ==...  4.1 us
  transfers between devices with their start and end apart: 40, of which 19 were waited for; matrix products, arithmetic and copies ran while one was open for 1% of the time, Pallas kernels for 9%

profile of v3, /device:TPU:1, one launch (start us, length us, event | category | flops | bytes accessed | tf_op | source)
XLA Modules:
  0.0 119.2 jit_solution(12669969603380483044)
XLA Ops:
  6.3 1.6 %collective-permute-start.4 = (bf16[256,256]{1,0:T(8,128)(2,1)S(1)}, bf16[256,256]{1,0:T(8,128)(2,1)S(1)}, u32[]{:S(2)}, u32[]{:S(2)}) collective-permute-start(bf16[256,256]{1,0:T(8,128)(2,1)S(1)} %shard_map.87.refs_4_), channel_id=1, source_target_pairs={{0,2},{1,17},{2,4},{3,19},{4,6},{5,21},{6,0},{7,23},{8,10},{9,25},... | collective-permute-start | bytes 393224 | tf_op jit(solution)/shard_map/ppermute | solution.py:77
  8.0 2.1 %collective-permute-start.5 = (bf16[256,256]{1,0:T(8,128)(2,1)S(1)}, bf16[256,256]{1,0:T(8,128)(2,1)S(1)}, u32[]{:S(2)}, u32[]{:S(2)}) collective-permute-start(bf16[256,256]{1,0:T(8,128)(2,1)S(1)} %shard_map.87.refs_4_), channel_id=1, source_target_pairs={{0,6},{1,49},{2,0},{3,51},{4,2},{5,53},{6,4},{7,55},{8,14},{9,57},... | collective-permute-start | bytes 393224 | tf_op jit(solution)/shard_map/ppermute | solution.py:77
  12.5 3.2 %collective-permute-done.6.refs_3_ = bf16[256,256]{1,0:T(8,128)(2,1)S(1)} collective-permute-done((bf16[256,256]{1,0:T(8,128)(2,1)S(1)}, bf16[256,256]{1,0:T(8,128)(2,1)S(1)}, u32[]{:S(2)}, u32[]{:S(2)}) %collective-permute-start.6) | collective-permute-done | bytes 131104 | tf_op jit(solution)/shard_map/ppermute | solution.py:77
  18.0 2.1 %collective-permute-start.1 = (s32[128]{0:T(128)S(1)}, s32[128]{0:T(128)S(1)}, u32[]{:S(2)}, u32[]{:S(2)}) collective-permute-start(s32[128]{0:T(128)S(1)} %reshape.10.lists), channel_id=1, source_target_pairs={{0,1},{1,0},{2,3},{3,2},{4,5},{5,4},{6,7},{7,6},{8,9},{9,8},{10,11... | collective-permute-start | bytes 1544 | tf_op jit(solution)/shard_map/ppermute | solution.py:77
  20.9 1.9 %collective-permute-start.14 = (bf16[1024,256]{1,0:T(8,128)(2,1)S(1)}, bf16[1024,256]{1,0:T(8,128)(2,1)S(1)}, u32[]{:S(2)}, u32[]{:S(2)}) collective-permute-start(bf16[1024,256]{1,0:T(8,128)(2,1)S(1)} %get-tuple-element.77.refs_2_), channel_id=1, source_target_pairs={{0,48},{1,7},{2,50},{3,1},{4,52},{5,3},{6,54},{7,5},{8,56},{9,15},... | collective-permute-start | bytes 1572872 | tf_op jit(solution)/shard_map/ppermute | solution.py:77
  22.9 3.6 %shard_map.88 = (bf16[256,3072]{1,0:T(8,128)(2,1)S(1)}, bf16[256,4096]{1,0:T(8,128)(2,1)S(1)}, bf16[256,1024]{1,0:T(8,128)(2,1)S(1)}) custom-call(s32[2]{0:T(128)S(1)} %pad_add_fusion.place.refs_0_, s32[32]{0:T(128)S(1)} %stack.161.order, s32[128]{0:T(128)S(1)} %collective-permute-done.1.lists, bf16[64,2,128,128]{3,2,1,0:T(8,128)(2,1)} %collective-permute-done.2.source), custom_call_target="tpu_custom_call" | custom-call | bytes 8388608 | tf_op jit(solution)/shard_map/pallas_call | solution.py:128
  29.8 2.7 %collective-permute-start.16 = (bf16[512,256]{1,0:T(8,128)(2,1)S(1)}, bf16[512,256]{1,0:T(8,128)(2,1)S(1)}, u32[]{:S(2)}, u32[]{:S(2)}) collective-permute-start(bf16[512,256]{1,0:T(8,128)(2,1)S(1)} %get-tuple-element.76), channel_id=1, source_target_pairs={{0,48},{1,7},{2,50},{3,1},{4,52},{5,3},{6,54},{7,5},{8,56},{9,15},... | collective-permute-start | bytes 786440 | tf_op jit(solution)/shard_map/ppermute | solution.py:77
  32.4 1.8 %shard_map.85 = (bf16[256,3072]{1,0:T(8,128)(2,1)S(1)}, bf16[256,4096]{1,0:T(8,128)(2,1)S(1)}, bf16[256,1024]{1,0:T(8,128)(2,1)S(1)}) custom-call(s32[2]{0:T(128)S(1)} %pad_add_fusion.place.refs_0_, s32[32]{0:T(128)S(1)} %stack.161.order, s32[128]{0:T(128)S(1)} %reshape.10.lists, bf16[64,2,128,128]{3,2,1,0:T(8,128)(2,1)S(1)} %bitcast.40), custom_call_target="tpu_custom_call" | custom-call | bytes 8388608 | tf_op jit(solution)/shard_map/pallas_call | solution.py:128
  36.6 2.5 %collective-permute-start.12 = (bf16[512,256]{1,0:T(8,128)(2,1)S(1)}, bf16[512,256]{1,0:T(8,128)(2,1)S(1)}, u32[]{:S(2)}, u32[]{:S(2)}) collective-permute-start(bf16[512,256]{1,0:T(8,128)(2,1)S(1)} %get-tuple-element.68), channel_id=1, source_target_pairs={{0,48},{1,7},{2,50},{3,1},{4,52},{5,3},{6,54},{7,5},{8,56},{9,15},... | collective-permute-start | bytes 786440 | tf_op jit(solution)/shard_map/ppermute | solution.py:77
  43.9 2.8 %collective-permute-start.17 = (bf16[256,256]{1,0:T(8,128)(2,1)S(1)}, bf16[256,256]{1,0:T(8,128)(2,1)S(1)}, u32[]{:S(2)}, u32[]{:S(2)}) collective-permute-start(bf16[256,256]{1,0:T(8,128)(2,1)S(1)} %get-tuple-element.79), channel_id=1, source_target_pairs={{0,64},{1,65},{2,66},{3,67},{4,68},{5,69},{6,70},{7,71},{8,72},{9,... | collective-permute-start | bytes 393224 | tf_op jit(solution)/shard_map/ppermute | solution.py:77
  46.8 2.6 %collective-permute-done.17.got = bf16[256,256]{1,0:T(8,128)(2,1)S(1)} collective-permute-done((bf16[256,256]{1,0:T(8,128)(2,1)S(1)}, bf16[256,256]{1,0:T(8,128)(2,1)S(1)}, u32[]{:S(2)}, u32[]{:S(2)}) %collective-permute-start.17) | collective-permute-done | bytes 131104 | tf_op jit(solution)/shard_map/ppermute | solution.py:77
  49.4 6.5 %collective-permute-start.18 = (f32[256,256]{1,0:T(8,128)S(1)}, f32[256,256]{1,0:T(8,128)S(1)}, u32[]{:S(2)}, u32[]{:S(2)}) collective-permute-start(f32[256,256]{1,0:T(8,128)S(1)} %shard_map.96.half_sum), channel_id=1, source_target_pairs={{0,1},{1,0},{2,3},{3,2},{4,5},{5,4},{6,7},{7,6},{8,9},{9,8},{10,11... | collective-permute-start | bytes 786440 | tf_op jit(solution)/shard_map/ppermute | solution.py:77
  57.4 2.0 %shard_map.97 = (bf16[128,512]{1,0:T(8,128)(2,1)}, bf16[512,256]{1,0:T(8,128)(2,1)S(1)}, bf16[512,256]{1,0:T(8,128)(2,1)S(1)}, bf16[256,256]{1,0:T(8,128)(2,1)S(1)}, bf16[256,256]{1,0:T(8,128)(2,1)S(1)}) custom-call(s32[2]{0:T(128)S(1)} %pad_add_fusion.place.refs_0_, s32[2]{0:T(128)S(1)} %broadcast_select_fusion.ring, f32[256,256]{1,0:T(8,128)S(1)} %shard_map.96.half_sum, ...), custom_call_target="tpu_custom_call" | custom-call | tf_op jit(solution)/shard_map/pallas_call | solution.py:421
  59.3 3.0 %collective-permute-start.22 = (bf16[512,256]{1,0:T(8,128)(2,1)S(1)}, bf16[512,256]{1,0:T(8,128)(2,1)S(1)}, u32[]{:S(2)}, u32[]{:S(2)}) collective-permute-start(bf16[512,256]{1,0:T(8,128)(2,1)S(1)} %get-tuple-element.83), channel_id=1, source_target_pairs={{0,6},{1,49},{2,0},{3,51},{4,2},{5,53},{6,4},{7,55},{8,14},{9,57},... | collective-permute-start | bytes 786440 | tf_op jit(solution)/shard_map/ppermute | solution.py:77
  64.7 4.2 %collective-permute-done.20.refs_0_ = bf16[256,256]{1,0:T(8,128)(2,1)S(1)} collective-permute-done((bf16[256,256]{1,0:T(8,128)(2,1)S(1)}, bf16[256,256]{1,0:T(8,128)(2,1)S(1)}, u32[]{:S(2)}, u32[]{:S(2)}) %collective-permute-start.20) | collective-permute-done | bytes 131104 | tf_op jit(solution)/shard_map/ppermute | solution.py:77
  70.6 2.5 %collective-permute-start.29 = (bf16[1280,256]{1,0:T(8,128)(2,1)S(1)}, bf16[1280,256]{1,0:T(8,128)(2,1)S(1)}, u32[]{:S(2)}, u32[]{:S(2)}) collective-permute-start(bf16[1280,256]{1,0:T(8,128)(2,1)S(1)} %get-tuple-element.92.refs_2_), channel_id=1, source_target_pairs={{0,48},{1,7},{2,50},{3,1},{4,52},{5,3},{6,54},{7,5},{8,56},{9,15},... | collective-permute-start | bytes 1966088 | tf_op jit(solution)/shard_map/ppermute | solution.py:77
  74.6 5.3 %collective-permute-done.24.refs_1_ = bf16[512,256]{1,0:T(8,128)(2,1)S(1)} collective-permute-done((bf16[512,256]{1,0:T(8,128)(2,1)S(1)}, bf16[512,256]{1,0:T(8,128)(2,1)S(1)}, u32[]{:S(2)}, u32[]{:S(2)}) %collective-permute-start.24) | collective-permute-done | bytes 262176 | tf_op jit(solution)/shard_map/ppermute | solution.py:77
  81.5 2.7 %collective-permute-start.27 = (bf16[1024,256]{1,0:T(8,128)(2,1)S(1)}, bf16[1024,256]{1,0:T(8,128)(2,1)S(1)}, u32[]{:S(2)}, u32[]{:S(2)}) collective-permute-start(bf16[1024,256]{1,0:T(8,128)(2,1)S(1)} %shard_map.99.refs_2_), channel_id=1, source_target_pairs={{0,48},{1,7},{2,50},{3,1},{4,52},{5,3},{6,54},{7,5},{8,56},{9,15},... | collective-permute-start | bytes 1572872 | tf_op jit(solution)/shard_map/ppermute | solution.py:77
  84.3 2.7 %collective-permute-start.36 = (bf16[512,256]{1,0:T(8,128)(2,1)S(1)}, bf16[512,256]{1,0:T(8,128)(2,1)S(1)}, u32[]{:S(2)}, u32[]{:S(2)}) collective-permute-start(bf16[512,256]{1,0:T(8,128)(2,1)S(1)} %get-tuple-element.99), channel_id=1, source_target_pairs={{0,48},{1,7},{2,50},{3,1},{4,52},{5,3},{6,54},{7,5},{8,56},{9,15},... | collective-permute-start | bytes 786440 | tf_op jit(solution)/shard_map/ppermute | solution.py:77
  87.0 4.1 %collective-permute-done.26.left.refs_5_ = bf16[1024,256]{1,0:T(8,128)(2,1)S(1)} collective-permute-done((bf16[1024,256]{1,0:T(8,128)(2,1)S(1)}, bf16[1024,256]{1,0:T(8,128)(2,1)S(1)}, u32[]{:S(2)}, u32[]{:S(2)}) %collective-permute-start.26) | collective-permute-done | bytes 524320 | tf_op jit(solution)/shard_map/ppermute | solution.py:77
  91.2 2.7 %collective-permute-start.35 = (bf16[512,256]{1,0:T(8,128)(2,1)S(1)}, bf16[512,256]{1,0:T(8,128)(2,1)S(1)}, u32[]{:S(2)}, u32[]{:S(2)}) collective-permute-start(bf16[512,256]{1,0:T(8,128)(2,1)S(1)} %get-tuple-element.97), channel_id=1, source_target_pairs={{0,48},{1,7},{2,50},{3,1},{4,52},{5,3},{6,54},{7,5},{8,56},{9,15},... | collective-permute-start | bytes 786440 | tf_op jit(solution)/shard_map/ppermute | solution.py:77
  95.6 2.8 %collective-permute-start.32 = (bf16[256,256]{1,0:T(8,128)(2,1)S(1)}, bf16[256,256]{1,0:T(8,128)(2,1)S(1)}, u32[]{:S(2)}, u32[]{:S(2)}) collective-permute-start(bf16[256,256]{1,0:T(8,128)(2,1)S(1)} %add_convert_fusion.1), channel_id=1, source_target_pairs={{0,64},{1,65},{2,66},{3,67},{4,68},{5,69},{6,70},{7,71},{8,72},{9,... | collective-permute-start | bytes 393224 | tf_op jit(solution)/shard_map/ppermute | solution.py:77
  103.9 2.8 %collective-permute-start.37 = (bf16[256,256]{1,0:T(8,128)(2,1)S(1)}, bf16[256,256]{1,0:T(8,128)(2,1)S(1)}, u32[]{:S(2)}, u32[]{:S(2)}) collective-permute-start(bf16[256,256]{1,0:T(8,128)(2,1)S(1)} %add_convert_fusion.part.mine), channel_id=1, source_target_pairs={{0,2},{1,17},{2,0},{3,19},{4,6},{5,21},{6,4},{7,23},{8,10},{9,25},... | collective-permute-start | bytes 393224 | tf_op jit(solution)/shard_map/ppermute | solution.py:77
  109.2 5.6 %collective-permute-start.39 = (bf16[640,256]{1,0:T(8,128)(2,1)S(1)}, bf16[640,256]{1,0:T(8,128)(2,1)S(1)}, u32[]{:S(2)}, u32[]{:S(2)}) collective-permute-start(bf16[640,256]{1,0:T(8,128)(2,1)S(1)} %get-tuple-element.105), channel_id=1, source_target_pairs={{0,1},{1,0},{2,3},{3,2},{4,5},{5,4},{6,7},{7,6},{8,9},{9,8},{10,11... | collective-permute-start | bytes 983048 | tf_op jit(solution)/shard_map/ppermute | solution.py:77
  (98 shorter events, 44.7 us)
Async XLA Ops:
  4.6 18.3 %collective-permute-start.2 = (bf16[64,2,128,128]{3,2,1,0:T(8,128)(2,1)}, bf16[64,2,128,128]{3,2,1,0:T(8,128)(2,1)}, u32[]{:S(2)}, u32[]{:S(2)}) collective-permute-start(bf16[64,2,128,128]{3,2,1,0:T(8,128)(2,1)} %bitcast.39), channel_id=1, source_target_pairs={{0,1},{1,0},{2,3},{3,2},{4,5},{5,4},{6,7},{7,6},{8,9},{9,8},{10,11... | collective-permute-start | bytes 12582920 | tf_op jit(solution)/shard_map/ppermute | solution.py:77
  15.8 10.8 %collective-permute-start.7 = (bf16[512,256]{1,0:T(8,128)(2,1)S(1)}, bf16[512,256]{1,0:T(8,128)(2,1)S(1)}, u32[]{:S(2)}, u32[]{:S(2)}) collective-permute-start(bf16[512,256]{1,0:T(8,128)(2,1)S(1)} %get-tuple-element.61), channel_id=1, source_target_pairs={{0,8},{1,9},{2,10},{3,11},{4,12},{5,13},{6,14},{7,15},{8,0},{9,1},... | collective-permute-start | bytes 786440 | tf_op jit(solution)/shard_map/ppermute | solution.py:77
  16.1 10.4 %collective-permute-start.8 = (bf16[256,256]{1,0:T(8,128)(2,1)S(1)}, bf16[256,256]{1,0:T(8,128)(2,1)S(1)}, u32[]{:S(2)}, u32[]{:S(2)}) collective-permute-start(bf16[256,256]{1,0:T(8,128)(2,1)S(1)} %collective-permute-done.3.refs_0_), channel_id=1, source_target_pairs={{0,4},{1,33},{2,6},{3,35},{4,0},{5,37},{6,2},{7,39},{8,12},{9,41},... | collective-permute-start | bytes 393224 | tf_op jit(solution)/shard_map/ppermute | solution.py:77
  20.1 9.5 %collective-permute-start.13 = (bf16[1024,256]{1,0:T(8,128)(2,1)S(1)}, bf16[1024,256]{1,0:T(8,128)(2,1)S(1)}, u32[]{:S(2)}, u32[]{:S(2)}) collective-permute-start(bf16[1024,256]{1,0:T(8,128)(2,1)S(1)} %get-tuple-element.77.refs_2_), channel_id=1, source_target_pairs={{0,16},{1,3},{2,18},{3,5},{4,20},{5,7},{6,22},{7,1},{8,24},{9,11},... | collective-permute-start | bytes 1572872 | tf_op jit(solution)/shard_map/ppermute | solution.py:77
  20.9 8.7 %collective-permute-start.14 = (bf16[1024,256]{1,0:T(8,128)(2,1)S(1)}, bf16[1024,256]{1,0:T(8,128)(2,1)S(1)}, u32[]{:S(2)}, u32[]{:S(2)}) collective-permute-start(bf16[1024,256]{1,0:T(8,128)(2,1)S(1)} %get-tuple-element.77.refs_2_), channel_id=1, source_target_pairs={{0,48},{1,7},{2,50},{3,1},{4,52},{5,3},{6,54},{7,5},{8,56},{9,15},... | collective-permute-start | bytes 1572872 | tf_op jit(solution)/shard_map/ppermute | solution.py:77
  26.6 8.4 %collective-permute-start.10 = (bf16[1024,256]{1,0:T(8,128)(2,1)S(1)}, bf16[1024,256]{1,0:T(8,128)(2,1)S(1)}, u32[]{:S(2)}, u32[]{:S(2)}) collective-permute-start(bf16[1024,256]{1,0:T(8,128)(2,1)S(1)} %shard_map.90.refs_2_), channel_id=1, source_target_pairs={{0,48},{1,7},{2,50},{3,1},{4,52},{5,3},{6,54},{7,5},{8,56},{9,15},... | collective-permute-start | bytes 1572872 | tf_op jit(solution)/shard_map/ppermute | solution.py:77
  26.7 9.6 %collective-permute-start.9 = (bf16[1024,256]{1,0:T(8,128)(2,1)S(1)}, bf16[1024,256]{1,0:T(8,128)(2,1)S(1)}, u32[]{:S(2)}, u32[]{:S(2)}) collective-permute-start(bf16[1024,256]{1,0:T(8,128)(2,1)S(1)} %shard_map.90.refs_2_), channel_id=1, source_target_pairs={{0,16},{1,3},{2,18},{3,5},{4,20},{5,7},{6,22},{7,1},{8,24},{9,11},... | collective-permute-start | bytes 1572872 | tf_op jit(solution)/shard_map/ppermute | solution.py:77
  29.7 10.3 %collective-permute-start.15 = (bf16[512,256]{1,0:T(8,128)(2,1)S(1)}, bf16[512,256]{1,0:T(8,128)(2,1)S(1)}, u32[]{:S(2)}, u32[]{:S(2)}) collective-permute-start(bf16[512,256]{1,0:T(8,128)(2,1)S(1)} %get-tuple-element.75), channel_id=1, source_target_pairs={{0,16},{1,3},{2,18},{3,5},{4,20},{5,7},{6,22},{7,1},{8,24},{9,11},... | collective-permute-start | bytes 786440 | tf_op jit(solution)/shard_map/ppermute | solution.py:77
  29.8 10.3 %collective-permute-start.16 = (bf16[512,256]{1,0:T(8,128)(2,1)S(1)}, bf16[512,256]{1,0:T(8,128)(2,1)S(1)}, u32[]{:S(2)}, u32[]{:S(2)}) collective-permute-start(bf16[512,256]{1,0:T(8,128)(2,1)S(1)} %get-tuple-element.76), channel_id=1, source_target_pairs={{0,48},{1,7},{2,50},{3,1},{4,52},{5,3},{6,54},{7,5},{8,56},{9,15},... | collective-permute-start | bytes 786440 | tf_op jit(solution)/shard_map/ppermute | solution.py:77
  49.4 8.0 %collective-permute-start.18 = (f32[256,256]{1,0:T(8,128)S(1)}, f32[256,256]{1,0:T(8,128)S(1)}, u32[]{:S(2)}, u32[]{:S(2)}) collective-permute-start(f32[256,256]{1,0:T(8,128)S(1)} %shard_map.96.half_sum), channel_id=1, source_target_pairs={{0,1},{1,0},{2,3},{3,2},{4,5},{5,4},{6,7},{7,6},{8,9},{9,8},{10,11... | collective-permute-start | bytes 786440 | tf_op jit(solution)/shard_map/ppermute | solution.py:77
  59.3 9.6 %collective-permute-start.21 = (bf16[512,256]{1,0:T(8,128)(2,1)S(1)}, bf16[512,256]{1,0:T(8,128)(2,1)S(1)}, u32[]{:S(2)}, u32[]{:S(2)}) collective-permute-start(bf16[512,256]{1,0:T(8,128)(2,1)S(1)} %get-tuple-element.83), channel_id=1, source_target_pairs={{0,2},{1,17},{2,4},{3,19},{4,6},{5,21},{6,0},{7,23},{8,10},{9,25},... | collective-permute-start | bytes 786440 | tf_op jit(solution)/shard_map/ppermute | solution.py:77
  59.3 9.6 %collective-permute-start.22 = (bf16[512,256]{1,0:T(8,128)(2,1)S(1)}, bf16[512,256]{1,0:T(8,128)(2,1)S(1)}, u32[]{:S(2)}, u32[]{:S(2)}) collective-permute-start(bf16[512,256]{1,0:T(8,128)(2,1)S(1)} %get-tuple-element.83), channel_id=1, source_target_pairs={{0,6},{1,49},{2,0},{3,51},{4,2},{5,53},{6,4},{7,55},{8,14},{9,57},... | collective-permute-start | bytes 786440 | tf_op jit(solution)/shard_map/ppermute | solution.py:77
  62.3 8.0 %collective-permute-start.23 = (bf16[512,256]{1,0:T(8,128)(2,1)S(1)}, bf16[512,256]{1,0:T(8,128)(2,1)S(1)}, u32[]{:S(2)}, u32[]{:S(2)}) collective-permute-start(bf16[512,256]{1,0:T(8,128)(2,1)S(1)} %get-tuple-element.84), channel_id=1, source_target_pairs={{0,4},{1,33},{2,6},{3,35},{4,0},{5,37},{6,2},{7,39},{8,12},{9,41},... | collective-permute-start | bytes 786440 | tf_op jit(solution)/shard_map/ppermute | solution.py:77
  70.4 13.8 %collective-permute-start.28 = (bf16[1280,256]{1,0:T(8,128)(2,1)S(1)}, bf16[1280,256]{1,0:T(8,128)(2,1)S(1)}, u32[]{:S(2)}, u32[]{:S(2)}) collective-permute-start(bf16[1280,256]{1,0:T(8,128)(2,1)S(1)} %get-tuple-element.92.refs_2_), channel_id=1, source_target_pairs={{0,16},{1,3},{2,18},{3,5},{4,20},{5,7},{6,22},{7,1},{8,24},{9,11},... | collective-permute-start | bytes 1966088 | tf_op jit(solution)/shard_map/ppermute | solution.py:77
  70.6 13.6 %collective-permute-start.29 = (bf16[1280,256]{1,0:T(8,128)(2,1)S(1)}, bf16[1280,256]{1,0:T(8,128)(2,1)S(1)}, u32[]{:S(2)}, u32[]{:S(2)}) collective-permute-start(bf16[1280,256]{1,0:T(8,128)(2,1)S(1)} %get-tuple-element.92.refs_2_), channel_id=1, source_target_pairs={{0,48},{1,7},{2,50},{3,1},{4,52},{5,3},{6,54},{7,5},{8,56},{9,15},... | collective-permute-start | bytes 1966088 | tf_op jit(solution)/shard_map/ppermute | solution.py:77
  74.3 7.1 %collective-permute-start.25 = (bf16[256,256]{1,0:T(8,128)(2,1)S(1)}, bf16[256,256]{1,0:T(8,128)(2,1)S(1)}, u32[]{:S(2)}, u32[]{:S(2)}) collective-permute-start(bf16[256,256]{1,0:T(8,128)(2,1)S(1)} %collective-permute-done.20.refs_0_), channel_id=1, source_target_pairs={{0,4},{1,33},{2,6},{3,35},{4,0},{5,37},{6,2},{7,39},{8,12},{9,41},... | collective-permute-start | bytes 393224 | tf_op jit(solution)/shard_map/ppermute | solution.py:77
  81.5 9.6 %collective-permute-start.26 = (bf16[1024,256]{1,0:T(8,128)(2,1)S(1)}, bf16[1024,256]{1,0:T(8,128)(2,1)S(1)}, u32[]{:S(2)}, u32[]{:S(2)}) collective-permute-start(bf16[1024,256]{1,0:T(8,128)(2,1)S(1)} %shard_map.99.refs_2_), channel_id=1, source_target_pairs={{0,16},{1,3},{2,18},{3,5},{4,20},{5,7},{6,22},{7,1},{8,24},{9,11},... | collective-permute-start | bytes 1572872 | tf_op jit(solution)/shard_map/ppermute | solution.py:77
  81.5 9.5 %collective-permute-start.27 = (bf16[1024,256]{1,0:T(8,128)(2,1)S(1)}, bf16[1024,256]{1,0:T(8,128)(2,1)S(1)}, u32[]{:S(2)}, u32[]{:S(2)}) collective-permute-start(bf16[1024,256]{1,0:T(8,128)(2,1)S(1)} %shard_map.99.refs_2_), channel_id=1, source_target_pairs={{0,48},{1,7},{2,50},{3,1},{4,52},{5,3},{6,54},{7,5},{8,56},{9,15},... | collective-permute-start | bytes 1572872 | tf_op jit(solution)/shard_map/ppermute | solution.py:77
  84.3 11.0 %collective-permute-start.30 = (bf16[768,256]{1,0:T(8,128)(2,1)S(1)}, bf16[768,256]{1,0:T(8,128)(2,1)S(1)}, u32[]{:S(2)}, u32[]{:S(2)}) collective-permute-start(bf16[768,256]{1,0:T(8,128)(2,1)S(1)} %get-tuple-element.95), channel_id=1, source_target_pairs={{0,16},{1,3},{2,18},{3,5},{4,20},{5,7},{6,22},{7,1},{8,24},{9,11},... | collective-permute-start | bytes 1179656 | tf_op jit(solution)/shard_map/ppermute | solution.py:77
  84.3 14.0 %collective-permute-start.36 = (bf16[512,256]{1,0:T(8,128)(2,1)S(1)}, bf16[512,256]{1,0:T(8,128)(2,1)S(1)}, u32[]{:S(2)}, u32[]{:S(2)}) collective-permute-start(bf16[512,256]{1,0:T(8,128)(2,1)S(1)} %get-tuple-element.99), channel_id=1, source_target_pairs={{0,48},{1,7},{2,50},{3,1},{4,52},{5,3},{6,54},{7,5},{8,56},{9,15},... | collective-permute-start | bytes 786440 | tf_op jit(solution)/shard_map/ppermute | solution.py:77
  91.1 10.4 %collective-permute-start.34 = (bf16[512,256]{1,0:T(8,128)(2,1)S(1)}, bf16[512,256]{1,0:T(8,128)(2,1)S(1)}, u32[]{:S(2)}, u32[]{:S(2)}) collective-permute-start(bf16[512,256]{1,0:T(8,128)(2,1)S(1)} %get-tuple-element.91), channel_id=1, source_target_pairs={{0,16},{1,3},{2,18},{3,5},{4,20},{5,7},{6,22},{7,1},{8,24},{9,11},... | collective-permute-start | bytes 786440 | tf_op jit(solution)/shard_map/ppermute | solution.py:77
  91.2 10.3 %collective-permute-start.35 = (bf16[512,256]{1,0:T(8,128)(2,1)S(1)}, bf16[512,256]{1,0:T(8,128)(2,1)S(1)}, u32[]{:S(2)}, u32[]{:S(2)}) collective-permute-start(bf16[512,256]{1,0:T(8,128)(2,1)S(1)} %get-tuple-element.97), channel_id=1, source_target_pairs={{0,48},{1,7},{2,50},{3,1},{4,52},{5,3},{6,54},{7,5},{8,56},{9,15},... | collective-permute-start | bytes 786440 | tf_op jit(solution)/shard_map/ppermute | solution.py:77
  95.3 8.5 %collective-permute-start.31 = (bf16[256,256]{1,0:T(8,128)(2,1)S(1)}, bf16[256,256]{1,0:T(8,128)(2,1)S(1)}, u32[]{:S(2)}, u32[]{:S(2)}) collective-permute-start(bf16[256,256]{1,0:T(8,128)(2,1)S(1)} %add_convert_fusion.1), channel_id=1, source_target_pairs={{0,8},{1,9},{2,10},{3,11},{4,12},{5,13},{6,14},{7,15},{8,0},{9,1},... | collective-permute-start | bytes 393224 | tf_op jit(solution)/shard_map/ppermute | solution.py:77
  95.6 8.3 %collective-permute-start.32 = (bf16[256,256]{1,0:T(8,128)(2,1)S(1)}, bf16[256,256]{1,0:T(8,128)(2,1)S(1)}, u32[]{:S(2)}, u32[]{:S(2)}) collective-permute-start(bf16[256,256]{1,0:T(8,128)(2,1)S(1)} %add_convert_fusion.1), channel_id=1, source_target_pairs={{0,64},{1,65},{2,66},{3,67},{4,68},{5,69},{6,70},{7,71},{8,72},{9,... | collective-permute-start | bytes 393224 | tf_op jit(solution)/shard_map/ppermute | solution.py:77
  (21 other events, 129.7 us)

commit v4 on v3

--- a/solution.py
+++ b/solution.py
@@ -50,42 +50,33 @@
     ]
 
 
-def along_y(d):
-    return lambda r, z, x, y, c: (r, z, x, (y + d) % 4, c)
-
-
-def along_z(d):
-    return lambda r, z, x, y, c: (r, (z + d) % 4, x, y, c)
-
-
 def first_ring(d):
-    return pairs(lambda r, z, x, y, c: (along_z(d) if c else along_y(d))(r, z, x, y, c))
+    return pairs(lambda r, z, x, y, c: (r, z ^ d, x, y, c) if c else (r, z, x, y ^ d, c))
 
 
 def second_ring(d):
-    return pairs(lambda r, z, x, y, c: (along_y(d) if c else along_z(d))(r, z, x, y, c))
+    return pairs(lambda r, z, x, y, c: (r, z, x, y ^ d, c) if c else (r, z ^ d, x, y, c))
 
 
 TO_PLANE = pairs(lambda r, z, x, y, c: (r, z, 1 - x, y, c))
 TO_CORE = pairs(lambda r, z, x, y, c: (r, z, x, y, 1 - c))
 TO_REP = pairs(lambda r, z, x, y, c: (1 - r, z, x, y, c))
 TO_PLANE_REP = pairs(lambda r, z, x, y, c: (1 - r, z, 1 - x, y, c))
-NEAR = pairs(lambda r, z, x, y, c: (r, z ^ 1, x, y, c) if c else (r, z, x, y ^ 1, c))
 
 
 def move(value, wiring):
     return lax.ppermute(value, AXES, wiring)
 
 
-FIRST = (0, -1, 1, 2)
+FIRST = (0, 1, 3, 2)
 GROUPS = (
-    ((0, 0, FIRST), (0, -1, FIRST), (0, 1, FIRST)),
+    ((0, 0, FIRST), (0, 1, FIRST), (0, 3, FIRST)),
     (
         (1, 0, FIRST),
         (0, 2, FIRST[:2]),
         (0, 2, FIRST[2:]),
-        (1, -1, FIRST),
         (1, 1, FIRST),
+        (1, 3, FIRST),
     ),
     ((1, 2, FIRST[:2]), (1, 2, FIRST[2:])),
 )
@@ -98,8 +89,8 @@
     for group in GROUPS:
         for plane, second, firsts in group:
             for first in firsts:
-                zz = jnp.where(c == 0, z + second, z + first) & 3
-                yy = jnp.where(c == 0, y + first, y + second) & 3
+                zz = jnp.where(c == 0, z ^ second, z ^ first)
+                yy = jnp.where(c == 0, y ^ first, y ^ second)
                 xx = x if plane == 0 else 1 - x
                 chips.append((zz * 2 + xx) * 4 + yy)
     return jnp.stack(chips).astype(jnp.int32)
@@ -112,7 +103,7 @@
         for i in range(size):
             for q in range(2):
                 tile_at = 2 * order[at + i] + (c if q == 0 else 1 - c)
-                one, two = lists[2 * tile_at], lists[2 * tile_at + 1]
+                one, two = lists[0, tile_at], lists[1, tile_at]
                 for h in range(2):
                     present = jnp.where(jnp.logical_or(one == h, two == h), 1.0, 0.0)
                     keep = jnp.full((16, T), present, jnp.float32)
@@ -190,7 +181,7 @@
 
 
 def row_kernel(extra, *refs):
-    _, left, right, far, block = refs[:5]
+    right, left, far, _, block = refs[:5]
     refs = refs[5:]
     if extra:
         piece, refs = refs[0], refs[1:]
@@ -207,11 +198,11 @@
         row[4 * rows :] = (pair + others).astype(row.dtype)
 
 
-def join_rows_kernel(*refs):
-    at, out = 0, refs[-1]
-    for part in refs[:-1]:
-        out[at : at + part.shape[0]] = part[...]
-        at += part.shape[0]
+def theirs_kernel(far, rest, first, out):
+    rows = 2 * T
+    out[:rows] = first[...]
+    out[rows : 3 * rows] = rest[...]
+    out[3 * rows :] = far[...]
 
 
 def far_kernel(left, right, out_a, out_b):
@@ -243,38 +234,37 @@
     other = move(block, TO_PLANE)
     from_far = move(to_far, first_ring(2))
     from_left = move(to_side, first_ring(1))
-    from_right = move(to_side, first_ring(-1))
+    from_right = move(to_side, first_ring(3))
     more = 2 * T if extra else 0
     mine, rest = local_call(
         functools.partial(row_kernel, extra),
         (bf16(8 * T + more, H), bf16(4 * T, H)),
+        from_right,
+        from_left,
+        from_far,
         other,
-        from_left,
-        from_right,
-        from_far,
         block,
         *([piece] if extra else []),
     )
     other_rest = move(rest, TO_PLANE)
     other_far = move(other, first_ring(2))
     left = move(mine, second_ring(1))
-    right = move(mine, second_ring(-1))
-    panels_sib = get_sib(mine)
-    other_rest = after(other_rest, panels_sib[0])
-    theirs = local_call(join_rows_kernel, bf16(8 * T, H), other, other_rest, other_far)
+    right = move(mine, second_ring(3))
+    theirs = local_call(theirs_kernel, bf16(8 * T, H), other_far, other_rest, other)
     left_x = move(theirs, second_ring(1))
-    right_x = move(theirs, second_ring(-1))
+    right_x = move(theirs, second_ring(3))
     left, right, theirs_here = lax.optimization_barrier((left, right, theirs))
-    to_a, to_b = local_call(far_kernel, (bf16(4 * T + more, H), bf16(4 * T, H)), left, right)
+    to_a, to_b = local_call(far_kernel, (bf16(4 * T + more, H), bf16(4 * T, H)), right, left)
     far_a = move(to_a, second_ring(1))
-    far_b = move(to_b, second_ring(-1))
+    far_b = move(to_b, second_ring(3))
     part = f32(4 * T, H)
-    panels_own = get_own(block)
+    panels_sib = get_sib(to_b)
+    left_x, right_x, _ = lax.optimization_barrier((left_x, right_x, panels_sib[0]))
+    to_a, to_b = local_call(far_kernel, (bf16(4 * T, H), bf16(4 * T, H)), right_x, left_x)
+    panels_own = get_own(to_b)
     panels = tuple(zip(panels_own, panels_sib))
-    left_x, right_x, _ = lax.optimization_barrier((left_x, right_x, panels_own[0]))
-    to_a, to_b = local_call(far_kernel, (bf16(4 * T, H), bf16(4 * T, H)), left_x, right_x)
     far_ax = move(to_a, second_ring(1))
-    far_bx = move(to_b, second_ring(-1))
+    far_bx = move(to_b, second_ring(3))
     mine = after(mine, to_a)
     total = product(place, panels[0], (4, 4, 4), (mine, left, right), None, part)
     total = product(
@@ -295,11 +285,10 @@
     return outs, whole.astype(jnp.bfloat16)
 
 
-def split_kernel(place, rows, here, there):
-    low, high = rows[:, :H], rows[:, H:]
+def pair_kernel(place, here, there, out):
     first = place[1] == 0
-    here[...] = jnp.where(first, low, high)
-    there[...] = jnp.where(first, high, low)
+    for s, rows in enumerate((here, there)):
+        out[s * T : (s + 1) * T] = jnp.where(first, rows[:, :H], rows[:, H:])
 
 
 def add_kernel(keep, got, out):
@@ -354,8 +343,20 @@
     to_core[3 * T :] = near[...]
 
 
-def final_kernel(place, mine, core, weight, out):
+def final_kernel(place, ring, mine, core, weight, part, near, out, term):
     c = place[1]
+    p, q = ring[0] & 1, ring[1] & 1
+    halves = (
+        (part[...], c, p),
+        (near[...], c, 1 - p),
+        (core[T : 3 * T], 1 - c, q),
+        (core[3 * T :], 1 - c, 1 - q),
+    )
+    for half, side, at in halves:
+        rows = pl.ds(pl.multiple_of(side * H + at * T, T), T)
+        value = half.astype(jnp.float32)
+        term[rows, :H] = value[:T]
+        term[rows, H:] = value[T:]
     low = jnp.where(c == 0, mine[...], core[:T])
     high = jnp.where(c == 0, core[:T], mine[...])
     contract = (((1,), (1,)), ((), ()))
@@ -365,22 +366,6 @@
     ).astype(out.dtype)
 
 
-def join_kernel(place, ring, mine, near, core, out):
-    c = place[1]
-    p, q = ring[0] & 1, ring[1] & 1
-    parts = (
-        (mine[...], c, p),
-        (near[...], c, 1 - p),
-        (core[T : 3 * T], 1 - c, q),
-        (core[3 * T :], 1 - c, 1 - q),
-    )
-    for part, side, half in parts:
-        rows = pl.ds(pl.multiple_of(side * H + half * T, T), T)
-        value = part.astype(jnp.float32)
-        out[rows, :H] = value[:T]
-        out[rows, H:] = value[T:]
-
-
 def on_device(features, weight, tile_values, tile_list, train_mask, cotangent):
     r = lax.axis_index("rep")
     b = lax.axis_index("blk")
@@ -389,21 +374,22 @@
     ring = jnp.where(c == 0, jnp.stack([y, z]), jnp.stack([z, y])).astype(jnp.int32)
     order = chip_order(z, x, y, c)
 
-    here, there = local_call(split_kernel, (bf16(T, H), bf16(T, H)), place, features)
-    block = local_call(join_rows_kernel, bf16(2 * T, H), here, move(there, TO_CORE))
+    lists = tile_list[0, 0].T
+    there, lists_sibling = lax.optimization_barrier(
+        (move(features, TO_CORE), move(lists, TO_CORE))
+    )
+    block = local_call(pair_kernel, bf16(2 * T, H), place, features, there)
 
     own = tile_values[0, 0]
-    lists = tile_list.reshape(T)
     factor = cotangent * train_mask.astype(jnp.bfloat16)[:, None]
     sibling = move(after(own, block), TO_CORE)
-    lists_sibling = move(after(lists, block), TO_CORE)
     factor_sibling = move(after(factor, block), TO_CORE)
 
     panels = {}
 
     def lay_out(name, lists, source):
         def now(started):
-            panels[name] = lay_out_tiles(place, order, lists, source)
+            panels[name] = lay_out_tiles(place, after(order, started), lists, source)
             return panels[name]
 
         return now
@@ -442,16 +428,21 @@
         lambda started: panels["sibling"],
         (f32(2 * T, H), bf16(2 * T, H)),
     )
-    near = move(part, NEAR)
+    near = move(part, first_ring(1))
     mine, to_core = local_call(
         settle_kernel, (bf16(T, H), bf16(5 * T, H)), keep, move(send, TO_REP), part, near
     )
     got_core = move(to_core, TO_CORE)
-    feature_grad = local_call(
-        final_kernel, bf16(T, 2 * H), place, mine, got_core, weight
-    )
-    weight_grad = local_call(
-        join_kernel, f32(2 * H, 2 * H), place, ring, part, near, got_core
+    feature_grad, weight_grad = local_call(
+        final_kernel,
+        (bf16(T, 2 * H), f32(2 * H, 2 * H)),
+        place,
+        ring,
+        mine,
+        got_core,
+        weight,
+        part,
+        near,
     )
     return (act, weight_grad, feature_grad)
 

time: 119 us -> 114 us (0.958)
  starting transfers between devices: 61.9 us -> 55 us
  waiting for transfers between devices: 36.2 us -> 38.1 us
    ppermute x40, starting transfers between devices: 61.9 us -> 55 us  [move(): return lax.ppermute(value, AXES, wiring)]
    ppermute x40, waiting for transfers between devices: 36.2 us -> 38.1 us  [move(): return lax.ppermute(value, AXES, wiring)]
    pallas_call x14 -> x12, Pallas kernels: 4.1 us -> 3.58 us  [local_call(): pl.pallas_call(kernel, out_shape=out_shape, in_specs=[SMEM if a.dtype ==...]
  transfers between devices with their start and end apart: 40 -> 40, of which waited for: 19 -> 22; matrix products, arithmetic and copies ran while one was open for 1% -> 0% of each run, Pallas kernels for 9% -> 11%
where the time goes in v4:
time: 114 us
  starting transfers between devices  55 us (48%)
  waiting for transfers between devices  38.1 us (33%)
  Pallas kernels  18.3 us (16%)
    ppermute x40, starting transfers between devices, move(): return lax.ppermute(value, AXES, wiring)  55 us
    ppermute x40, waiting for transfers between devices, move(): return lax.ppermute(value, AXES, wiring)  38.1 us
    pallas_call x6, Pallas kernels, product(): pl.pallas_call(functools.partial(product_kernel, counts, total is not Non...  7.35 us
    pallas_call x2, Pallas kernels, lay_out_tiles(): pl.pallas_call(tiles_kernel, out_shape=tuple((bf16(2 * T, n * 2 * T) for...  5.4 us
    pallas_call x12, Pallas kernels, local_call(): pl.pallas_call(kernel, out_shape=out_shape, in_specs=[SMEM if a.dtype ==...  3.58 us
  transfers between devices with their start and end apart: 40, of which 22 were waited for; matrix products, arithmetic and copies ran while one was open for 0% of the time, Pallas kernels for 11%

profile of v4, /device:TPU:1, one launch (start us, length us, event | category | flops | bytes accessed | tf_op | source)
XLA Modules:
  0.0 113.8 jit_solution(6917453852000020234)
XLA Ops:
  5.2 3.7 %collective-permute-start.6 = (bf16[256,256]{1,0:T(8,128)(2,1)S(1)}, bf16[256,256]{1,0:T(8,128)(2,1)S(1)}, u32[]{:S(2)}, u32[]{:S(2)}) collective-permute-start(bf16[256,256]{1,0:T(8,128)(2,1)S(1)} %shard_map.85.refs_4_), channel_id=1, source_target_pairs={{0,4},{1,33},{2,6},{3,35},{4,0},{5,37},{6,2},{7,39},{8,12},{9,41},... | collective-permute-start | bytes 393224 | tf_op jit(solution)/shard_map/ppermute | solution.py:68
  11.6 2.1 %collective-permute-done.5.refs_1_ = bf16[256,256]{1,0:T(8,128)(2,1)S(1)} collective-permute-done((bf16[256,256]{1,0:T(8,128)(2,1)S(1)}, bf16[256,256]{1,0:T(8,128)(2,1)S(1)}, u32[]{:S(2)}, u32[]{:S(2)}) %collective-permute-start.5) | collective-permute-done | bytes 131104 | tf_op jit(solution)/shard_map/ppermute | solution.py:68
  17.6 2.7 %collective-permute-start.11 = (bf16[1024,256]{1,0:T(8,128)(2,1)S(1)}, bf16[1024,256]{1,0:T(8,128)(2,1)S(1)}, u32[]{:S(2)}, u32[]{:S(2)}) collective-permute-start(bf16[1024,256]{1,0:T(8,128)(2,1)S(1)} %get-tuple-element.78.refs_2_), channel_id=1, source_target_pairs={{0,48},{1,7},{2,50},{3,5},{4,52},{5,3},{6,54},{7,1},{8,56},{9,15},... | collective-permute-start | bytes 1572872 | tf_op jit(solution)/shard_map/ppermute | solution.py:68
  22.3 2.4 %collective-permute-start.9 = (bf16[1024,256]{1,0:T(8,128)(2,1)S(1)}, bf16[1024,256]{1,0:T(8,128)(2,1)S(1)}, u32[]{:S(2)}, u32[]{:S(2)}) collective-permute-start(bf16[1024,256]{1,0:T(8,128)(2,1)S(1)} %shard_map.87.refs_2_), channel_id=1, source_target_pairs={{0,48},{1,7},{2,50},{3,5},{4,52},{5,3},{6,54},{7,1},{8,56},{9,15},... | collective-permute-start | bytes 1572872 | tf_op jit(solution)/shard_map/ppermute | solution.py:68
  24.7 3.9 %collective-permute-done.11.left.refs_4_ = bf16[1024,256]{1,0:T(8,128)(2,1)S(1)} collective-permute-done((bf16[1024,256]{1,0:T(8,128)(2,1)S(1)}, bf16[1024,256]{1,0:T(8,128)(2,1)S(1)}, u32[]{:S(2)}, u32[]{:S(2)}) %collective-permute-start.11) | collective-permute-done | bytes 524320 | tf_op jit(solution)/shard_map/ppermute | solution.py:68
  32.2 3.6 %shard_map.89 = (bf16[256,3072]{1,0:T(8,128)(2,1)S(1)}, bf16[256,4096]{1,0:T(8,128)(2,1)S(1)}, bf16[256,1024]{1,0:T(8,128)(2,1)S(1)}) custom-call(s32[2]{0:T(128)S(1)} %pad_add_fusion.place.refs_0_, s32[32]{0:T(128)S(1)} %stack.161.order, s32[2,64]{1,0:T(2,128)S(1)} %collective-permute-done.1.lists, bf16[64,2,128,128]{3,2,1,0:T(8,128)(2,1)} %collective-permute-done.12.source), custom_call_target="tpu_custom_call" | custom-call | bytes 8388608 | tf_op jit(solution)/shard_map/pallas_call | solution.py:119
  37.5 1.8 %shard_map.91 = (bf16[256,3072]{1,0:T(8,128)(2,1)S(1)}, bf16[256,4096]{1,0:T(8,128)(2,1)S(1)}, bf16[256,1024]{1,0:T(8,128)(2,1)S(1)}) custom-call(s32[2]{0:T(128)S(1)} %pad_add_fusion.place.refs_0_, s32[32]{0:T(128)S(1)} %stack.161.order, s32[2,64]{1,0:T(2,128)S(1)} %bitcast.43, bf16[64,2,128,128]{3,2,1,0:T(8,128)(2,1)S(1)} %bitcast.41), custom_call_target="tpu_custom_call" | custom-call | bytes 8388608 | tf_op jit(solution)/shard_map/pallas_call | solution.py:119
  40.3 2.2 %shard_map.93.refs_5_ = f32[512,256]{1,0:T(8,128)S(1)} custom-call(bf16[256,4096]{1,0:T(8,128)(2,1)S(1)} %get-tuple-element.73.refs_0_, bf16[256,4096]{1,0:T(8,128)(2,1)S(1)} %get-tuple-element.74.refs_1_, bf16[1024,256]{1,0:T(8,128)(2,1)S(1)} %shard_map.87.refs_2_, bf16[512,256]{1,0:T(8,128)(2,1)S(1)} %collective-permute-done.15.refs_3_, ...), custom_call_target="tpu_custom_call" | custom-call | flops 1073741824 | bytes 6815744 | tf_op jit(solution)/shard_map/pallas_call | solution.py:169
  43.7 2.5 %collective-permute-start.17 = (bf16[256,256]{1,0:T(8,128)(2,1)S(1)}, bf16[256,256]{1,0:T(8,128)(2,1)S(1)}, u32[]{:S(2)}, u32[]{:S(2)}) collective-permute-start(bf16[256,256]{1,0:T(8,128)(2,1)S(1)} %get-tuple-element.80), channel_id=1, source_target_pairs={{0,64},{1,65},{2,66},{3,67},{4,68},{5,69},{6,70},{7,71},{8,72},{9,... | collective-permute-start | bytes 393224 | tf_op jit(solution)/shard_map/ppermute | solution.py:68
  46.3 2.9 %collective-permute-done.17.got = bf16[256,256]{1,0:T(8,128)(2,1)S(1)} collective-permute-done((bf16[256,256]{1,0:T(8,128)(2,1)S(1)}, bf16[256,256]{1,0:T(8,128)(2,1)S(1)}, u32[]{:S(2)}, u32[]{:S(2)}) %collective-permute-start.17) | collective-permute-done | bytes 131104 | tf_op jit(solution)/shard_map/ppermute | solution.py:68
  49.2 5.6 %collective-permute-start.18 = (f32[256,256]{1,0:T(8,128)S(1)}, f32[256,256]{1,0:T(8,128)S(1)}, u32[]{:S(2)}, u32[]{:S(2)}) collective-permute-start(f32[256,256]{1,0:T(8,128)S(1)} %shard_map.95.half_sum), channel_id=1, source_target_pairs={{0,1},{1,0},{2,3},{3,2},{4,5},{5,4},{6,7},{7,6},{8,9},{9,8},{10,11... | collective-permute-start | bytes 786440 | tf_op jit(solution)/shard_map/ppermute | solution.py:68
  56.3 2.0 %shard_map.96 = (bf16[128,512]{1,0:T(8,128)(2,1)}, bf16[512,256]{1,0:T(8,128)(2,1)S(1)}, bf16[512,256]{1,0:T(8,128)(2,1)S(1)}, bf16[256,256]{1,0:T(8,128)(2,1)S(1)}, bf16[256,256]{1,0:T(8,128)(2,1)S(1)}) custom-call(s32[2]{0:T(128)S(1)} %pad_add_fusion.place.refs_0_, s32[2]{0:T(128)S(1)} %broadcast_select_fusion.ring, f32[256,256]{1,0:T(8,128)S(1)} %shard_map.95.half_sum, ...), custom_call_target="tpu_custom_call" | custom-call | tf_op jit(solution)/shard_map/pallas_call | solution.py:407
  59.8 1.7 %collective-permute-start.22 = (bf16[512,256]{1,0:T(8,128)(2,1)S(1)}, bf16[512,256]{1,0:T(8,128)(2,1)S(1)}, u32[]{:S(2)}, u32[]{:S(2)}) collective-permute-start(bf16[512,256]{1,0:T(8,128)(2,1)S(1)} %get-tuple-element.84), channel_id=1, source_target_pairs={{0,6},{1,49},{2,4},{3,51},{4,2},{5,53},{6,0},{7,55},{8,14},{9,57},... | collective-permute-start | bytes 786440 | tf_op jit(solution)/shard_map/ppermute | solution.py:68
  61.7 3.9 %collective-permute-done.20.refs_3_.first = bf16[256,256]{1,0:T(8,128)(2,1)S(1)} collective-permute-done((bf16[256,256]{1,0:T(8,128)(2,1)S(1)}, bf16[256,256]{1,0:T(8,128)(2,1)S(1)}, u32[]{:S(2)}, u32[]{:S(2)}) %collective-permute-start.20) | collective-permute-done | bytes 131104 | tf_op jit(solution)/shard_map/ppermute | solution.py:68
  69.6 1.9 %collective-permute-start.21 = (bf16[256,256]{1,0:T(8,128)(2,1)S(1)}, bf16[256,256]{1,0:T(8,128)(2,1)S(1)}, u32[]{:S(2)}, u32[]{:S(2)}) collective-permute-start(bf16[256,256]{1,0:T(8,128)(2,1)S(1)} %collective-permute-done.20.refs_3_.first), channel_id=1, source_target_pairs={{0,4},{1,33},{2,6},{3,35},{4,0},{5,37},{6,2},{7,39},{8,12},{9,41},... | collective-permute-start | bytes 393224 | tf_op jit(solution)/shard_map/ppermute | solution.py:68
  71.5 3.5 %collective-permute-done.21.far = bf16[256,256]{1,0:T(8,128)(2,1)S(1)} collective-permute-done((bf16[256,256]{1,0:T(8,128)(2,1)S(1)}, bf16[256,256]{1,0:T(8,128)(2,1)S(1)}, u32[]{:S(2)}, u32[]{:S(2)}) %collective-permute-start.21) | collective-permute-done | bytes 131104 | tf_op jit(solution)/shard_map/ppermute | solution.py:68
  75.7 1.8 %collective-permute-start.27 = (bf16[1024,256]{1,0:T(8,128)(2,1)S(1)}, bf16[1024,256]{1,0:T(8,128)(2,1)S(1)}, u32[]{:S(2)}, u32[]{:S(2)}) collective-permute-start(bf16[1024,256]{1,0:T(8,128)(2,1)S(1)} %shard_map.98.refs_2_), channel_id=1, source_target_pairs={{0,48},{1,7},{2,50},{3,5},{4,52},{5,3},{6,54},{7,1},{8,56},{9,15},... | collective-permute-start | bytes 1572872 | tf_op jit(solution)/shard_map/ppermute | solution.py:68
  77.5 1.9 %collective-permute-start.26 = (bf16[1024,256]{1,0:T(8,128)(2,1)S(1)}, bf16[1024,256]{1,0:T(8,128)(2,1)S(1)}, u32[]{:S(2)}, u32[]{:S(2)}) collective-permute-start(bf16[1024,256]{1,0:T(8,128)(2,1)S(1)} %shard_map.98.refs_2_), channel_id=1, source_target_pairs={{0,16},{1,3},{2,18},{3,1},{4,20},{5,7},{6,22},{7,5},{8,24},{9,11},... | collective-permute-start | bytes 1572872 | tf_op jit(solution)/shard_map/ppermute | solution.py:68
  82.4 3.9 %collective-permute-done.27.left.refs_6_ = bf16[1024,256]{1,0:T(8,128)(2,1)S(1)} collective-permute-done((bf16[1024,256]{1,0:T(8,128)(2,1)S(1)}, bf16[1024,256]{1,0:T(8,128)(2,1)S(1)}, u32[]{:S(2)}, u32[]{:S(2)}) %collective-permute-start.27) | collective-permute-done | bytes 524320 | tf_op jit(solution)/shard_map/ppermute | solution.py:68
  90.6 3.0 %collective-permute-start.37 = (bf16[256,256]{1,0:T(8,128)(2,1)S(1)}, bf16[256,256]{1,0:T(8,128)(2,1)S(1)}, u32[]{:S(2)}, u32[]{:S(2)}) collective-permute-start(bf16[256,256]{1,0:T(8,128)(2,1)S(1)} %add_convert_fusion.1), channel_id=1, source_target_pairs={{0,72},{1,73},{2,74},{3,75},{4,76},{5,77},{6,78},{7,79},{8,64},{9,... | collective-permute-start | bytes 393224 | tf_op jit(solution)/shard_map/ppermute | solution.py:68
  97.5 2.6 %collective-permute-start.34 = (bf16[256,256]{1,0:T(8,128)(2,1)S(1)}, bf16[256,256]{1,0:T(8,128)(2,1)S(1)}, u32[]{:S(2)}, u32[]{:S(2)}) collective-permute-start(bf16[256,256]{1,0:T(8,128)(2,1)S(1)} %get-tuple-element.100), channel_id=1, source_target_pairs={{0,64},{1,65},{2,66},{3,67},{4,68},{5,69},{6,70},{7,71},{8,72},{9,... | collective-permute-start | bytes 393224 | tf_op jit(solution)/shard_map/ppermute | solution.py:68
  100.9 3.1 %collective-permute-done.34.got = bf16[256,256]{1,0:T(8,128)(2,1)S(1)} collective-permute-done((bf16[256,256]{1,0:T(8,128)(2,1)S(1)}, bf16[256,256]{1,0:T(8,128)(2,1)S(1)}, u32[]{:S(2)}, u32[]{:S(2)}) %collective-permute-start.34) | collective-permute-done | bytes 131104 | tf_op jit(solution)/shard_map/ppermute | solution.py:68
  104.5 6.2 %collective-permute-start.39 = (bf16[640,256]{1,0:T(8,128)(2,1)S(1)}, bf16[640,256]{1,0:T(8,128)(2,1)S(1)}, u32[]{:S(2)}, u32[]{:S(2)}) collective-permute-start(bf16[640,256]{1,0:T(8,128)(2,1)S(1)} %get-tuple-element.106), channel_id=1, source_target_pairs={{0,1},{1,0},{2,3},{3,2},{4,5},{5,4},{6,7},{7,6},{8,9},{9,8},{10,11... | collective-permute-start | bytes 983048 | tf_op jit(solution)/shard_map/ppermute | solution.py:68
  112.0 1.8 %shard_map.105 = (bf16[128,512]{1,0:T(8,128)(2,1)}, f32[512,512]{1,0:T(8,128)}) custom-call(s32[2]{0:T(128)S(1)} %pad_add_fusion.place.refs_0_, s32[2]{0:T(128)S(1)} %broadcast_select_fusion.ring, bf16[128,256]{1,0:T(8,128)(2,1)S(1)} %get-tuple-element.105.mine, bf16[640,256]{1,0:T(8,128)(2,1)S(1)} %collective-permute-done.39.core, ...), custom_call_target="tpu_custom_call" | custom-call | tf_op jit(solution)/shard_map/pallas_call | solution.py:222
  (96 shorter events, 42.0 us)
Async XLA Ops:
  5.0 27.2 %collective-permute-start.12 = (bf16[64,2,128,128]{3,2,1,0:T(8,128)(2,1)}, bf16[64,2,128,128]{3,2,1,0:T(8,128)(2,1)}, u32[]{:S(2)}, u32[]{:S(2)}) collective-permute-start(bf16[64,2,128,128]{3,2,1,0:T(8,128)(2,1)} %bitcast.40), channel_id=1, source_target_pairs={{0,1},{1,0},{2,3},{3,2},{4,5},{5,4},{6,7},{7,6},{8,9},{9,8},{10,11... | collective-permute-start | bytes 12582920 | tf_op jit(solution)/shard_map/ppermute | solution.py:68
  15.0 7.2 %collective-permute-start.7 = (bf16[512,256]{1,0:T(8,128)(2,1)S(1)}, bf16[512,256]{1,0:T(8,128)(2,1)S(1)}, u32[]{:S(2)}, u32[]{:S(2)}) collective-permute-start(bf16[512,256]{1,0:T(8,128)(2,1)S(1)} %get-tuple-element.57), channel_id=1, source_target_pairs={{0,8},{1,9},{2,10},{3,11},{4,12},{5,13},{6,14},{7,15},{8,0},{9,1},... | collective-permute-start | bytes 786440 | tf_op jit(solution)/shard_map/ppermute | solution.py:68
  17.6 11.0 %collective-permute-start.11 = (bf16[1024,256]{1,0:T(8,128)(2,1)S(1)}, bf16[1024,256]{1,0:T(8,128)(2,1)S(1)}, u32[]{:S(2)}, u32[]{:S(2)}) collective-permute-start(bf16[1024,256]{1,0:T(8,128)(2,1)S(1)} %get-tuple-element.78.refs_2_), channel_id=1, source_target_pairs={{0,48},{1,7},{2,50},{3,5},{4,52},{5,3},{6,54},{7,1},{8,56},{9,15},... | collective-permute-start | bytes 1572872 | tf_op jit(solution)/shard_map/ppermute | solution.py:68
  20.4 8.9 %collective-permute-start.10 = (bf16[1024,256]{1,0:T(8,128)(2,1)S(1)}, bf16[1024,256]{1,0:T(8,128)(2,1)S(1)}, u32[]{:S(2)}, u32[]{:S(2)}) collective-permute-start(bf16[1024,256]{1,0:T(8,128)(2,1)S(1)} %get-tuple-element.78.refs_2_), channel_id=1, source_target_pairs={{0,16},{1,3},{2,18},{3,1},{4,20},{5,7},{6,22},{7,5},{8,24},{9,11},... | collective-permute-start | bytes 1572872 | tf_op jit(solution)/shard_map/ppermute | solution.py:68
  22.3 13.4 %collective-permute-start.9 = (bf16[1024,256]{1,0:T(8,128)(2,1)S(1)}, bf16[1024,256]{1,0:T(8,128)(2,1)S(1)}, u32[]{:S(2)}, u32[]{:S(2)}) collective-permute-start(bf16[1024,256]{1,0:T(8,128)(2,1)S(1)} %shard_map.87.refs_2_), channel_id=1, source_target_pairs={{0,48},{1,7},{2,50},{3,5},{4,52},{5,3},{6,54},{7,1},{8,56},{9,15},... | collective-permute-start | bytes 1572872 | tf_op jit(solution)/shard_map/ppermute | solution.py:68
  24.7 11.1 %collective-permute-start.8 = (bf16[1024,256]{1,0:T(8,128)(2,1)S(1)}, bf16[1024,256]{1,0:T(8,128)(2,1)S(1)}, u32[]{:S(2)}, u32[]{:S(2)}) collective-permute-start(bf16[1024,256]{1,0:T(8,128)(2,1)S(1)} %shard_map.87.refs_2_), channel_id=1, source_target_pairs={{0,16},{1,3},{2,18},{3,1},{4,20},{5,7},{6,22},{7,5},{8,24},{9,11},... | collective-permute-start | bytes 1572872 | tf_op jit(solution)/shard_map/ppermute | solution.py:68
  30.1 10.3 %collective-permute-start.15 = (bf16[512,256]{1,0:T(8,128)(2,1)}, bf16[512,256]{1,0:T(8,128)(2,1)S(1)}, u32[]{:S(2)}, u32[]{:S(2)}) collective-permute-start(bf16[512,256]{1,0:T(8,128)(2,1)} %get-tuple-element.76), channel_id=1, source_target_pairs={{0,16},{1,3},{2,18},{3,1},{4,20},{5,7},{6,22},{7,5},{8,24},{9,11},... | collective-permute-start | bytes 786440 | tf_op jit(solution)/shard_map/ppermute | solution.py:68
  30.9 9.4 %collective-permute-start.16 = (bf16[512,256]{1,0:T(8,128)(2,1)}, bf16[512,256]{1,0:T(8,128)(2,1)}, u32[]{:S(2)}, u32[]{:S(2)}) collective-permute-start(bf16[512,256]{1,0:T(8,128)(2,1)} %get-tuple-element.61), channel_id=1, source_target_pairs={{0,48},{1,7},{2,50},{3,5},{4,52},{5,3},{6,54},{7,1},{8,56},{9,15},... | collective-permute-start | bytes 786440 | tf_op jit(solution)/shard_map/ppermute | solution.py:68
  35.8 6.8 %collective-permute-start.14 = (bf16[512,256]{1,0:T(8,128)(2,1)S(1)}, bf16[512,256]{1,0:T(8,128)(2,1)S(1)}, u32[]{:S(2)}, u32[]{:S(2)}) collective-permute-start(bf16[512,256]{1,0:T(8,128)(2,1)S(1)} %get-tuple-element.68), channel_id=1, source_target_pairs={{0,48},{1,7},{2,50},{3,5},{4,52},{5,3},{6,54},{7,1},{8,56},{9,15},... | collective-permute-start | bytes 786440 | tf_op jit(solution)/shard_map/ppermute | solution.py:68
  49.2 7.1 %collective-permute-start.18 = (f32[256,256]{1,0:T(8,128)S(1)}, f32[256,256]{1,0:T(8,128)S(1)}, u32[]{:S(2)}, u32[]{:S(2)}) collective-permute-start(f32[256,256]{1,0:T(8,128)S(1)} %shard_map.95.half_sum), channel_id=1, source_target_pairs={{0,1},{1,0},{2,3},{3,2},{4,5},{5,4},{6,7},{7,6},{8,9},{9,8},{10,11... | collective-permute-start | bytes 786440 | tf_op jit(solution)/shard_map/ppermute | solution.py:68
  58.2 7.4 %collective-permute-start.24 = (bf16[512,256]{1,0:T(8,128)(2,1)S(1)}, bf16[512,256]{1,0:T(8,128)(2,1)S(1)}, u32[]{:S(2)}, u32[]{:S(2)}) collective-permute-start(bf16[512,256]{1,0:T(8,128)(2,1)S(1)} %get-tuple-element.85), channel_id=1, source_target_pairs={{0,4},{1,33},{2,6},{3,35},{4,0},{5,37},{6,2},{7,39},{8,12},{9,41},... | collective-permute-start | bytes 786440 | tf_op jit(solution)/shard_map/ppermute | solution.py:68
  59.4 7.2 %collective-permute-start.23 = (bf16[512,256]{1,0:T(8,128)(2,1)S(1)}, bf16[512,256]{1,0:T(8,128)(2,1)S(1)}, u32[]{:S(2)}, u32[]{:S(2)}) collective-permute-start(bf16[512,256]{1,0:T(8,128)(2,1)S(1)} %get-tuple-element.84), channel_id=1, source_target_pairs={{0,2},{1,17},{2,0},{3,19},{4,6},{5,21},{6,4},{7,23},{8,10},{9,25},... | collective-permute-start | bytes 786440 | tf_op jit(solution)/shard_map/ppermute | solution.py:68
  59.8 8.3 %collective-permute-start.22 = (bf16[512,256]{1,0:T(8,128)(2,1)S(1)}, bf16[512,256]{1,0:T(8,128)(2,1)S(1)}, u32[]{:S(2)}, u32[]{:S(2)}) collective-permute-start(bf16[512,256]{1,0:T(8,128)(2,1)S(1)} %get-tuple-element.84), channel_id=1, source_target_pairs={{0,6},{1,49},{2,4},{3,51},{4,2},{5,53},{6,0},{7,55},{8,14},{9,57},... | collective-permute-start | bytes 786440 | tf_op jit(solution)/shard_map/ppermute | solution.py:68
  68.1 12.6 %collective-permute-start.31 = (bf16[1280,256]{1,0:T(8,128)(2,1)S(1)}, bf16[1280,256]{1,0:T(8,128)(2,1)S(1)}, u32[]{:S(2)}, u32[]{:S(2)}) collective-permute-start(bf16[1280,256]{1,0:T(8,128)(2,1)S(1)} %get-tuple-element.98.refs_2_), channel_id=1, source_target_pairs={{0,48},{1,7},{2,50},{3,5},{4,52},{5,3},{6,54},{7,1},{8,56},{9,15},... | collective-permute-start | bytes 1966088 | tf_op jit(solution)/shard_map/ppermute | solution.py:68
  69.4 11.4 %collective-permute-start.30 = (bf16[1280,256]{1,0:T(8,128)(2,1)S(1)}, bf16[1280,256]{1,0:T(8,128)(2,1)S(1)}, u32[]{:S(2)}, u32[]{:S(2)}) collective-permute-start(bf16[1280,256]{1,0:T(8,128)(2,1)S(1)} %get-tuple-element.98.refs_2_), channel_id=1, source_target_pairs={{0,16},{1,3},{2,18},{3,1},{4,20},{5,7},{6,22},{7,5},{8,24},{9,11},... | collective-permute-start | bytes 1966088 | tf_op jit(solution)/shard_map/ppermute | solution.py:68
  75.7 10.7 %collective-permute-start.27 = (bf16[1024,256]{1,0:T(8,128)(2,1)S(1)}, bf16[1024,256]{1,0:T(8,128)(2,1)S(1)}, u32[]{:S(2)}, u32[]{:S(2)}) collective-permute-start(bf16[1024,256]{1,0:T(8,128)(2,1)S(1)} %shard_map.98.refs_2_), channel_id=1, source_target_pairs={{0,48},{1,7},{2,50},{3,5},{4,52},{5,3},{6,54},{7,1},{8,56},{9,15},... | collective-permute-start | bytes 1572872 | tf_op jit(solution)/shard_map/ppermute | solution.py:68
  77.5 8.8 %collective-permute-start.26 = (bf16[1024,256]{1,0:T(8,128)(2,1)S(1)}, bf16[1024,256]{1,0:T(8,128)(2,1)S(1)}, u32[]{:S(2)}, u32[]{:S(2)}) collective-permute-start(bf16[1024,256]{1,0:T(8,128)(2,1)S(1)} %shard_map.98.refs_2_), channel_id=1, source_target_pairs={{0,16},{1,3},{2,18},{3,1},{4,20},{5,7},{6,22},{7,5},{8,24},{9,11},... | collective-permute-start | bytes 1572872 | tf_op jit(solution)/shard_map/ppermute | solution.py:68
  80.8 9.7 %collective-permute-start.32 = (bf16[768,256]{1,0:T(8,128)(2,1)S(1)}, bf16[768,256]{1,0:T(8,128)(2,1)S(1)}, u32[]{:S(2)}, u32[]{:S(2)}) collective-permute-start(bf16[768,256]{1,0:T(8,128)(2,1)S(1)} %get-tuple-element.96), channel_id=1, source_target_pairs={{0,16},{1,3},{2,18},{3,1},{4,20},{5,7},{6,22},{7,5},{8,24},{9,11},... | collective-permute-start | bytes 1179656 | tf_op jit(solution)/shard_map/ppermute | solution.py:68
  80.9 13.3 %collective-permute-start.33 = (bf16[512,256]{1,0:T(8,128)(2,1)S(1)}, bf16[512,256]{1,0:T(8,128)(2,1)S(1)}, u32[]{:S(2)}, u32[]{:S(2)}) collective-permute-start(bf16[512,256]{1,0:T(8,128)(2,1)S(1)} %get-tuple-element.97), channel_id=1, source_target_pairs={{0,48},{1,7},{2,50},{3,5},{4,52},{5,3},{6,54},{7,1},{8,56},{9,15},... | collective-permute-start | bytes 786440 | tf_op jit(solution)/shard_map/ppermute | solution.py:68
  86.4 10.1 %collective-permute-start.28 = (bf16[512,256]{1,0:T(8,128)(2,1)S(1)}, bf16[512,256]{1,0:T(8,128)(2,1)S(1)}, u32[]{:S(2)}, u32[]{:S(2)}) collective-permute-start(bf16[512,256]{1,0:T(8,128)(2,1)S(1)} %get-tuple-element.90), channel_id=1, source_target_pairs={{0,16},{1,3},{2,18},{3,1},{4,20},{5,7},{6,22},{7,5},{8,24},{9,11},... | collective-permute-start | bytes 786440 | tf_op jit(solution)/shard_map/ppermute | solution.py:68
  87.9 8.6 %collective-permute-start.29 = (bf16[512,256]{1,0:T(8,128)(2,1)S(1)}, bf16[512,256]{1,0:T(8,128)(2,1)S(1)}, u32[]{:S(2)}, u32[]{:S(2)}) collective-permute-start(bf16[512,256]{1,0:T(8,128)(2,1)S(1)} %get-tuple-element.91), channel_id=1, source_target_pairs={{0,48},{1,7},{2,50},{3,5},{4,52},{5,3},{6,54},{7,1},{8,56},{9,15},... | collective-permute-start | bytes 786440 | tf_op jit(solution)/shard_map/ppermute | solution.py:68
  90.6 9.6 %collective-permute-start.37 = (bf16[256,256]{1,0:T(8,128)(2,1)S(1)}, bf16[256,256]{1,0:T(8,128)(2,1)S(1)}, u32[]{:S(2)}, u32[]{:S(2)}) collective-permute-start(bf16[256,256]{1,0:T(8,128)(2,1)S(1)} %add_convert_fusion.1), channel_id=1, source_target_pairs={{0,72},{1,73},{2,74},{3,75},{4,76},{5,77},{6,78},{7,79},{8,64},{9,... | collective-permute-start | bytes 393224 | tf_op jit(solution)/shard_map/ppermute | solution.py:68
  93.6 6.6 %collective-permute-start.36 = (bf16[256,256]{1,0:T(8,128)(2,1)S(1)}, bf16[256,256]{1,0:T(8,128)(2,1)S(1)}, u32[]{:S(2)}, u32[]{:S(2)}) collective-permute-start(bf16[256,256]{1,0:T(8,128)(2,1)S(1)} %add_convert_fusion.1), channel_id=1, source_target_pairs={{0,64},{1,65},{2,66},{3,67},{4,68},{5,69},{6,70},{7,71},{8,72},{9,... | collective-permute-start | bytes 393224 | tf_op jit(solution)/shard_map/ppermute | solution.py:68
  104.5 7.5 %collective-permute-start.39 = (bf16[640,256]{1,0:T(8,128)(2,1)S(1)}, bf16[640,256]{1,0:T(8,128)(2,1)S(1)}, u32[]{:S(2)}, u32[]{:S(2)}) collective-permute-start(bf16[640,256]{1,0:T(8,128)(2,1)S(1)} %get-tuple-element.106), channel_id=1, source_target_pairs={{0,1},{1,0},{2,3},{3,2},{4,5},{5,4},{6,7},{7,6},{8,9},{9,8},{10,11... | collective-permute-start | bytes 983048 | tf_op jit(solution)/shard_map/ppermute | solution.py:68
  (22 other events, 117.1 us)

commit v5 on v4

--- a/solution.py
+++ b/solution.py
@@ -181,7 +181,7 @@
 
 
 def row_kernel(extra, *refs):
-    right, left, far, _, block = refs[:5]
+    far, right, left, _, block = refs[:5]
     refs = refs[5:]
     if extra:
         piece, refs = refs[0], refs[1:]
@@ -239,9 +239,9 @@
     mine, rest = local_call(
         functools.partial(row_kernel, extra),
         (bf16(8 * T + more, H), bf16(4 * T, H)),
+        from_far,
         from_right,
         from_left,
-        from_far,
         other,
         block,
         *([piece] if extra else []),
@@ -259,14 +259,17 @@
     far_b = move(to_b, second_ring(3))
     part = f32(4 * T, H)
     panels_sib = get_sib(to_b)
-    left_x, right_x, _ = lax.optimization_barrier((left_x, right_x, panels_sib[0]))
+    first = panels_sib[0]
+    if extra:
+        panels = tuple(zip(get_own(to_b), panels_sib))
+        first = total = product(place, panels[0], (4, 4, 4), (mine, left, right), None, part)
+    left_x, right_x, _ = lax.optimization_barrier((left_x, right_x, first))
     to_a, to_b = local_call(far_kernel, (bf16(4 * T, H), bf16(4 * T, H)), right_x, left_x)
-    panels_own = get_own(to_b)
-    panels = tuple(zip(panels_own, panels_sib))
     far_ax = move(to_a, second_ring(1))
     far_bx = move(to_b, second_ring(3))
-    mine = after(mine, to_a)
-    total = product(place, panels[0], (4, 4, 4), (mine, left, right), None, part)
+    if not extra:
+        panels = tuple(zip(get_own(to_b), panels_sib))
+        total = product(place, panels[0], (4, 4, 4), (after(mine, to_a), left, right), None, part)
     total = product(
         place, panels[1], (4, 2, 2, 4, 4), (theirs_here, far_a, far_b, left_x, right_x), total, part
     )

time: 114 us -> 114 us (level)
  starting transfers between devices: 55 us -> 53.4 us
  waiting for transfers between devices: 38.1 us -> 39.5 us
    ppermute x40, starting transfers between devices: 55 us -> 53.4 us  [move(): return lax.ppermute(value, AXES, wiring)]
    ppermute x40, waiting for transfers between devices: 38.1 us -> 39.5 us  [move(): return lax.ppermute(value, AXES, wiring)]
where the time goes in v5:
time: 114 us
  starting transfers between devices  53.4 us (47%)
  waiting for transfers between devices  39.5 us (35%)
  Pallas kernels  18.3 us (16%)
    ppermute x40, starting transfers between devices, move(): return lax.ppermute(value, AXES, wiring)  53.4 us
    ppermute x40, waiting for transfers between devices, move(): return lax.ppermute(value, AXES, wiring)  39.5 us
    pallas_call x6, Pallas kernels, product(): pl.pallas_call(functools.partial(product_kernel, counts, total is not Non...  7.34 us
    pallas_call x2, Pallas kernels, lay_out_tiles(): pl.pallas_call(tiles_kernel, out_shape=tuple((bf16(2 * T, n * 2 * T) for...  5.4 us
    pallas_call x12, Pallas kernels, local_call(): pl.pallas_call(kernel, out_shape=out_shape, in_specs=[SMEM if a.dtype ==...  3.58 us
  transfers between devices with their start and end apart: 40, of which 22 were waited for; matrix products, arithmetic and copies ran while one was open for 0% of the time, Pallas kernels for 11%

profile of v5, /device:TPU:1, one launch (start us, length us, event | category | flops | bytes accessed | tf_op | source)
XLA Modules:
  0.0 113.6 jit_solution(12910733048548305699)
XLA Ops:
  6.5 3.6 %collective-permute-start.4 = (bf16[256,256]{1,0:T(8,128)(2,1)S(1)}, bf16[256,256]{1,0:T(8,128)(2,1)S(1)}, u32[]{:S(2)}, u32[]{:S(2)}) collective-permute-start(bf16[256,256]{1,0:T(8,128)(2,1)S(1)} %shard_map.85.refs_4_), channel_id=1, source_target_pairs={{0,4},{1,33},{2,6},{3,35},{4,0},{5,37},{6,2},{7,39},{8,12},{9,41},... | collective-permute-start | bytes 393224 | tf_op jit(solution)/shard_map/ppermute | solution.py:68
  10.9 1.9 %collective-permute-done.4.refs_0_ = bf16[256,256]{1,0:T(8,128)(2,1)S(1)} collective-permute-done((bf16[256,256]{1,0:T(8,128)(2,1)S(1)}, bf16[256,256]{1,0:T(8,128)(2,1)S(1)}, u32[]{:S(2)}, u32[]{:S(2)}) %collective-permute-start.4) | collective-permute-done | bytes 131104 | tf_op jit(solution)/shard_map/ppermute | solution.py:68
  12.8 2.7 %collective-permute-done.5.refs_1_ = bf16[256,256]{1,0:T(8,128)(2,1)S(1)} collective-permute-done((bf16[256,256]{1,0:T(8,128)(2,1)S(1)}, bf16[256,256]{1,0:T(8,128)(2,1)S(1)}, u32[]{:S(2)}, u32[]{:S(2)}) %collective-permute-start.5) | collective-permute-done | bytes 131104 | tf_op jit(solution)/shard_map/ppermute | solution.py:68
  18.5 1.9 %collective-permute-start.11 = (bf16[1024,256]{1,0:T(8,128)(2,1)S(1)}, bf16[1024,256]{1,0:T(8,128)(2,1)S(1)}, u32[]{:S(2)}, u32[]{:S(2)}) collective-permute-start(bf16[1024,256]{1,0:T(8,128)(2,1)S(1)} %get-tuple-element.77.refs_2_), channel_id=1, source_target_pairs={{0,48},{1,7},{2,50},{3,5},{4,52},{5,3},{6,54},{7,1},{8,56},{9,15},... | collective-permute-start | bytes 1572872 | tf_op jit(solution)/shard_map/ppermute | solution.py:68
  22.4 2.3 %collective-permute-start.8 = (bf16[1024,256]{1,0:T(8,128)(2,1)S(1)}, bf16[1024,256]{1,0:T(8,128)(2,1)S(1)}, u32[]{:S(2)}, u32[]{:S(2)}) collective-permute-start(bf16[1024,256]{1,0:T(8,128)(2,1)S(1)} %shard_map.87.refs_2_), channel_id=1, source_target_pairs={{0,16},{1,3},{2,18},{3,1},{4,20},{5,7},{6,22},{7,5},{8,24},{9,11},... | collective-permute-start | bytes 1572872 | tf_op jit(solution)/shard_map/ppermute | solution.py:68
  24.7 2.1 %collective-permute-start.9 = (bf16[1024,256]{1,0:T(8,128)(2,1)S(1)}, bf16[1024,256]{1,0:T(8,128)(2,1)S(1)}, u32[]{:S(2)}, u32[]{:S(2)}) collective-permute-start(bf16[1024,256]{1,0:T(8,128)(2,1)S(1)} %shard_map.87.refs_2_), channel_id=1, source_target_pairs={{0,48},{1,7},{2,50},{3,5},{4,52},{5,3},{6,54},{7,1},{8,56},{9,15},... | collective-permute-start | bytes 1572872 | tf_op jit(solution)/shard_map/ppermute | solution.py:68
  26.9 2.0 %collective-permute-done.11.left.refs_4_ = bf16[1024,256]{1,0:T(8,128)(2,1)S(1)} collective-permute-done((bf16[1024,256]{1,0:T(8,128)(2,1)S(1)}, bf16[1024,256]{1,0:T(8,128)(2,1)S(1)}, u32[]{:S(2)}, u32[]{:S(2)}) %collective-permute-start.11) | collective-permute-done | bytes 524320 | tf_op jit(solution)/shard_map/ppermute | solution.py:68
  29.7 2.1 %collective-permute-start.16 = (bf16[512,256]{1,0:T(8,128)(2,1)}, bf16[512,256]{1,0:T(8,128)(2,1)}, u32[]{:S(2)}, u32[]{:S(2)}) collective-permute-start(bf16[512,256]{1,0:T(8,128)(2,1)} %get-tuple-element.60), channel_id=1, source_target_pairs={{0,48},{1,7},{2,50},{3,5},{4,52},{5,3},{6,54},{7,1},{8,56},{9,15},... | collective-permute-start | bytes 786440 | tf_op jit(solution)/shard_map/ppermute | solution.py:68
  32.0 3.6 %shard_map.89 = (bf16[256,3072]{1,0:T(8,128)(2,1)S(1)}, bf16[256,4096]{1,0:T(8,128)(2,1)S(1)}, bf16[256,1024]{1,0:T(8,128)(2,1)S(1)}) custom-call(s32[2]{0:T(128)S(1)} %pad_add_fusion.place.refs_0_, s32[32]{0:T(128)S(1)} %stack.161.order, s32[2,64]{1,0:T(2,128)S(1)} %collective-permute-done.1.lists, bf16[64,2,128,128]{3,2,1,0:T(8,128)(2,1)} %collective-permute-done.12.source), custom_call_target="tpu_custom_call" | custom-call | bytes 8388608 | tf_op jit(solution)/shard_map/pallas_call | solution.py:119
  37.2 1.8 %shard_map.91 = (bf16[256,3072]{1,0:T(8,128)(2,1)S(1)}, bf16[256,4096]{1,0:T(8,128)(2,1)S(1)}, bf16[256,1024]{1,0:T(8,128)(2,1)S(1)}) custom-call(s32[2]{0:T(128)S(1)} %pad_add_fusion.place.refs_0_, s32[32]{0:T(128)S(1)} %stack.161.order, s32[2,64]{1,0:T(2,128)S(1)} %bitcast.43, bf16[64,2,128,128]{3,2,1,0:T(8,128)(2,1)S(1)} %bitcast.41), custom_call_target="tpu_custom_call" | custom-call | bytes 8388608 | tf_op jit(solution)/shard_map/pallas_call | solution.py:119
  40.0 2.2 %shard_map.93.refs_5_ = f32[512,256]{1,0:T(8,128)S(1)} custom-call(bf16[256,4096]{1,0:T(8,128)(2,1)S(1)} %get-tuple-element.72.refs_0_, bf16[256,4096]{1,0:T(8,128)(2,1)S(1)} %get-tuple-element.73.refs_1_, bf16[1024,256]{1,0:T(8,128)(2,1)S(1)} %shard_map.87.refs_2_, bf16[512,256]{1,0:T(8,128)(2,1)S(1)} %collective-permute-done.15.refs_3_, ...), custom_call_target="tpu_custom_call" | custom-call | flops 1073741824 | bytes 6815744 | tf_op jit(solution)/shard_map/pallas_call | solution.py:169
  44.0 2.8 %collective-permute-start.17 = (bf16[256,256]{1,0:T(8,128)(2,1)S(1)}, bf16[256,256]{1,0:T(8,128)(2,1)S(1)}, u32[]{:S(2)}, u32[]{:S(2)}) collective-permute-start(bf16[256,256]{1,0:T(8,128)(2,1)S(1)} %get-tuple-element.79), channel_id=1, source_target_pairs={{0,64},{1,65},{2,66},{3,67},{4,68},{5,69},{6,70},{7,71},{8,72},{9,... | collective-permute-start | bytes 393224 | tf_op jit(solution)/shard_map/ppermute | solution.py:68
  46.8 2.6 %collective-permute-done.17.got = bf16[256,256]{1,0:T(8,128)(2,1)S(1)} collective-permute-done((bf16[256,256]{1,0:T(8,128)(2,1)S(1)}, bf16[256,256]{1,0:T(8,128)(2,1)S(1)}, u32[]{:S(2)}, u32[]{:S(2)}) %collective-permute-start.17) | collective-permute-done | bytes 131104 | tf_op jit(solution)/shard_map/ppermute | solution.py:68
  49.4 5.5 %collective-permute-start.18 = (f32[256,256]{1,0:T(8,128)S(1)}, f32[256,256]{1,0:T(8,128)S(1)}, u32[]{:S(2)}, u32[]{:S(2)}) collective-permute-start(f32[256,256]{1,0:T(8,128)S(1)} %shard_map.95.half_sum), channel_id=1, source_target_pairs={{0,1},{1,0},{2,3},{3,2},{4,5},{5,4},{6,7},{7,6},{8,9},{9,8},{10,11... | collective-permute-start | bytes 786440 | tf_op jit(solution)/shard_map/ppermute | solution.py:68
  56.4 2.0 %shard_map.96 = (bf16[128,512]{1,0:T(8,128)(2,1)}, bf16[512,256]{1,0:T(8,128)(2,1)S(1)}, bf16[512,256]{1,0:T(8,128)(2,1)S(1)}, bf16[256,256]{1,0:T(8,128)(2,1)S(1)}, bf16[256,256]{1,0:T(8,128)(2,1)S(1)}) custom-call(s32[2]{0:T(128)S(1)} %pad_add_fusion.place.refs_0_, s32[2]{0:T(128)S(1)} %broadcast_select_fusion.ring, f32[256,256]{1,0:T(8,128)S(1)} %shard_map.95.half_sum, ...), custom_call_target="tpu_custom_call" | custom-call | tf_op jit(solution)/shard_map/pallas_call | solution.py:410
  62.3 2.9 %collective-permute-done.20.refs_3_.first = bf16[256,256]{1,0:T(8,128)(2,1)S(1)} collective-permute-done((bf16[256,256]{1,0:T(8,128)(2,1)S(1)}, bf16[256,256]{1,0:T(8,128)(2,1)S(1)}, u32[]{:S(2)}, u32[]{:S(2)}) %collective-permute-start.20) | collective-permute-done | bytes 131104 | tf_op jit(solution)/shard_map/ppermute | solution.py:68
  65.5 2.8 %collective-permute-done.23.refs_1_ = bf16[512,256]{1,0:T(8,128)(2,1)S(1)} collective-permute-done((bf16[512,256]{1,0:T(8,128)(2,1)S(1)}, bf16[512,256]{1,0:T(8,128)(2,1)S(1)}, u32[]{:S(2)}, u32[]{:S(2)}) %collective-permute-start.23) | collective-permute-done | bytes 262176 | tf_op jit(solution)/shard_map/ppermute | solution.py:68
  72.1 6.5 %collective-permute-done.21.far = bf16[256,256]{1,0:T(8,128)(2,1)S(1)} collective-permute-done((bf16[256,256]{1,0:T(8,128)(2,1)S(1)}, bf16[256,256]{1,0:T(8,128)(2,1)S(1)}, u32[]{:S(2)}, u32[]{:S(2)}) %collective-permute-start.21) | collective-permute-done | bytes 131104 | tf_op jit(solution)/shard_map/ppermute | solution.py:68
  78.7 1.8 %collective-permute-start.27 = (bf16[1024,256]{1,0:T(8,128)(2,1)S(1)}, bf16[1024,256]{1,0:T(8,128)(2,1)S(1)}, u32[]{:S(2)}, u32[]{:S(2)}) collective-permute-start(bf16[1024,256]{1,0:T(8,128)(2,1)S(1)} %shard_map.98.refs_2_), channel_id=1, source_target_pairs={{0,48},{1,7},{2,50},{3,5},{4,52},{5,3},{6,54},{7,1},{8,56},{9,15},... | collective-permute-start | bytes 1572872 | tf_op jit(solution)/shard_map/ppermute | solution.py:68
  83.9 3.2 %collective-permute-done.26.right.refs_5_ = bf16[1024,256]{1,0:T(8,128)(2,1)S(1)} collective-permute-done((bf16[1024,256]{1,0:T(8,128)(2,1)S(1)}, bf16[1024,256]{1,0:T(8,128)(2,1)S(1)}, u32[]{:S(2)}, u32[]{:S(2)}) %collective-permute-start.26) | collective-permute-done | bytes 524320 | tf_op jit(solution)/shard_map/ppermute | solution.py:68
  91.7 2.7 %collective-permute-start.36 = (bf16[256,256]{1,0:T(8,128)(2,1)S(1)}, bf16[256,256]{1,0:T(8,128)(2,1)S(1)}, u32[]{:S(2)}, u32[]{:S(2)}) collective-permute-start(bf16[256,256]{1,0:T(8,128)(2,1)S(1)} %add_convert_fusion.1), channel_id=1, source_target_pairs={{0,64},{1,65},{2,66},{3,67},{4,68},{5,69},{6,70},{7,71},{8,72},{9,... | collective-permute-start | bytes 393224 | tf_op jit(solution)/shard_map/ppermute | solution.py:68
  99.8 3.5 %collective-permute-done.34.got = bf16[256,256]{1,0:T(8,128)(2,1)S(1)} collective-permute-done((bf16[256,256]{1,0:T(8,128)(2,1)S(1)}, bf16[256,256]{1,0:T(8,128)(2,1)S(1)}, u32[]{:S(2)}, u32[]{:S(2)}) %collective-permute-start.34) | collective-permute-done | bytes 131104 | tf_op jit(solution)/shard_map/ppermute | solution.py:68
  103.9 6.6 %collective-permute-start.39 = (bf16[640,256]{1,0:T(8,128)(2,1)S(1)}, bf16[640,256]{1,0:T(8,128)(2,1)S(1)}, u32[]{:S(2)}, u32[]{:S(2)}) collective-permute-start(bf16[640,256]{1,0:T(8,128)(2,1)S(1)} %get-tuple-element.104), channel_id=1, source_target_pairs={{0,1},{1,0},{2,3},{3,2},{4,5},{5,4},{6,7},{7,6},{8,9},{9,8},{10,11... | collective-permute-start | bytes 983048 | tf_op jit(solution)/shard_map/ppermute | solution.py:68
  111.8 1.8 %shard_map.105 = (bf16[128,512]{1,0:T(8,128)(2,1)}, f32[512,512]{1,0:T(8,128)}) custom-call(s32[2]{0:T(128)S(1)} %pad_add_fusion.place.refs_0_, s32[2]{0:T(128)S(1)} %broadcast_select_fusion.ring, bf16[128,256]{1,0:T(8,128)(2,1)S(1)} %get-tuple-element.103.mine, bf16[640,256]{1,0:T(8,128)(2,1)S(1)} %collective-permute-done.39.core, ...), custom_call_target="tpu_custom_call" | custom-call | tf_op jit(solution)/shard_map/pallas_call | solution.py:222
  (96 shorter events, 41.8 us)
Async XLA Ops:
  5.0 27.0 %collective-permute-start.12 = (bf16[64,2,128,128]{3,2,1,0:T(8,128)(2,1)}, bf16[64,2,128,128]{3,2,1,0:T(8,128)(2,1)}, u32[]{:S(2)}, u32[]{:S(2)}) collective-permute-start(bf16[64,2,128,128]{3,2,1,0:T(8,128)(2,1)} %bitcast.40), channel_id=1, source_target_pairs={{0,1},{1,0},{2,3},{3,2},{4,5},{5,4},{6,7},{7,6},{8,9},{9,8},{10,11... | collective-permute-start | bytes 12582920 | tf_op jit(solution)/shard_map/ppermute | solution.py:68
  17.2 9.7 %collective-permute-start.10 = (bf16[1024,256]{1,0:T(8,128)(2,1)S(1)}, bf16[1024,256]{1,0:T(8,128)(2,1)S(1)}, u32[]{:S(2)}, u32[]{:S(2)}) collective-permute-start(bf16[1024,256]{1,0:T(8,128)(2,1)S(1)} %get-tuple-element.77.refs_2_), channel_id=1, source_target_pairs={{0,16},{1,3},{2,18},{3,1},{4,20},{5,7},{6,22},{7,5},{8,24},{9,11},... | collective-permute-start | bytes 1572872 | tf_op jit(solution)/shard_map/ppermute | solution.py:68
  18.5 10.5 %collective-permute-start.11 = (bf16[1024,256]{1,0:T(8,128)(2,1)S(1)}, bf16[1024,256]{1,0:T(8,128)(2,1)S(1)}, u32[]{:S(2)}, u32[]{:S(2)}) collective-permute-start(bf16[1024,256]{1,0:T(8,128)(2,1)S(1)} %get-tuple-element.77.refs_2_), channel_id=1, source_target_pairs={{0,48},{1,7},{2,50},{3,5},{4,52},{5,3},{6,54},{7,1},{8,56},{9,15},... | collective-permute-start | bytes 1572872 | tf_op jit(solution)/shard_map/ppermute | solution.py:68
  22.4 13.2 %collective-permute-start.8 = (bf16[1024,256]{1,0:T(8,128)(2,1)S(1)}, bf16[1024,256]{1,0:T(8,128)(2,1)S(1)}, u32[]{:S(2)}, u32[]{:S(2)}) collective-permute-start(bf16[1024,256]{1,0:T(8,128)(2,1)S(1)} %shard_map.87.refs_2_), channel_id=1, source_target_pairs={{0,16},{1,3},{2,18},{3,1},{4,20},{5,7},{6,22},{7,5},{8,24},{9,11},... | collective-permute-start | bytes 1572872 | tf_op jit(solution)/shard_map/ppermute | solution.py:68
  24.7 10.9 %collective-permute-start.9 = (bf16[1024,256]{1,0:T(8,128)(2,1)S(1)}, bf16[1024,256]{1,0:T(8,128)(2,1)S(1)}, u32[]{:S(2)}, u32[]{:S(2)}) collective-permute-start(bf16[1024,256]{1,0:T(8,128)(2,1)S(1)} %shard_map.87.refs_2_), channel_id=1, source_target_pairs={{0,48},{1,7},{2,50},{3,5},{4,52},{5,3},{6,54},{7,1},{8,56},{9,15},... | collective-permute-start | bytes 1572872 | tf_op jit(solution)/shard_map/ppermute | solution.py:68
  29.7 10.2 %collective-permute-start.15 = (bf16[512,256]{1,0:T(8,128)(2,1)}, bf16[512,256]{1,0:T(8,128)(2,1)S(1)}, u32[]{:S(2)}, u32[]{:S(2)}) collective-permute-start(bf16[512,256]{1,0:T(8,128)(2,1)} %get-tuple-element.75), channel_id=1, source_target_pairs={{0,16},{1,3},{2,18},{3,1},{4,20},{5,7},{6,22},{7,5},{8,24},{9,11},... | collective-permute-start | bytes 786440 | tf_op jit(solution)/shard_map/ppermute | solution.py:68
  29.7 10.2 %collective-permute-start.16 = (bf16[512,256]{1,0:T(8,128)(2,1)}, bf16[512,256]{1,0:T(8,128)(2,1)}, u32[]{:S(2)}, u32[]{:S(2)}) collective-permute-start(bf16[512,256]{1,0:T(8,128)(2,1)} %get-tuple-element.60), channel_id=1, source_target_pairs={{0,48},{1,7},{2,50},{3,5},{4,52},{5,3},{6,54},{7,1},{8,56},{9,15},... | collective-permute-start | bytes 786440 | tf_op jit(solution)/shard_map/ppermute | solution.py:68
  49.4 7.0 %collective-permute-start.18 = (f32[256,256]{1,0:T(8,128)S(1)}, f32[256,256]{1,0:T(8,128)S(1)}, u32[]{:S(2)}, u32[]{:S(2)}) collective-permute-start(f32[256,256]{1,0:T(8,128)S(1)} %shard_map.95.half_sum), channel_id=1, source_target_pairs={{0,1},{1,0},{2,3},{3,2},{4,5},{5,4},{6,7},{7,6},{8,9},{9,8},{10,11... | collective-permute-start | bytes 786440 | tf_op jit(solution)/shard_map/ppermute | solution.py:68
  58.4 7.1 %collective-permute-start.22 = (bf16[512,256]{1,0:T(8,128)(2,1)S(1)}, bf16[512,256]{1,0:T(8,128)(2,1)S(1)}, u32[]{:S(2)}, u32[]{:S(2)}) collective-permute-start(bf16[512,256]{1,0:T(8,128)(2,1)S(1)} %get-tuple-element.83), channel_id=1, source_target_pairs={{0,4},{1,33},{2,6},{3,35},{4,0},{5,37},{6,2},{7,39},{8,12},{9,41},... | collective-permute-start | bytes 786440 | tf_op jit(solution)/shard_map/ppermute | solution.py:68
  58.9 9.4 %collective-permute-start.23 = (bf16[512,256]{1,0:T(8,128)(2,1)S(1)}, bf16[512,256]{1,0:T(8,128)(2,1)S(1)}, u32[]{:S(2)}, u32[]{:S(2)}) collective-permute-start(bf16[512,256]{1,0:T(8,128)(2,1)S(1)} %get-tuple-element.84), channel_id=1, source_target_pairs={{0,6},{1,49},{2,4},{3,51},{4,2},{5,53},{6,0},{7,55},{8,14},{9,57},... | collective-permute-start | bytes 786440 | tf_op jit(solution)/shard_map/ppermute | solution.py:68
  60.3 7.9 %collective-permute-start.24 = (bf16[512,256]{1,0:T(8,128)(2,1)S(1)}, bf16[512,256]{1,0:T(8,128)(2,1)S(1)}, u32[]{:S(2)}, u32[]{:S(2)}) collective-permute-start(bf16[512,256]{1,0:T(8,128)(2,1)S(1)} %get-tuple-element.84), channel_id=1, source_target_pairs={{0,2},{1,17},{2,0},{3,19},{4,6},{5,21},{6,4},{7,23},{8,10},{9,25},... | collective-permute-start | bytes 786440 | tf_op jit(solution)/shard_map/ppermute | solution.py:68
  68.3 12.2 %collective-permute-start.28 = (bf16[1280,256]{1,0:T(8,128)(2,1)S(1)}, bf16[1280,256]{1,0:T(8,128)(2,1)S(1)}, u32[]{:S(2)}, u32[]{:S(2)}) collective-permute-start(bf16[1280,256]{1,0:T(8,128)(2,1)S(1)} %get-tuple-element.87.refs_2_), channel_id=1, source_target_pairs={{0,16},{1,3},{2,18},{3,1},{4,20},{5,7},{6,22},{7,5},{8,24},{9,11},... | collective-permute-start | bytes 1966088 | tf_op jit(solution)/shard_map/ppermute | solution.py:68
  69.4 12.3 %collective-permute-start.29 = (bf16[1280,256]{1,0:T(8,128)(2,1)S(1)}, bf16[1280,256]{1,0:T(8,128)(2,1)S(1)}, u32[]{:S(2)}, u32[]{:S(2)}) collective-permute-start(bf16[1280,256]{1,0:T(8,128)(2,1)S(1)} %get-tuple-element.87.refs_2_), channel_id=1, source_target_pairs={{0,48},{1,7},{2,50},{3,5},{4,52},{5,3},{6,54},{7,1},{8,56},{9,15},... | collective-permute-start | bytes 1966088 | tf_op jit(solution)/shard_map/ppermute | solution.py:68
  70.3 8.3 %collective-permute-start.25 = (bf16[512,256]{1,0:T(8,128)(2,1)S(1)}, bf16[512,256]{1,0:T(8,128)(2,1)S(1)}, u32[]{:S(2)}, u32[]{:S(2)}) collective-permute-start(bf16[512,256]{1,0:T(8,128)(2,1)S(1)} %get-tuple-element.86), channel_id=1, source_target_pairs={{0,8},{1,9},{2,10},{3,11},{4,12},{5,13},{6,14},{7,15},{8,0},{9,1},... | collective-permute-start | bytes 786440 | tf_op jit(solution)/shard_map/ppermute | solution.py:68
  71.5 7.1 %collective-permute-start.21 = (bf16[256,256]{1,0:T(8,128)(2,1)S(1)}, bf16[256,256]{1,0:T(8,128)(2,1)S(1)}, u32[]{:S(2)}, u32[]{:S(2)}) collective-permute-start(bf16[256,256]{1,0:T(8,128)(2,1)S(1)} %collective-permute-done.20.refs_3_.first), channel_id=1, source_target_pairs={{0,4},{1,33},{2,6},{3,35},{4,0},{5,37},{6,2},{7,39},{8,12},{9,41},... | collective-permute-start | bytes 393224 | tf_op jit(solution)/shard_map/ppermute | solution.py:68
  78.7 8.4 %collective-permute-start.26 = (bf16[1024,256]{1,0:T(8,128)(2,1)S(1)}, bf16[1024,256]{1,0:T(8,128)(2,1)S(1)}, u32[]{:S(2)}, u32[]{:S(2)}) collective-permute-start(bf16[1024,256]{1,0:T(8,128)(2,1)S(1)} %shard_map.98.refs_2_), channel_id=1, source_target_pairs={{0,16},{1,3},{2,18},{3,1},{4,20},{5,7},{6,22},{7,5},{8,24},{9,11},... | collective-permute-start | bytes 1572872 | tf_op jit(solution)/shard_map/ppermute | solution.py:68
  78.7 9.6 %collective-permute-start.27 = (bf16[1024,256]{1,0:T(8,128)(2,1)S(1)}, bf16[1024,256]{1,0:T(8,128)(2,1)S(1)}, u32[]{:S(2)}, u32[]{:S(2)}) collective-permute-start(bf16[1024,256]{1,0:T(8,128)(2,1)S(1)} %shard_map.98.refs_2_), channel_id=1, source_target_pairs={{0,48},{1,7},{2,50},{3,5},{4,52},{5,3},{6,54},{7,1},{8,56},{9,15},... | collective-permute-start | bytes 1572872 | tf_op jit(solution)/shard_map/ppermute | solution.py:68
  81.8 9.5 %collective-permute-start.32 = (bf16[768,256]{1,0:T(8,128)(2,1)S(1)}, bf16[768,256]{1,0:T(8,128)(2,1)S(1)}, u32[]{:S(2)}, u32[]{:S(2)}) collective-permute-start(bf16[768,256]{1,0:T(8,128)(2,1)S(1)} %get-tuple-element.95), channel_id=1, source_target_pairs={{0,16},{1,3},{2,18},{3,1},{4,20},{5,7},{6,22},{7,5},{8,24},{9,11},... | collective-permute-start | bytes 1179656 | tf_op jit(solution)/shard_map/ppermute | solution.py:68
  81.9 12.6 %collective-permute-start.33 = (bf16[512,256]{1,0:T(8,128)(2,1)S(1)}, bf16[512,256]{1,0:T(8,128)(2,1)S(1)}, u32[]{:S(2)}, u32[]{:S(2)}) collective-permute-start(bf16[512,256]{1,0:T(8,128)(2,1)S(1)} %get-tuple-element.96), channel_id=1, source_target_pairs={{0,48},{1,7},{2,50},{3,5},{4,52},{5,3},{6,54},{7,1},{8,56},{9,15},... | collective-permute-start | bytes 786440 | tf_op jit(solution)/shard_map/ppermute | solution.py:68
  88.4 8.1 %collective-permute-start.30 = (bf16[512,256]{1,0:T(8,128)(2,1)S(1)}, bf16[512,256]{1,0:T(8,128)(2,1)S(1)}, u32[]{:S(2)}, u32[]{:S(2)}) collective-permute-start(bf16[512,256]{1,0:T(8,128)(2,1)S(1)} %get-tuple-element.92), channel_id=1, source_target_pairs={{0,16},{1,3},{2,18},{3,1},{4,20},{5,7},{6,22},{7,5},{8,24},{9,11},... | collective-permute-start | bytes 786440 | tf_op jit(solution)/shard_map/ppermute | solution.py:68
  88.6 7.9 %collective-permute-start.31 = (bf16[512,256]{1,0:T(8,128)(2,1)S(1)}, bf16[512,256]{1,0:T(8,128)(2,1)S(1)}, u32[]{:S(2)}, u32[]{:S(2)}) collective-permute-start(bf16[512,256]{1,0:T(8,128)(2,1)S(1)} %get-tuple-element.93), channel_id=1, source_target_pairs={{0,48},{1,7},{2,50},{3,5},{4,52},{5,3},{6,54},{7,1},{8,56},{9,15},... | collective-permute-start | bytes 786440 | tf_op jit(solution)/shard_map/ppermute | solution.py:68
  91.3 7.5 %collective-permute-start.35 = (bf16[256,256]{1,0:T(8,128)(2,1)S(1)}, bf16[256,256]{1,0:T(8,128)(2,1)S(1)}, u32[]{:S(2)}, u32[]{:S(2)}) collective-permute-start(bf16[256,256]{1,0:T(8,128)(2,1)S(1)} %add_convert_fusion.1), channel_id=1, source_target_pairs={{0,8},{1,9},{2,10},{3,11},{4,12},{5,13},{6,14},{7,15},{8,0},{9,1},... | collective-permute-start | bytes 393224 | tf_op jit(solution)/shard_map/ppermute | solution.py:68
  91.7 7.2 %collective-permute-start.36 = (bf16[256,256]{1,0:T(8,128)(2,1)S(1)}, bf16[256,256]{1,0:T(8,128)(2,1)S(1)}, u32[]{:S(2)}, u32[]{:S(2)}) collective-permute-start(bf16[256,256]{1,0:T(8,128)(2,1)S(1)} %add_convert_fusion.1), channel_id=1, source_target_pairs={{0,64},{1,65},{2,66},{3,67},{4,68},{5,69},{6,70},{7,71},{8,72},{9,... | collective-permute-start | bytes 393224 | tf_op jit(solution)/shard_map/ppermute | solution.py:68
  103.9 7.9 %collective-permute-start.39 = (bf16[640,256]{1,0:T(8,128)(2,1)S(1)}, bf16[640,256]{1,0:T(8,128)(2,1)S(1)}, u32[]{:S(2)}, u32[]{:S(2)}) collective-permute-start(bf16[640,256]{1,0:T(8,128)(2,1)S(1)} %get-tuple-element.104), channel_id=1, source_target_pairs={{0,1},{1,0},{2,3},{3,2},{4,5},{5,4},{6,7},{7,6},{8,9},{9,8},{10,11... | collective-permute-start | bytes 983048 | tf_op jit(solution)/shard_map/ppermute | solution.py:68
  (22 other events, 120.5 us)
